TPU v7x, 512 devices: a whole 4x4x16 slice. The times are simulated.
512 devices in a mesh: ex: 16 (over x_hi, y, core), dim: 32 (over z, x_lo).
Axes of the slice: x: 4 (x_hi: 2, x_lo: 2; x = x_hi * 2 + x_lo), y: 4, z: 16, core: 2. Of those that a mesh axis runs over, the one named last changes fastest.
Arguments:
- query_grads: bfloat16 [1024, 65536], P('ex', 'dim'), may hold values from -6 to 6
- precond: bfloat16 [32, 2048, 2048], P('dim', None, 'ex'), may hold values from -0.125 to 0.125
- codes: bfloat16 [16384, 65536], P('ex', 'dim'), may hold values from -1 to 1
- scales: float32 [16384, 512], P('ex', 'dim'), may hold values from 0.2 to 2
Outputs:
- scores: float32 [1024, 16384], P('dim', 'ex')
All inputs are finite; a program needn't handle non-finite values.
Results may differ from a plain program's by a relative error of at most 0.0041.
Values may be sent and summed in bfloat16 or wider, within the bound.
No kernel may reach another device: no remote copies, remote signals or barrier semaphores. Data moves between devices by JAX's collectives and lax.ppermute only.
A program may use at most 64 MiB of HBM per device.

v0:
```python
import jax
import jax.numpy as jnp
from jax import lax
from jax.sharding import PartitionSpec as P


def shards(query_grads, precond, codes, scales):
    example_rows, layer_width = codes.shape
    block_count = scales.shape[1]
    expanded = codes.astype(jnp.float32).reshape(
        example_rows, block_count, layer_width // block_count
    )
    dequantized = (
        (expanded * scales[:, :, None]).reshape(example_rows, layer_width).astype(jnp.bfloat16)
    )
    weights = precond[0]
    column_part = jnp.dot(
        lax.all_gather(query_grads, "ex", axis=0, tiled=True),
        weights,
        preferred_element_type=jnp.float32,
    ).astype(jnp.bfloat16)
    conditioned = lax.all_gather(column_part, "ex", axis=1, tiled=True)
    summed = lax.psum_scatter(
        lax.dot_general(
            conditioned, dequantized, (((1,), (1,)), ((), ())), preferred_element_type=jnp.float32
        ),
        "dim",
        scatter_dimension=0,
        tiled=True,
    )
    return summed * float(layer_width * lax.axis_size("dim")) ** (-0.5)


def solution(mesh):
    placed = (P("ex", "dim"), P("dim", None, "ex"), P("ex", "dim"), P("ex", "dim"))
    return jax.shard_map(
        shards, mesh=mesh, in_specs=placed, out_specs=P("dim", "ex"), check_vma=False
    )
```

profile of v0, /device:TPU:8, one launch (start us, length us, event | category | flops | bytes accessed | tf_op | source)
XLA Modules:
  0.0 322.2 jit_solution(6335250065651854964)
XLA Ops:
  6.5 0.0 copy-start
  6.5 0.0 copy-start.1
  6.5 0.0 all-gather.3.cloned.1.call-start
  6.5 0.7 all-gather.3.cloned.1.call-update
  7.3 0.0 all-gather.5.cloned.1.call-start
  7.3 77.1 %all-gather.3.cloned.1.call-done = bf16[1024,2048]{1,0:T(8,128)(2,1)} async-done(((bf16[64,2048]{1,0:T(8,128)(2,1)}), bf16[1024,2048]{1,0:T(8,128)(2,1)}) %all-gather.3.cloned.1.call-update) | async-done | bytes 4194320 | tf_op jit(solution)/shard_map/all_gather | solution.py:18
  84.4 0.0 copy-done
  84.4 4.1 %convolution_convert_fusion = bf16[1024,128]{1,0:T(8,128)(2,1)} fusion(bf16[1024,2048]{1,0:T(8,128)(2,1)} %all-gather.3.cloned.1.call-done, bf16[1,2048,128]{2,1,0:T(8,128)(2,1)S(1)} %copy-done), kind=kOutput, calls=%fused_computation.3 | convolution fusion | flops 537001984 | bytes 4980736 | tf_op jit(solution)/shard_map/dot_general | solution.py:17
  88.6 0.0 all-gather.5.cloned.1.call-update
  88.6 0.0 reduce-scatter.2.cloned.1.call-start
  88.7 0.0 copy-done.1
  88.7 0.2 copy.5
  88.9 69.8 %all-gather.5.cloned.1.call-done = bf16[1024,2048]{1,0:T(8,128)(2,1)} async-done(((bf16[1024,128]{1,0:T(8,128)(2,1)}), bf16[1024,2048]{1,0:T(8,128)(2,1)}) %all-gather.5.cloned.1.call-update) | async-done | bytes 4194320 | tf_op jit(solution)/shard_map/all_gather | solution.py:22
  158.6 0.0 copy-start.2
  158.6 0.0 copy-start.3
  158.7 2.3 mul.17
  161.0 0.0 copy-done.2
  161.0 1.2 copy-done.3
  162.1 6.5 %fusion.1 = f32[1024,1024]{1,0:T(8,128)} fusion(bf16[1024,2048]{1,0:T(8,128)(2,1)S(1)} %copy-done.3, f32[128,8,16,128]{3,2,1,0:T(8,128)S(1)} %bitcast.11, bf16[1024,2048]{1,0:T(8,128)(2,1)S(1)} %copy-done.2), kind=kOutput, calls=%fused_computation.2 | convolution fusion | flops 4301258752 | bytes 20971520 | tf_op jit(solution)/shard_map/dot_general | solution.py:24
  168.6 0.0 reduce-scatter.2.cloned.1.call-update
  168.6 145.5 %reduce-scatter.2.cloned.1.call-done = f32[32,1024]{1,0:T(8,128)} async-done(((f32[1024,1024]{1,0:T(8,128)}), f32[32,1024]{1,0:T(8,128)}) %reduce-scatter.2.cloned.1.call-update) | async-done | bytes 131088 | tf_op jit(solution)/shard_map/reduce_scatter | solution.py:23
  314.1 1.6 broadcast_multiply_fusion
Async XLA Ops:
  6.5 77.9 %copy-start = (bf16[1,2048,128]{2,1,0:T(8,128)(2,1)S(1)}, bf16[1,2048,128]{2,1,0:T(8,128)(2,1)}, u32[]{:S(2)}) copy-start(bf16[1,2048,128]{2,1,0:T(8,128)(2,1)} %param.5) | copy-start | bytes 1572868
  6.5 82.1 %copy-start.1 = (f32[1024,16]{0,1:T(8,128)S(1)}, f32[1024,16]{0,1:T(8,128)}, u32[]{:S(2)}) copy-start(f32[1024,16]{0,1:T(8,128)} %param.7) | copy-start | bytes 196612
  6.5 77.9 %all-gather.3.cloned.1.call-start = ((), (), s32[]{:S(2)}) async-start(), calls=%async_computation.1 | async-start | bytes 4456448 | tf_op jit(solution)/shard_map/all_gather | solution.py:18
  7.3 151.4 %all-gather.5.cloned.1.call-start = ((), (), s32[]{:S(2)}) async-start(), calls=%async_computation.2 | async-start | bytes 4456448 | tf_op jit(solution)/shard_map/all_gather | solution.py:22
  88.6 225.5 %reduce-scatter.2.cloned.1.call-start = ((), (), s32[]{:S(2)}) async-start(), calls=%async_computation.3 | async-start | bytes 4325376 | tf_op jit(solution)/shard_map/reduce_scatter | solution.py:23
  158.6 2.3 copy-start.2
  158.6 3.5 %copy-start.3 = (bf16[1024,2048]{1,0:T(8,128)(2,1)S(1)}, bf16[1024,2048]{1,0:T(8,128)(2,1)}, u32[]{:S(2)}) copy-start(bf16[1024,2048]{1,0:T(8,128)(2,1)} %all-gather.5.cloned.1.call-done) | copy-start | bytes 12582916
Sparse Core Ops, SparseCore 0:
  10.7 73.6 all-gather.2
  88.7 69.8 all-gather.4
  168.7 145.3 reduce-scatter.1
where the time goes:
time: 322 us
  waiting for transfers between devices  293 us (91%)
  between operations  13.1 us (4%)
  matrix products  10.6 us (3%)
  local copies, waits for them, and re-layouts  3.65 us (1%)
    reduce_scatter x1, waiting for transfers between devices, shards(): lax.psum_scatter(lax.dot_general(conditioned, dequantized, (((1,), (1,)),...  145 us
    all_gather x1, waiting for transfers between devices, shards(): lax.all_gather(query_grads, 'ex', axis=0, tiled=True)  77.1 us
    all_gather x1, waiting for transfers between devices, shards(): conditioned = lax.all_gather(column_part, 'ex', axis=1, tiled=True)  69.8 us
    dot_general x1, matrix products, shards(): lax.dot_general(conditioned, dequantized, (((1,), (1,)), ((), ())), prefe...  6.48 us
  transfers between devices with their start and end apart: 3, of which 3 were waited for; matrix products, arithmetic and copies ran while one was open for 0% of the time, Pallas kernels for 0%

commit v1 on v0

v1 whole, which is shorter than its diff:
```python
import jax
import jax.numpy as jnp
from jax import lax
from jax.sharding import PartitionSpec as P

CORES, ROWS_Y, ROWS_X = 2, 4, 2
NEAR, FAR = 4, 8


def shards(query_grads, precond, codes, scales):
    own_queries, width = query_grads.shape
    own_columns = precond.shape[2]
    examples, blocks = scales.shape
    ex_size = lax.axis_size("ex")
    slots = FAR * NEAR
    tile = own_queries * ex_size // slots // CORES
    chips = ROWS_X * ROWS_Y
    block_rows = own_queries * ROWS_Y
    place = lax.axis_index("ex")
    core, x_hi = place % CORES, place // (ROWS_Y * CORES)
    core_swap = [(e, e ^ 1) for e in range(ex_size)]
    x_swap = [(e, e ^ (ROWS_Y * CORES)) for e in range(ex_size)]
    beside = [[x * ROWS_Y * CORES + i for i in range(ROWS_Y * CORES)] for x in range(ROWS_X)]
    same_core = [[chip * CORES + c for chip in range(chips)] for c in range(CORES)]
    near = [[far * NEAR + i for i in range(NEAR)] for far in range(FAR)]
    far = [
        [(chip * CORES + c) * slots + f * NEAR + i for f in range(FAR) for c in range(CORES)]
        for chip in range(chips)
        for i in range(NEAR)
    ]

    halves = query_grads.reshape(2, CORES, tile, width).transpose(1, 0, 2, 3)
    halves = jnp.broadcast_to(halves[None], (ROWS_Y, CORES, 2, tile, width))
    grads = lax.all_to_all(
        halves.reshape(ROWS_Y * CORES, 2 * tile, width),
        "ex", 0, 0, tiled=True, axis_index_groups=beside,
    ).reshape(block_rows, width)

    own = precond[0]
    across = lax.ppermute(own, "ex", x_swap)
    both = jnp.stack([jnp.where(x_hi == 0, own, across), jnp.where(x_hi == 0, across, own)])
    other = lax.ppermute(both, "ex", core_swap)
    first, second = jnp.where(core == 0, both, other), jnp.where(core == 0, other, both)
    weights = jnp.concatenate([first[0], second[0], first[1], second[1]], axis=1)

    expanded = codes.astype(jnp.float32).reshape(examples, blocks, width // blocks)
    mine = (expanded * scales[:, :, None]).reshape(examples, width).astype(jnp.bfloat16)
    theirs = lax.ppermute(mine, "ex", core_swap)
    store = jnp.concatenate(
        [jnp.where(core == 0, mine, theirs), jnp.where(core == 0, theirs, mine)], axis=0
    )

    part = jnp.dot(grads, weights, preferred_element_type=jnp.float32).astype(jnp.bfloat16)
    parts = lax.all_to_all(
        jnp.broadcast_to(part[None], (chips,) + part.shape),
        "ex", 0, 0, tiled=True, axis_index_groups=same_core,
    )
    pair = CORES * own_columns
    conditioned = (
        parts.reshape(ROWS_X, ROWS_Y, ROWS_Y, NEAR, tile, ROWS_X, pair)
        .transpose(3, 0, 2, 4, 5, 1, 6)
        .reshape(slots * tile, width)
    )

    term = lax.dot_general(
        conditioned, store, (((1,), (1,)), ((), ())), preferred_element_type=jnp.float32
    ).astype(jnp.bfloat16)
    terms = lax.all_to_all(
        term.reshape(NEAR, FAR * tile, CORES * examples),
        "dim", 0, 0, tiled=True, axis_index_groups=near,
    )
    layers = (
        jnp.sum(terms.astype(jnp.float32), axis=0)
        .astype(jnp.bfloat16)
        .reshape(FAR, tile, CORES, examples)
        .transpose(0, 2, 1, 3)
        .reshape(FAR * CORES, tile, examples)
    )
    sums = lax.all_to_all(layers, ("ex", "dim"), 0, 0, tiled=True, axis_index_groups=far)
    total = jnp.sum(sums.astype(jnp.float32).reshape(FAR, CORES * tile, examples), axis=0)
    return total * float(width * lax.axis_size("dim")) ** (-0.5)


def solution(mesh):
    placed = (P("ex", "dim"), P("dim", None, "ex"), P("ex", "dim"), P("ex", "dim"))
    return jax.shard_map(
        shards, mesh=mesh, in_specs=placed, out_specs=P("dim", "ex"), check_vma=False
    )
```

time: 322 us -> 187 us (0.58)
  the two profiles are of different devices: /device:TPU:8 before, /device:TPU:1 now
where the time goes in v1:
time: 187 us; the launch traced here: 186 us
  blocking collectives  104 us (56%)
  waiting for transfers between devices  22.3 us (12%)
  starting transfers between devices  19.6 us (10%)
  local copies, waits for them, and re-layouts  15.6 us (8%)
  other arithmetic  14.7 us (8%)
  matrix products  9.54 us (5%)
    all_to_all x1, blocking collectives, shards(): lax.all_to_all(layers, ('ex', 'dim'), 0, 0, tiled=True, axis_index_groups...  49.1 us
    all_to_all x1, blocking collectives, shards(): lax.all_to_all(jnp.broadcast_to(part[None], (chips,) + part.shape), 'ex',...  30.5 us
    all_to_all x1, blocking collectives, shards(): lax.all_to_all(term.reshape(NEAR, FAR * tile, CORES * examples), 'dim', 0...  24.8 us
    all_to_all x1, waiting for transfers between devices, shards(): lax.all_to_all(halves.reshape(ROWS_Y * CORES, 2 * tile, width), 'ex', 0,...  14.9 us
    ppermute x1, starting transfers between devices, shards(): other = lax.ppermute(both, 'ex', core_swap)  7.6 us
    dot_general x1, matrix products, shards(): lax.dot_general(conditioned, store, (((1,), (1,)), ((), ())), preferred_e...  7.56 us
    ppermute x1, waiting for transfers between devices, shards(): across = lax.ppermute(own, 'ex', x_swap)  7.41 us
    convert_element_type x1, other arithmetic, shards(): (expanded * scales[:, :, None]).reshape(examples, width)  7.27 us
  transfers between devices with their start and end apart: 4, of which 2 were waited for; matrix products, arithmetic and copies ran while one was open for 13% of the time, Pallas kernels for 0%

profile of v1, /device:TPU:1, one launch (start us, length us, event | category | flops | bytes accessed | tf_op | source)
XLA Modules:
  0.0 186.3 jit_solution(8401022399123235279)
XLA Ops:
  0.0 5.5 %collective-permute-start = (bf16[2048,128]{1,0:T(8,128)(2,1)}, bf16[2048,128]{1,0:T(8,128)(2,1)S(1)}, u32[]{:S(2)}, u32[]{:S(2)}) collective-permute-start(bf16[2048,128]{1,0:T(8,128)(2,1)} %bitcast.43), channel_id=1, source_target_pairs={{0,256},{32,288},{64,320},{96,352},{128,384},{160,416},{192,448},{... | collective-permute-start | bytes 1572872 | tf_op jit(solution)/shard_map/ppermute | solution.py:40
  5.5 1.0 copy.14
  6.5 7.4 %collective-permute-done = bf16[2048,128]{1,0:T(8,128)(2,1)S(1)} collective-permute-done((bf16[2048,128]{1,0:T(8,128)(2,1)}, bf16[2048,128]{1,0:T(8,128)(2,1)S(1)}, u32[]{:S(2)}, u32[]{:S(2)}) %collective-permute-start) | collective-permute-done | bytes 524320 | tf_op jit(solution)/shard_map/ppermute | solution.py:40
  14.0 1.1 select_bitcast_fusion.1
  15.1 1.1 pad_maximum_fusion
  16.2 7.6 %collective-permute-start.1 = (bf16[2,2048,128]{2,1,0:T(8,128)(2,1)}, bf16[2,2048,128]{2,1,0:T(8,128)(2,1)S(1)}, u32[]{:S(2)}, u32[]{:S(2)}) collective-permute-start(bf16[2,2048,128]{2,1,0:T(8,128)(2,1)} %pad_maximum_fusion), channel_id=1, source_target_pairs={{0,32},{32,0},{64,96},{96,64},{128,160},{160,128},{192,224},{224,1... | collective-permute-start | bytes 3145736 | tf_op jit(solution)/shard_map/ppermute | solution.py:42
  23.8 2.3 %mul.17 = f32[1024,16,128]{2,1,0:T(8,128)S(1)} broadcast(f32[1024,16]{1,0:T(8,128)S(1)} %copy.14), dimensions={0,1} | broadcast | bytes 8454144 | tf_op jit(solution)/shard_map/mul | solution.py:47
  26.1 0.0 copy-start.1
  26.1 7.3 %fusion = bf16[1024,2048]{1,0:T(8,128)(2,1)} fusion(f32[128,8,16,128]{3,2,1,0:T(8,128)S(1)} %bitcast.37, bf16[1024,2048]{1,0:T(8,128)(2,1)} %param.6), kind=kLoop, calls=%fused_computation.1 | loop fusion | flops 6291456 | bytes 16777216 | tf_op jit(solution)/shard_map/convert_element_type | solution.py:47
  33.4 1.9 %collective-permute-start.2 = (bf16[1024,2048]{1,0:T(8,128)(2,1)}, bf16[1024,2048]{1,0:T(8,128)(2,1)}, u32[]{:S(2)}, u32[]{:S(2)}) collective-permute-start(bf16[1024,2048]{1,0:T(8,128)(2,1)} %fusion), channel_id=1, source_target_pairs={{0,32},{32,0},{64,96},{96,64},{128,160},{160,128},{192,224},{224,1... | collective-permute-start | bytes 12582920 | tf_op jit(solution)/shard_map/ppermute | solution.py:48
  35.3 0.0 copy-done.1
  35.4 1.1 broadcast_in_dim.4
  36.5 4.6 %all-to-all-start = ((bf16[8,32,2048]{2,1,0:T(8,128)(2,1)}), bf16[8,32,2048]{2,1,0:T(8,128)(2,1)}, u32[]{:S(2)}, u32[]{:S(2)}) async-start(bf16[8,32,2048]{2,1,0:T(8,128)(2,1)} %bitcast.9), calls=%async_computation | async-start | bytes 2097152 | tf_op jit(solution)/shard_map/all_to_all | solution.py:34
  41.1 0.0 collective-permute-done.1
  41.1 0.1 broadcast_select_fusion.3
  41.2 0.1 slice_bitcast_fusion.2
  41.4 14.9 %all-to-all-done = bf16[8,32,2048]{2,1,0:T(8,128)(2,1)} async-done(((bf16[8,32,2048]{2,1,0:T(8,128)(2,1)}), bf16[8,32,2048]{2,1,0:T(8,128)(2,1)}, u32[]{:S(2)}, u32[]{:S(2)}) %all-to-all-start) | async-done | bytes 1048608 | tf_op jit(solution)/shard_map/all_to_all | solution.py:34
  56.3 2.0 %fusion.19 = bf16[256,512]{0,1:T(8,128)(2,1)S(1)} fusion(bf16[256,2048]{1,0:T(8,128)(2,1)} %bitcast.10, bf16[2048,128]{1,0:T(8,128)(2,1)S(1)} %get-tuple-element.12, bf16[2048,128]{1,0:T(8,128)(2,1)S(1)} %get-tuple-element.15, bf16[2048,128]{1,0:T(8,128)(2,1)S(1)} %get-tuple-element.11, bf16[2048,128]{1,0:T(8,128)(2,1)S(1)} %get-tuple-element.16), kind=kOutput, calls=%fused_computation.18 | convolution fusion | flops 545390592 | bytes 3407872 | tf_op jit(solution)/shard_map/dot_general | solution.py:53
  58.3 0.1 copy.12
  58.4 0.2 broadcast_in_dim.5
  58.6 30.5 %all_to_all.20 = bf16[8,256,512]{2,1,0:T(8,128)(2,1)S(1)} all-to-all(bf16[8,256,512]{2,1,0:T(8,128)(2,1)S(1)} %broadcast_in_dim.5), channel_id=1, replica_groups={{0,64,128,192,256,320,384,448},{32,96,160,224,288,352,416,480},{1,65,12..., dimensions={0} | all-to-all | bytes 4194304 | tf_op jit(solution)/shard_map/all_to_all | solution.py:54
  89.1 2.1 %reshape.39 = bf16[2,4,4,4,16,2,256]{6,5,4,3,2,1,0:T(2,128)(2,1)} reshape(bf16[8,256,512]{2,1,0:T(8,128)(2,1)S(1)} %all_to_all.20) | data formatting | bytes 4194304 | tf_op jit(solution)/shard_map/reshape | solution.py:60
  91.2 5.2 %copy.13 = bf16[4,2,4,16,2,4,256]{6,5,4,3,2,1,0:T(4,128)(2,1)S(1)} copy(bf16[4,2,4,16,2,4,256]{6,4,3,0,2,5,1:T(2,128)(2,1)} %bitcast.38) | data formatting | bytes 4194304 | tf_op jit(solution)/shard_map/transpose | solution.py:61
  96.4 2.8 %reshape.40 = bf16[512,2048]{1,0:T(8,128)(2,1)} reshape(bf16[4,2,4,16,2,4,256]{6,5,4,3,2,1,0:T(4,128)(2,1)S(1)} %copy.13) | data formatting | bytes 4194304 | tf_op jit(solution)/shard_map/reshape | solution.py:62
  99.2 0.0 copy-start
  99.2 0.0 collective-permute-done.2
  99.2 3.9 %broadcast_select_fusion.1 = (bf16[1024,2048]{1,0:T(8,128)(2,1)S(1)}, bf16[1024,2048]{1,0:T(8,128)(2,1)S(1)}) fusion(bf16[1024,2048]{1,0:T(8,128)(2,1)} %fusion, bf16[1024,2048]{1,0:T(8,128)(2,1)} %collective-permute-done.2, pred[]{:T(512)S(6)} %eq.6), kind=kLoop, calls=%fused_computation.7 | loop fusion | flops 4194304 | bytes 16777216 | tf_op jit(solution)/shard_map/jit(_where)/select_n | solution.py:50
  103.1 0.1 copy-done
  103.2 7.6 %fusion.5 = bf16[512,2048]{1,0:T(8,128)(2,1)S(1)} fusion(bf16[512,2048]{1,0:T(8,128)(2,1)S(1)} %copy-done, bf16[1024,2048]{1,0:T(8,128)(2,1)S(1)} %get-tuple-element.6, bf16[1024,2048]{1,0:T(8,128)(2,1)S(1)} %get-tuple-element.5), kind=kOutput, calls=%fused_computation.8 | convolution fusion | flops 4312793088 | bytes 12582912 | tf_op jit(solution)/shard_map/dot_general | solution.py:65
  110.8 24.8 %all_to_all.21 = bf16[4,128,2048]{2,1,0:T(8,128)(2,1)S(1)} all-to-all(bf16[4,128,2048]{2,1,0:T(8,128)(2,1)S(1)} %bitcast.40), channel_id=1, replica_groups={{0,1,2,3},{4,5,6,7},{8,9,10,11},{12,13,14,15},{16,17,18,19},{20,21,22,2..., dimensions={0} | all-to-all | bytes 4194304 | tf_op jit(solution)/shard_map/all_to_all | solution.py:68
  135.6 0.4 reduce_sum.21
  136.0 0.4 reshape.42
  136.4 0.1 copy.15
  136.5 49.1 %all_to_all.22 = bf16[16,16,1024]{2,1,0:T(8,128)(2,1)S(1)} all-to-all(bf16[16,16,1024]{2,1,0:T(8,128)(2,1)S(1)} %bitcast.42), channel_id=1, replica_groups={{0,32,4,36,8,40,12,44,16,48,20,52,24,56,28,60},{1,33,5,37,9,41,13,45,17..., dimensions={0} | all-to-all | bytes 1048576 | tf_op jit(solution)/shard_map/all_to_all | solution.py:79
  185.6 0.1 convert_reduce_fusion
  185.7 0.7 broadcast_multiply_fusion
  (1 shorter events, 0.0 us)
Async XLA Ops:
  0.0 14.0 %collective-permute-start = (bf16[2048,128]{1,0:T(8,128)(2,1)}, bf16[2048,128]{1,0:T(8,128)(2,1)S(1)}, u32[]{:S(2)}, u32[]{:S(2)}) collective-permute-start(bf16[2048,128]{1,0:T(8,128)(2,1)} %bitcast.43), channel_id=1, source_target_pairs={{0,256},{32,288},{64,320},{96,352},{128,384},{160,416},{192,448},{... | collective-permute-start | bytes 1572872 | tf_op jit(solution)/shard_map/ppermute | solution.py:40
  16.2 24.9 %collective-permute-start.1 = (bf16[2,2048,128]{2,1,0:T(8,128)(2,1)}, bf16[2,2048,128]{2,1,0:T(8,128)(2,1)S(1)}, u32[]{:S(2)}, u32[]{:S(2)}) collective-permute-start(bf16[2,2048,128]{2,1,0:T(8,128)(2,1)} %pad_maximum_fusion), channel_id=1, source_target_pairs={{0,32},{32,0},{64,96},{96,64},{128,160},{160,128},{192,224},{224,1... | collective-permute-start | bytes 3145736 | tf_op jit(solution)/shard_map/ppermute | solution.py:42
  26.1 9.2 %copy-start.1 = (bf16[64,2048]{1,0:T(8,128)(2,1)S(1)}, bf16[64,2048]{1,0:T(8,128)(2,1)}, u32[]{:S(2)}) copy-start(bf16[64,2048]{1,0:T(8,128)(2,1)} %param.4) | copy-start | bytes 786436
  33.4 65.8 %collective-permute-start.2 = (bf16[1024,2048]{1,0:T(8,128)(2,1)}, bf16[1024,2048]{1,0:T(8,128)(2,1)}, u32[]{:S(2)}, u32[]{:S(2)}) collective-permute-start(bf16[1024,2048]{1,0:T(8,128)(2,1)} %fusion), channel_id=1, source_target_pairs={{0,32},{32,0},{64,96},{96,64},{128,160},{160,128},{192,224},{224,1... | collective-permute-start | bytes 12582920 | tf_op jit(solution)/shard_map/ppermute | solution.py:48
  36.5 19.8 %all-to-all-start = ((bf16[8,32,2048]{2,1,0:T(8,128)(2,1)}), bf16[8,32,2048]{2,1,0:T(8,128)(2,1)}, u32[]{:S(2)}, u32[]{:S(2)}) async-start(bf16[8,32,2048]{2,1,0:T(8,128)(2,1)} %bitcast.9), calls=%async_computation | async-start | bytes 2097152 | tf_op jit(solution)/shard_map/all_to_all | solution.py:34
  99.2 4.1 %copy-start = (bf16[512,2048]{1,0:T(8,128)(2,1)S(1)}, bf16[512,2048]{1,0:T(8,128)(2,1)}, u32[]{:S(2)}) copy-start(bf16[512,2048]{1,0:T(8,128)(2,1)} %reshape.40) | copy-start | bytes 6291460

commit v2 on v0

v2 whole, which is shorter than its diff:
```python
import jax
import jax.numpy as jnp
from jax import lax
from jax.experimental import pallas as pl
from jax.experimental.pallas import tpu as pltpu
from jax.sharding import PartitionSpec as P

CORES, ROWS_Y, ROWS_X = 2, 4, 2
PAIRS, SIDES = 8, 2
NEAR = 2 * SIDES
MIB = 1 << 20


def dequantize(codes_ref, scales_ref, out_ref):
    block = codes_ref.shape[1] // scales_ref.shape[1]
    for b in range(scales_ref.shape[1]):
        columns = slice(b * block, (b + 1) * block)
        entries = codes_ref[:, columns].astype(jnp.float32) * scales_ref[:, b : b + 1]
        out_ref[:, columns] = entries.astype(out_ref.dtype)


def dequantized(codes, scales):
    rows, width = codes.shape
    tile = 256
    return pl.pallas_call(
        dequantize,
        grid=(rows // tile,),
        in_specs=[
            pl.BlockSpec((tile, width), lambda r: (r, 0)),
            pl.BlockSpec((tile, scales.shape[1]), lambda r: (r, 0)),
        ],
        out_specs=pl.BlockSpec((tile, width), lambda r: (r, 0)),
        out_shape=jax.ShapeDtypeStruct(codes.shape, jnp.bfloat16),
        compiler_params=pltpu.CompilerParams(vmem_limit_bytes=24 * MIB),
        cost_estimate=pl.CostEstimate(
            flops=rows * width, bytes_accessed=4 * rows * width, transcendentals=0
        ),
    )(codes, scales)


def condition(core_ref, *refs):
    grads_refs, column_refs, (out_ref, grads, weights) = refs[:ROWS_Y], refs[ROWS_Y:-3], refs[-3:]
    rows, columns = grads_refs[0].shape[0], column_refs[0].shape[1]
    for d, ref in enumerate(grads_refs):
        grads[d * rows : (d + 1) * rows, :] = ref[...]
    for core in range(CORES):

        @pl.when(core_ref[0] == core)
        def _():
            for i, ref in enumerate(column_refs):
                at = (i ^ core) * columns
                weights[:, at : at + columns] = ref[...]

    part = jnp.dot(grads[...], weights[...], preferred_element_type=jnp.float32)
    for chip in range(out_ref.shape[0]):
        out_ref[chip] = part.astype(out_ref.dtype)


def conditioned_for(core, chips, grads, columns):
    rows, width = len(grads) * grads[0].shape[0], grads[0].shape[1]
    out = len(columns) * columns[0].shape[1]
    return pl.pallas_call(
        condition,
        in_specs=[pl.BlockSpec(memory_space=pltpu.SMEM)]
        + [pl.BlockSpec(memory_space=pltpu.VMEM)] * (len(grads) + len(columns)),
        out_specs=pl.BlockSpec(memory_space=pltpu.VMEM),
        out_shape=jax.ShapeDtypeStruct((chips, rows, out), jnp.bfloat16),
        scratch_shapes=[pltpu.VMEM((rows, width), jnp.bfloat16), pltpu.VMEM((width, out), jnp.bfloat16)],
        compiler_params=pltpu.CompilerParams(vmem_limit_bytes=24 * MIB),
        cost_estimate=pl.CostEstimate(
            flops=2 * rows * width * out,
            bytes_accessed=2 * (rows * width + width * out + chips * rows * out),
            transcendentals=0,
        ),
    )(core, *grads, *columns)


def score(core_ref, parts_ref, mine_ref, theirs_ref, out_ref, queries):
    chip_rows, columns = parts_ref.shape[1], parts_ref.shape[2] // ROWS_X
    rows = chip_rows // ROWS_Y
    step, half = pl.program_id(0), pl.num_programs(0) // CORES

    @pl.when(step == 0)
    def _():
        for x in range(ROWS_X):
            for y in range(ROWS_Y):
                for k in range(ROWS_X):
                    at = ((x ^ k) * ROWS_Y + y) * columns
                    for d in range(ROWS_Y):
                        to = x * chip_rows + (y - d) % ROWS_Y * rows
                        queries[to : to + rows, at : at + columns] = parts_ref[
                            x * ROWS_Y + y, d * rows : (d + 1) * rows, k * columns : (k + 1) * columns
                        ]

    def times(store_ref):
        term = lax.dot_general(
            queries[...], store_ref[...], (((1,), (1,)), ((), ())),
            preferred_element_type=jnp.float32,
        ).astype(out_ref.dtype)
        tile = term.shape[0] // (PAIRS * NEAR)
        for pair in range(PAIRS):
            for near in range(NEAR):
                row = (pair * NEAR + near) * tile
                out_ref[near, pair * tile : (pair + 1) * tile, :] = term[row : row + tile, :]

    @pl.when(step < half)
    def _():
        times(mine_ref)

    @pl.when(step >= half)
    def _():
        times(theirs_ref)


def scores_of(core, parts, mine, theirs):
    chips, chip_rows, columns = parts.shape
    rows = ROWS_X * chip_rows
    examples, width = mine.shape
    tile = 256
    half = examples // tile
    whole = lambda n, core_ref: (0, 0, 0)
    return pl.pallas_call(
        score,
        grid_spec=pltpu.PrefetchScalarGridSpec(
            num_scalar_prefetch=1,
            grid=(CORES * half,),
            in_specs=[
                pl.BlockSpec((chips, chip_rows, columns), whole),
                pl.BlockSpec((tile, width), lambda n, core_ref: (jnp.minimum(n, half - 1), 0)),
                pl.BlockSpec((tile, width), lambda n, core_ref: (jnp.maximum(n - half, 0), 0)),
            ],
            out_specs=pl.BlockSpec(
                (NEAR, rows // NEAR, tile),
                lambda n, core_ref: (0, 0, (n + core_ref[0] * half) % (CORES * half)),
            ),
            scratch_shapes=[pltpu.VMEM((rows, width), jnp.bfloat16)],
        ),
        out_shape=jax.ShapeDtypeStruct((NEAR, rows // NEAR, CORES * examples), jnp.bfloat16),
        compiler_params=pltpu.CompilerParams(vmem_limit_bytes=32 * MIB),
        cost_estimate=pl.CostEstimate(
            flops=2 * rows * width * CORES * examples,
            bytes_accessed=2 * (rows * width + CORES * (width + rows) * examples),
            transcendentals=0,
        ),
    )(core, parts, mine, theirs)


def add(terms_ref, out_ref):
    examples = out_ref.shape[2]
    for c in range(CORES):
        columns = slice(c * examples, (c + 1) * examples)
        total = terms_ref[0, :, columns].astype(jnp.float32)
        for i in range(1, NEAR):
            total += terms_ref[i, :, columns].astype(jnp.float32)
        for p in range(out_ref.shape[0] // CORES):
            tile = out_ref.shape[1]
            out_ref[p * CORES + c] = total[p * tile : (p + 1) * tile].astype(out_ref.dtype)


def added(terms, tile, examples):
    steps = 4
    rows = terms.shape[1] // steps
    return pl.pallas_call(
        add,
        grid=(steps,),
        in_specs=[pl.BlockSpec((NEAR, rows, CORES * examples), lambda s: (0, s, 0))],
        out_specs=pl.BlockSpec((PAIRS * CORES // steps, tile, examples), lambda s: (s, 0, 0)),
        out_shape=jax.ShapeDtypeStruct((PAIRS * CORES, tile, examples), jnp.bfloat16),
        compiler_params=pltpu.CompilerParams(vmem_limit_bytes=16 * MIB),
        cost_estimate=pl.CostEstimate(
            flops=terms.size, bytes_accessed=3 * terms.size, transcendentals=0
        ),
    )(terms)


def shards(query_grads, precond, codes, scales):
    own_queries, width = query_grads.shape
    examples = codes.shape[0]
    ex_size, slots = lax.axis_size("ex"), lax.axis_size("dim")
    tile = own_queries * ex_size // slots // CORES
    chips = ROWS_X * ROWS_Y
    core = lax.axis_index("ex") % CORES
    core_swap = [(e, e ^ 1) for e in range(ex_size)]
    x_swap = [(e, e ^ (ROWS_Y * CORES)) for e in range(ex_size)]

    def y_shift(d):
        width_y = ROWS_Y * CORES
        return [(e, e // width_y * width_y + (e + d * CORES) % width_y) for e in range(ex_size)]

    same_core = [[chip * CORES + c for chip in range(chips)] for c in range(CORES)]
    near = [[pair * NEAR + i for i in range(NEAR)] for pair in range(PAIRS)]
    far = [
        [(chip * CORES + c) * slots + pair * NEAR + i for pair in range(PAIRS) for c in range(CORES)]
        for chip in range(chips)
        for i in range(NEAR)
    ]

    rows = query_grads.reshape(2, CORES, tile, width)
    kept = jnp.where(core == 0, rows[:, 0], rows[:, 1])
    swapped = lax.ppermute(jnp.where(core == 0, rows[:, 1], rows[:, 0]), "ex", core_swap)
    ours = jnp.concatenate(
        [jnp.where(core == 0, kept, swapped), jnp.where(core == 0, swapped, kept)], axis=0
    ).reshape(CORES * 2 * tile, width)
    above, below = (lax.ppermute(ours, "ex", y_shift(d)) for d in (1, ROWS_Y - 1))

    own = precond[0]
    across = lax.ppermute(own, "ex", x_swap)
    own_other = lax.ppermute(own, "ex", core_swap)
    across, own_other, above, below = lax.optimization_barrier((across, own_other, above, below))
    opposite = lax.ppermute(above, "ex", y_shift(1))
    across_other = lax.ppermute(across, "ex", core_swap)
    mine = dequantized(codes, scales)
    across_other, opposite, mine = lax.optimization_barrier((across_other, opposite, mine))

    parts = lax.all_to_all(
        conditioned_for(
            core.reshape(1), chips,
            [ours, above, opposite, below],
            [own, own_other, across, across_other],
        ),
        "ex", 0, 0, tiled=True, axis_index_groups=same_core,
    )

    theirs = lax.ppermute(mine, "ex", core_swap)

    terms = lax.all_to_all(
        scores_of(core.reshape(1), parts, mine, theirs),
        "dim", 0, 0, tiled=True, axis_index_groups=near,
    )
    sums = lax.all_to_all(
        added(terms, tile, examples), ("ex", "dim"), 0, 0, tiled=True, axis_index_groups=far
    )
    total = jnp.sum(sums.astype(jnp.float32).reshape(PAIRS, CORES * tile, examples), axis=0)
    return total * float(width * slots) ** (-0.5)


def solution(mesh):
    placed = (P("ex", "dim"), P("dim", None, "ex"), P("ex", "dim"), P("ex", "dim"))
    return jax.shard_map(
        shards, mesh=mesh, in_specs=placed, out_specs=P("dim", "ex"), check_vma=False
    )
```

time: 322 us -> 159 us (0.49)
  the two profiles are of different devices: /device:TPU:8 before, /device:TPU:1 now
where the time goes in v2:
time: 159 us; the launch traced here: 158 us
  blocking collectives  103 us (65%)
  starting transfers between devices  25.8 us (16%)
  waiting for transfers between devices  11.6 us (7%)
  Pallas kernels  10.9 us (7%)
  local copies, waits for them, and re-layouts  3.22 us (2%)
  other arithmetic  2.76 us (2%)
    all_to_all x1, blocking collectives, shards(): lax.all_to_all(added(terms, tile, examples), ('ex', 'dim'), 0, 0, tiled=T...  47.4 us
    all_to_all x1, blocking collectives, shards(): lax.all_to_all(conditioned_for(core.reshape(1), chips, [ours, above, oppo...  30.1 us
    all_to_all x1, blocking collectives, shards(): lax.all_to_all(scores_of(core.reshape(1), parts, mine, theirs), 'dim', 0,...  25.6 us
    ppermute x1, starting transfers between devices, shards(): lax.ppermute(jnp.where(core == 0, rows[:, 1], rows[:, 0]), 'ex', core_swap)  8.79 us
    pallas_call x1, Pallas kernels, scores_of(): pl.pallas_call(score, grid_spec=pltpu.PrefetchScalarGridSpec(num_scalar_p...  6.66 us
    ppermute x2, waiting for transfers between devices, shards(): lax.ppermute(ours, 'ex', y_shift(d))  6.55 us
    ppermute x2, starting transfers between devices, shards(): lax.ppermute(ours, 'ex', y_shift(d))  5.28 us
    ppermute x1, waiting for transfers between devices, shards(): opposite = lax.ppermute(above, 'ex', y_shift(1))  3.31 us
  transfers between devices with their start and end apart: 8, of which 4 were waited for; matrix products, arithmetic and copies ran while one was open for 1% of the time, Pallas kernels for 2%

profile of v2, /device:TPU:1, one launch (start us, length us, event | category | flops | bytes accessed | tf_op | source)
XLA Modules:
  0.0 157.5 jit_solution(5790675236813709125)
XLA Ops:
  0.0 1.0 select_bitcast_fusion
  1.0 8.8 %collective-permute-start = (bf16[2,16,2048]{2,1,0:T(8,128)(2,1)S(1)}, bf16[2,16,2048]{2,1,0:T(8,128)(2,1)S(1)}, u32[]{:S(2)}, u32[]{:S(2)}) collective-permute-start(bf16[2,16,2048]{2,1,0:T(8,128)(2,1)S(1)} %select_bitcast_fusion), channel_id=1, source_target_pairs={{0,32},{32,0},{64,96},{96,64},{128,160},{160,128},{192,224},{224,1... | collective-permute-start | bytes 393224 | tf_op jit(solution)/shard_map/ppermute | solution.py:200
  9.8 1.9 %collective-permute-start.2 = (bf16[2048,128]{1,0:T(8,128)(2,1)}, bf16[2048,128]{1,0:T(8,128)(2,1)S(1)}, u32[]{:S(2)}, u32[]{:S(2)}) collective-permute-start(bf16[2048,128]{1,0:T(8,128)(2,1)} %bitcast.36), channel_id=1, source_target_pairs={{0,32},{32,0},{64,96},{96,64},{128,160},{160,128},{192,224},{224,1... | collective-permute-start | bytes 1572872 | tf_op jit(solution)/shard_map/ppermute | solution.py:208
  11.7 1.9 %collective-permute-start.1 = (bf16[2048,128]{1,0:T(8,128)(2,1)}, bf16[2048,128]{1,0:T(8,128)(2,1)S(1)}, u32[]{:S(2)}, u32[]{:S(2)}) collective-permute-start(bf16[2048,128]{1,0:T(8,128)(2,1)} %bitcast.37), channel_id=1, source_target_pairs={{0,256},{32,288},{64,320},{96,352},{128,384},{160,416},{192,448},{... | collective-permute-start | bytes 1572872 | tf_op jit(solution)/shard_map/ppermute | solution.py:207
  13.6 0.0 collective-permute-done
  13.7 1.0 bitcast_select_fusion.1
  14.7 2.0 %collective-permute-start.4 = (bf16[64,2048]{1,0:T(8,128)(2,1)S(1)}, bf16[64,2048]{1,0:T(8,128)(2,1)S(1)}, u32[]{:S(2)}, u32[]{:S(2)}) collective-permute-start(bf16[64,2048]{1,0:T(8,128)(2,1)S(1)} %bitcast.33), channel_id=1, source_target_pairs={{0,192},{32,224},{64,0},{96,32},{128,64},{160,96},{192,128},{224,1... | collective-permute-start | bytes 786440 | tf_op jit(solution)/shard_map/ppermute | solution.py:204
  16.7 3.3 %collective-permute-start.3 = (bf16[64,2048]{1,0:T(8,128)(2,1)S(1)}, bf16[64,2048]{1,0:T(8,128)(2,1)S(1)}, u32[]{:S(2)}, u32[]{:S(2)}) collective-permute-start(bf16[64,2048]{1,0:T(8,128)(2,1)S(1)} %bitcast.34), channel_id=1, source_target_pairs={{0,64},{32,96},{64,128},{96,160},{128,192},{160,224},{192,0},{224,... | collective-permute-start | bytes 786440 | tf_op jit(solution)/shard_map/ppermute | solution.py:204
  20.0 4.0 %collective-permute-done.4.refs_3_ = bf16[64,2048]{1,0:T(8,128)(2,1)S(1)} collective-permute-done((bf16[64,2048]{1,0:T(8,128)(2,1)S(1)}, bf16[64,2048]{1,0:T(8,128)(2,1)S(1)}, u32[]{:S(2)}, u32[]{:S(2)}) %collective-permute-start.4) | collective-permute-done | bytes 262176 | tf_op jit(solution)/shard_map/ppermute | solution.py:204
  24.0 2.6 %collective-permute-done.3.refs_1_ = bf16[64,2048]{1,0:T(8,128)(2,1)S(1)} collective-permute-done((bf16[64,2048]{1,0:T(8,128)(2,1)S(1)}, bf16[64,2048]{1,0:T(8,128)(2,1)S(1)}, u32[]{:S(2)}, u32[]{:S(2)}) %collective-permute-start.3) | collective-permute-done | bytes 262176 | tf_op jit(solution)/shard_map/ppermute | solution.py:204
  26.6 0.0 collective-permute-done.2.refs_5_
  26.6 1.8 %collective-permute-done.1.refs_6_ = bf16[2048,128]{1,0:T(8,128)(2,1)S(1)} collective-permute-done((bf16[2048,128]{1,0:T(8,128)(2,1)}, bf16[2048,128]{1,0:T(8,128)(2,1)S(1)}, u32[]{:S(2)}, u32[]{:S(2)}) %collective-permute-start.1) | collective-permute-done | bytes 524320 | tf_op jit(solution)/shard_map/ppermute | solution.py:207
  28.3 3.2 %collective-permute-start.5 = (bf16[2048,128]{1,0:T(8,128)(2,1)S(1)}, bf16[2048,128]{1,0:T(8,128)(2,1)S(1)}, u32[]{:S(2)}, u32[]{:S(2)}) collective-permute-start(bf16[2048,128]{1,0:T(8,128)(2,1)S(1)} %collective-permute-done.1.refs_6_), channel_id=1, source_target_pairs={{0,32},{32,0},{64,96},{96,64},{128,160},{160,128},{192,224},{224,1... | collective-permute-start | bytes 1572872 | tf_op jit(solution)/shard_map/ppermute | solution.py:211
  31.6 1.9 %collective-permute-start.6 = (bf16[64,2048]{1,0:T(8,128)(2,1)S(1)}, bf16[64,2048]{1,0:T(8,128)(2,1)S(1)}, u32[]{:S(2)}, u32[]{:S(2)}) collective-permute-start(bf16[64,2048]{1,0:T(8,128)(2,1)S(1)} %collective-permute-done.3.refs_1_), channel_id=1, source_target_pairs={{0,64},{32,96},{64,128},{96,160},{128,192},{160,224},{192,0},{224,... | collective-permute-start | bytes 786440 | tf_op jit(solution)/shard_map/ppermute | solution.py:210
  33.5 1.0 copy.7.scales_ref
  34.5 0.0 copy-start
  34.6 2.2 %copy-done = bf16[1024,2048]{1,0:T(8,128)(2,1)S(1)} copy-done((bf16[1024,2048]{1,0:T(8,128)(2,1)S(1)}, bf16[1024,2048]{1,0:T(8,128)(2,1)}, u32[]{:S(2)}) %copy-start) | copy-done | bytes 4194328
  36.7 0.0 copy-start.1
  36.7 2.5 %shard_map.46.mine_ref = bf16[1024,2048]{1,0:T(8,128)(2,1)S(1)} custom-call(bf16[1024,2048]{1,0:T(8,128)(2,1)S(1)} %copy-done, f32[1024,16]{1,0:T(8,128)S(1)} %copy.7.scales_ref), custom_call_target="tpu_custom_call" | custom-call | flops 2097152 | bytes 8388608 | tf_op jit(solution)/shard_map/pallas_call | solution.py:25
  39.3 3.3 %collective-permute-done.6.refs_2_ = bf16[64,2048]{1,0:T(8,128)(2,1)S(1)} collective-permute-done((bf16[64,2048]{1,0:T(8,128)(2,1)S(1)}, bf16[64,2048]{1,0:T(8,128)(2,1)S(1)}, u32[]{:S(2)}, u32[]{:S(2)}) %collective-permute-start.6) | collective-permute-done | bytes 262176 | tf_op jit(solution)/shard_map/ppermute | solution.py:210
  42.6 0.0 collective-permute-done.5.refs_7_
  42.6 2.7 %collective-permute-start.7 = (bf16[1024,2048]{1,0:T(8,128)(2,1)S(1)}, bf16[1024,2048]{1,0:T(8,128)(2,1)S(1)}, u32[]{:S(2)}, u32[]{:S(2)}) collective-permute-start(bf16[1024,2048]{1,0:T(8,128)(2,1)S(1)} %shard_map.46.mine_ref), channel_id=1, source_target_pairs={{0,32},{32,0},{64,96},{96,64},{128,160},{160,128},{192,224},{224,1... | collective-permute-start | bytes 12582920 | tf_op jit(solution)/shard_map/ppermute | solution.py:224
  45.3 0.0 copy-done.1
  45.3 1.2 shard_map.47
  46.5 30.1 %all_to_all.15.parts_ref = bf16[8,256,512]{2,1,0:T(8,128)(2,1)S(1)} all-to-all(bf16[8,256,512]{2,1,0:T(8,128)(2,1)S(1)} %shard_map.47), channel_id=1, replica_groups={{0,64,128,192,256,320,384,448},{32,96,160,224,288,352,416,480},{1,65,12..., dimensions={0} | all-to-all | bytes 4194304 | tf_op jit(solution)/shard_map/all_to_all | solution.py:215
  76.6 0.0 collective-permute-done.7.theirs_ref
  76.6 6.7 %shard_map.48 = bf16[4,128,2048]{2,1,0:T(8,128)(2,1)S(1)} custom-call(s32[1]{0:T(128)} %bitcast.core_ref, bf16[8,256,512]{2,1,0:T(8,128)(2,1)S(1)} %all_to_all.15.parts_ref, bf16[1024,2048]{1,0:T(8,128)(2,1)S(1)} %shard_map.46.mine_ref, bf16[1024,2048]{1,0:T(8,128)(2,1)S(1)} %collective-permute-done.7.theirs_ref), custom_call_target="tpu_custom_call" | custom-call | flops 4294967296 | bytes 12582912 | tf_op jit(solution)/shard_map/pallas_call | solution.py:122
  83.3 25.6 %all_to_all.16.terms_ref = bf16[4,128,2048]{2,1,0:T(8,128)(2,1)S(1)} all-to-all(bf16[4,128,2048]{2,1,0:T(8,128)(2,1)S(1)} %shard_map.48), channel_id=1, replica_groups={{0,1,2,3},{4,5,6,7},{8,9,10,11},{12,13,14,15},{16,17,18,19},{20,21,22,2..., dimensions={0} | all-to-all | bytes 4194304 | tf_op jit(solution)/shard_map/all_to_all | solution.py:226
  108.9 0.5 shard_map.49
  109.4 47.4 %all_to_all.17 = bf16[16,16,1024]{2,1,0:T(8,128)(2,1)S(1)} all-to-all(bf16[16,16,1024]{2,1,0:T(8,128)(2,1)S(1)} %shard_map.49), channel_id=1, replica_groups={{0,32,4,36,8,40,12,44,16,48,20,52,24,56,28,60},{1,33,5,37,9,41,13,45,17..., dimensions={0} | all-to-all | bytes 1048576 | tf_op jit(solution)/shard_map/all_to_all | solution.py:230
  156.8 0.1 convert_reduce_fusion
  156.9 0.7 broadcast_multiply_fusion
  (1 shorter events, 0.0 us)
Async XLA Ops:
  1.0 12.7 %collective-permute-start = (bf16[2,16,2048]{2,1,0:T(8,128)(2,1)S(1)}, bf16[2,16,2048]{2,1,0:T(8,128)(2,1)S(1)}, u32[]{:S(2)}, u32[]{:S(2)}) collective-permute-start(bf16[2,16,2048]{2,1,0:T(8,128)(2,1)S(1)} %select_bitcast_fusion), channel_id=1, source_target_pairs={{0,32},{32,0},{64,96},{96,64},{128,160},{160,128},{192,224},{224,1... | collective-permute-start | bytes 393224 | tf_op jit(solution)/shard_map/ppermute | solution.py:200
  9.8 16.8 %collective-permute-start.2 = (bf16[2048,128]{1,0:T(8,128)(2,1)}, bf16[2048,128]{1,0:T(8,128)(2,1)S(1)}, u32[]{:S(2)}, u32[]{:S(2)}) collective-permute-start(bf16[2048,128]{1,0:T(8,128)(2,1)} %bitcast.36), channel_id=1, source_target_pairs={{0,32},{32,0},{64,96},{96,64},{128,160},{160,128},{192,224},{224,1... | collective-permute-start | bytes 1572872 | tf_op jit(solution)/shard_map/ppermute | solution.py:208
  11.7 16.6 %collective-permute-start.1 = (bf16[2048,128]{1,0:T(8,128)(2,1)}, bf16[2048,128]{1,0:T(8,128)(2,1)S(1)}, u32[]{:S(2)}, u32[]{:S(2)}) collective-permute-start(bf16[2048,128]{1,0:T(8,128)(2,1)} %bitcast.37), channel_id=1, source_target_pairs={{0,256},{32,288},{64,320},{96,352},{128,384},{160,416},{192,448},{... | collective-permute-start | bytes 1572872 | tf_op jit(solution)/shard_map/ppermute | solution.py:207
  14.7 9.3 %collective-permute-start.4 = (bf16[64,2048]{1,0:T(8,128)(2,1)S(1)}, bf16[64,2048]{1,0:T(8,128)(2,1)S(1)}, u32[]{:S(2)}, u32[]{:S(2)}) collective-permute-start(bf16[64,2048]{1,0:T(8,128)(2,1)S(1)} %bitcast.33), channel_id=1, source_target_pairs={{0,192},{32,224},{64,0},{96,32},{128,64},{160,96},{192,128},{224,1... | collective-permute-start | bytes 786440 | tf_op jit(solution)/shard_map/ppermute | solution.py:204
  16.7 9.8 %collective-permute-start.3 = (bf16[64,2048]{1,0:T(8,128)(2,1)S(1)}, bf16[64,2048]{1,0:T(8,128)(2,1)S(1)}, u32[]{:S(2)}, u32[]{:S(2)}) collective-permute-start(bf16[64,2048]{1,0:T(8,128)(2,1)S(1)} %bitcast.34), channel_id=1, source_target_pairs={{0,64},{32,96},{64,128},{96,160},{128,192},{160,224},{192,0},{224,... | collective-permute-start | bytes 786440 | tf_op jit(solution)/shard_map/ppermute | solution.py:204
  28.3 14.3 %collective-permute-start.5 = (bf16[2048,128]{1,0:T(8,128)(2,1)S(1)}, bf16[2048,128]{1,0:T(8,128)(2,1)S(1)}, u32[]{:S(2)}, u32[]{:S(2)}) collective-permute-start(bf16[2048,128]{1,0:T(8,128)(2,1)S(1)} %collective-permute-done.1.refs_6_), channel_id=1, source_target_pairs={{0,32},{32,0},{64,96},{96,64},{128,160},{160,128},{192,224},{224,1... | collective-permute-start | bytes 1572872 | tf_op jit(solution)/shard_map/ppermute | solution.py:211
  31.6 11.0 %collective-permute-start.6 = (bf16[64,2048]{1,0:T(8,128)(2,1)S(1)}, bf16[64,2048]{1,0:T(8,128)(2,1)S(1)}, u32[]{:S(2)}, u32[]{:S(2)}) collective-permute-start(bf16[64,2048]{1,0:T(8,128)(2,1)S(1)} %collective-permute-done.3.refs_1_), channel_id=1, source_target_pairs={{0,64},{32,96},{64,128},{96,160},{128,192},{160,224},{192,0},{224,... | collective-permute-start | bytes 786440 | tf_op jit(solution)/shard_map/ppermute | solution.py:210
  34.5 2.2 %copy-start = (bf16[1024,2048]{1,0:T(8,128)(2,1)S(1)}, bf16[1024,2048]{1,0:T(8,128)(2,1)}, u32[]{:S(2)}) copy-start(bf16[1024,2048]{1,0:T(8,128)(2,1)} %codes_ref.1) | copy-start | bytes 12582916
  36.7 8.6 %copy-start.1 = (bf16[1,2048,128]{2,1,0:T(8,128)(2,1)S(1)}, bf16[1,2048,128]{2,1,0:T(8,128)(2,1)}, u32[]{:S(2)}) copy-start(bf16[1,2048,128]{2,1,0:T(8,128)(2,1)} %param.5) | copy-start | bytes 1572868
  42.6 34.0 %collective-permute-start.7 = (bf16[1024,2048]{1,0:T(8,128)(2,1)S(1)}, bf16[1024,2048]{1,0:T(8,128)(2,1)S(1)}, u32[]{:S(2)}, u32[]{:S(2)}) collective-permute-start(bf16[1024,2048]{1,0:T(8,128)(2,1)S(1)} %shard_map.46.mine_ref), channel_id=1, source_target_pairs={{0,32},{32,0},{64,96},{96,64},{128,160},{160,128},{192,224},{224,1... | collective-permute-start | bytes 12582920 | tf_op jit(solution)/shard_map/ppermute | solution.py:224

commit v3 on v2

v3 whole, which is shorter than its diff:
```python
import functools

import jax
import jax.numpy as jnp
from jax import lax
from jax.experimental import pallas as pl
from jax.experimental.pallas import tpu as pltpu
from jax.sharding import PartitionSpec as P

CORES, ROWS_Y, ROWS_X = 2, 4, 2
PAIRS, SIDES = 8, 2
NEAR = 2 * SIDES
MIB = 1 << 20


def dequantize(codes_ref, scales_ref, out_ref):
    block = codes_ref.shape[1] // scales_ref.shape[1]
    for b in range(scales_ref.shape[1]):
        columns = slice(b * block, (b + 1) * block)
        entries = codes_ref[:, columns].astype(jnp.float32) * scales_ref[:, b : b + 1]
        out_ref[:, columns] = entries.astype(out_ref.dtype)


def dequantized(codes, scales):
    rows, width = codes.shape
    tile = 256
    return pl.pallas_call(
        dequantize,
        grid=(rows // tile,),
        in_specs=[
            pl.BlockSpec((tile, width), lambda r: (r, 0)),
            pl.BlockSpec((tile, scales.shape[1]), lambda r: (r, 0)),
        ],
        out_specs=pl.BlockSpec((tile, width), lambda r: (r, 0)),
        out_shape=jax.ShapeDtypeStruct(codes.shape, jnp.bfloat16),
        compiler_params=pltpu.CompilerParams(vmem_limit_bytes=56 * MIB),
        cost_estimate=pl.CostEstimate(
            flops=rows * width, bytes_accessed=4 * rows * width, transcendentals=0
        ),
    )(codes, scales)


def copy_halves(grads_ref, out_ref):
    tile = out_ref.shape[1] // 2
    for b in range(2):
        for core in range(CORES):
            row = (b * CORES + core) * tile
            entries = grads_ref[row : row + tile, :]
            for y in range(ROWS_Y):
                out_ref[y * CORES + core, b * tile : (b + 1) * tile, :] = entries


def spread(grads, tile):
    rows, width = grads.shape
    return pl.pallas_call(
        copy_halves,
        in_specs=[pl.BlockSpec(memory_space=pltpu.VMEM)],
        out_specs=pl.BlockSpec(memory_space=pltpu.VMEM),
        out_shape=jax.ShapeDtypeStruct((ROWS_Y * CORES, 2 * tile, width), grads.dtype),
        compiler_params=pltpu.CompilerParams(vmem_limit_bytes=8 * MIB),
        cost_estimate=pl.CostEstimate(
            flops=0, bytes_accessed=2 * (1 + ROWS_Y) * rows * width, transcendentals=0
        ),
    )(grads)


def condition(place_ref, *refs):
    grads_ref, column_refs, (part_ref, parts_ref, weights) = refs[0], refs[1:-3], refs[-3:]
    columns = column_refs[0].shape[1]
    for core in range(CORES):

        @pl.when(place_ref[0] == core)
        def _():
            for i, ref in enumerate(column_refs):
                at = (i ^ core) * columns
                weights[:, at : at + columns] = ref[...]

    part = jnp.dot(grads_ref[...], weights[...], preferred_element_type=jnp.float32)
    part_ref[...] = part.astype(part_ref.dtype)
    for y in range(ROWS_Y):
        parts_ref[y] = part.astype(part_ref.dtype)


def conditioned_for(place, grads, columns):
    rows, width = grads.shape
    out = len(columns) * columns[0].shape[1]
    return pl.pallas_call(
        condition,
        in_specs=[pl.BlockSpec(memory_space=pltpu.SMEM)]
        + [pl.BlockSpec(memory_space=pltpu.VMEM)] * (1 + len(columns)),
        out_specs=[pl.BlockSpec(memory_space=pltpu.VMEM)] * 2,
        out_shape=[
            jax.ShapeDtypeStruct((rows, out), jnp.bfloat16),
            jax.ShapeDtypeStruct((ROWS_Y, rows, out), jnp.bfloat16),
        ],
        scratch_shapes=[pltpu.VMEM((width, out), jnp.bfloat16)],
        compiler_params=pltpu.CompilerParams(vmem_limit_bytes=12 * MIB),
        cost_estimate=pl.CostEstimate(
            flops=2 * rows * width * out,
            bytes_accessed=2 * (rows * width + width * out + (1 + ROWS_Y) * rows * out),
            transcendentals=0,
        ),
    )(place, grads, *columns)


def score(far, place_ref, *refs):
    part_refs, (mine_ref, theirs_ref, out_ref, queries) = refs[:ROWS_Y], refs[-4:]
    block_rows, columns = part_refs[0].shape[0], part_refs[0].shape[1] // ROWS_X
    rows = block_rows // ROWS_Y
    step, half = pl.program_id(0), pl.num_programs(0) // CORES

    @pl.when(step == 0)
    def _():
        x = lax.rem(place_ref[2] + far, ROWS_X)
        for i, ref in enumerate(part_refs):
            y = lax.rem(place_ref[1] + ROWS_Y - i, ROWS_Y) if far else i
            for k in range(ROWS_X):
                at = (lax.rem(x + k, ROWS_X) * ROWS_Y + y) * columns
                queries[:, pl.ds(pl.multiple_of(at, columns), columns)] = ref[
                    :, k * columns : (k + 1) * columns
                ]

    def times(store_ref):
        term = lax.dot_general(
            queries[...], store_ref[...], (((1,), (1,)), ((), ())),
            preferred_element_type=jnp.float32,
        ).astype(out_ref.dtype)
        tile = rows // NEAR
        for y in range(ROWS_Y):
            for near in range(NEAR):
                row = y * rows + near * tile
                out_ref[near, y * tile : (y + 1) * tile, :] = term[row : row + tile, :]

    @pl.when(step < half)
    def _():
        times(mine_ref)

    @pl.when(step >= half)
    def _():
        times(theirs_ref)


def scores_of(far, place, parts, mine, theirs, before=None):
    columns = parts[0].shape[-1]
    rows = parts[0].shape[-2]
    examples, width = mine.shape
    tile = 512
    half = examples // tile
    if far:
        part_specs = [pl.BlockSpec((rows, columns), lambda n, place_ref: (0, 0))] * ROWS_Y
    else:
        part_specs = [
            pl.BlockSpec((pl.squeezed, rows, columns), lambda n, place_ref, y=y: (y, 0, 0))
            for y in range(ROWS_Y)
        ]
    body = functools.partial(score, far)
    if before is not None:
        body = lambda place_ref, before_ref, *refs: score(far, place_ref, *refs)
    return pl.pallas_call(
        body,
        grid_spec=pltpu.PrefetchScalarGridSpec(
            num_scalar_prefetch=1,
            grid=(CORES * half,),
            in_specs=([] if before is None else [pl.BlockSpec(memory_space=pl.ANY)])
            + part_specs
            + [
                pl.BlockSpec((tile, width), lambda n, place_ref: (jnp.minimum(n, half - 1), 0)),
                pl.BlockSpec((tile, width), lambda n, place_ref: (jnp.maximum(n - half, 0), 0)),
            ],
            out_specs=pl.BlockSpec(
                (NEAR, rows // NEAR, tile),
                lambda n, place_ref: (
                    0,
                    lax.rem(place_ref[2] + far, ROWS_X),
                    lax.rem(n + place_ref[0] * half, CORES * half),
                ),
            ),
            scratch_shapes=[pltpu.VMEM((rows, width), jnp.bfloat16)],
        ),
        out_shape=jax.ShapeDtypeStruct((NEAR, ROWS_X * rows // NEAR, CORES * examples), jnp.bfloat16),
        input_output_aliases={} if before is None else {1: 0},
        compiler_params=pltpu.CompilerParams(vmem_limit_bytes=50 * MIB),
        cost_estimate=pl.CostEstimate(
            flops=2 * rows * width * CORES * examples,
            bytes_accessed=2 * (rows * width + CORES * (width + rows) * examples),
            transcendentals=0,
        ),
    )(place, *([] if before is None else [before]), *parts, mine, theirs)


def add(terms_ref, out_ref):
    examples = out_ref.shape[2]
    for c in range(CORES):
        columns = slice(c * examples, (c + 1) * examples)
        total = terms_ref[0, :, columns].astype(jnp.float32)
        for i in range(1, NEAR):
            total += terms_ref[i, :, columns].astype(jnp.float32)
        for p in range(out_ref.shape[0] // CORES):
            tile = out_ref.shape[1]
            out_ref[p * CORES + c] = total[p * tile : (p + 1) * tile].astype(out_ref.dtype)


def added(terms, tile, examples):
    steps = 4
    rows = terms.shape[1] // steps
    return pl.pallas_call(
        add,
        grid=(steps,),
        in_specs=[pl.BlockSpec((NEAR, rows, CORES * examples), lambda s: (0, s, 0))],
        out_specs=pl.BlockSpec((PAIRS * CORES // steps, tile, examples), lambda s: (s, 0, 0)),
        out_shape=jax.ShapeDtypeStruct((PAIRS * CORES, tile, examples), jnp.bfloat16),
        compiler_params=pltpu.CompilerParams(vmem_limit_bytes=8 * MIB),
        cost_estimate=pl.CostEstimate(
            flops=terms.size, bytes_accessed=3 * terms.size, transcendentals=0
        ),
    )(terms)


def shards(query_grads, precond, codes, scales):
    own_queries, width = query_grads.shape
    examples = codes.shape[0]
    ex_size, slots = lax.axis_size("ex"), lax.axis_size("dim")
    tile = own_queries * ex_size // slots // CORES
    chips = ROWS_X * ROWS_Y
    position = lax.axis_index("ex")
    place = jnp.stack([position % CORES, position // CORES % ROWS_Y, position // (CORES * ROWS_Y)])
    spots = [(x, y, c) for x in range(ROWS_X) for y in range(ROWS_Y) for c in range(CORES)]

    def shift(x_by, y_by, core_by):
        return [
            (e, ((x + x_by) % ROWS_X * ROWS_Y + (y + y_by) % ROWS_Y) * CORES + (c + core_by) % CORES)
            for e, (x, y, c) in enumerate(spots)
        ]

    chip_group = ROWS_Y * CORES
    beside = [list(range(x * chip_group, (x + 1) * chip_group)) for x in range(ROWS_X)]
    along_y = [
        [(x * ROWS_Y + y) * CORES + c for y in range(ROWS_Y)] for x in range(ROWS_X) for c in range(CORES)
    ]
    near = [[pair * NEAR + i for i in range(NEAR)] for pair in range(PAIRS)]
    far = [
        [(chip * CORES + c) * slots + pair * NEAR + i for pair in range(PAIRS) for c in range(CORES)]
        for chip in range(chips)
        for i in range(NEAR)
    ]

    own = precond[0]
    columns = [own] + [
        lax.ppermute(own, "ex", shift(x, 0, c)) for x, c in ((0, 1), (1, 0), (1, 1))
    ]

    grads = lax.all_to_all(
        spread(query_grads, tile),
        "ex", 0, 0, tiled=True, axis_index_groups=beside,
    ).reshape(ROWS_Y * CORES * 2 * tile, width)

    mine = dequantized(codes, scales)
    grads, mine, *columns = lax.optimization_barrier((grads, mine, *columns))
    part, copies = conditioned_for(place, grads, columns)
    theirs = lax.ppermute(mine, "ex", shift(0, 0, 1))

    parts = lax.all_to_all(copies, "ex", 0, 0, tiled=True, axis_index_groups=along_y)
    others = [lax.ppermute(part, "ex", shift(1, y, 0)) for y in range(ROWS_Y)]

    terms = scores_of(0, place, [parts] * ROWS_Y, mine, theirs)
    terms = scores_of(1, place, others, mine, theirs, terms)
    terms = lax.all_to_all(terms, "dim", 0, 0, tiled=True, axis_index_groups=near)
    sums = lax.all_to_all(
        added(terms, tile, examples), ("ex", "dim"), 0, 0, tiled=True, axis_index_groups=far
    )
    total = jnp.sum(sums.astype(jnp.float32).reshape(PAIRS, CORES * tile, examples), axis=0)
    return total * float(width * slots) ** (-0.5)


def solution(mesh):
    placed = (P("ex", "dim"), P("dim", None, "ex"), P("ex", "dim"), P("ex", "dim"))
    return jax.shard_map(
        shards, mesh=mesh, in_specs=placed, out_specs=P("dim", "ex"), check_vma=False
    )
```

time: 159 us -> 163 us (1.025)
  blocking collectives: 103 us -> 69.2 us
  starting transfers between devices: 25.8 us -> 43.4 us
  Pallas kernels: 10.9 us -> 24 us
  waiting for transfers between devices: 11.6 us -> 20.1 us
  other arithmetic: 2.76 us -> 0.82 us
    all_to_all x2 -> x1, blocking collectives: 55.7 us -> 25.8 us  [shards(): lax.all_to_all(terms, 'dim', 0, 0, tiled=True, axis_index_groups=near)]
    all_to_all x0 -> x2, starting transfers between devices: none -> 14.7 us  [the longest x1 10.3 us: shards(): lax.all_to_all(spread(query_grads, tile), 'ex', 0, 0, tiled=True, axis_in...]
    all_to_all x0 -> x2, waiting for transfers between devices: none -> 9.03 us  [the longest x1 9.02 us: shards(): lax.all_to_all(copies, 'ex', 0, 0, tiled=True, axis_index_groups=along_y)]
    pallas_call x1 -> x3, Pallas kernels: 6.66 us -> 14.9 us  [the longest x2 13.9 us: scores_of(): pl.pallas_call(body, grid_spec=pltpu.PrefetchScalarGridSpec(num_scalar_pr...]
    all_to_all x1, blocking collectives: 47.4 us -> 43.4 us  [shards(): lax.all_to_all(added(terms, tile, examples), ('ex', 'dim'), 0, 0, tiled=T...]
    pallas_call x1, Pallas kernels: 2.54 us -> 5.99 us  [dequantized(): pl.pallas_call(dequantize, grid=(rows // tile,), in_specs=[pl.BlockSpec((...]
    ppermute x8, starting transfers between devices: 25.8 us -> 28.7 us  [the longest x4 16.5 us: shards(): others = [lax.ppermute(part, 'ex', shift(1, y, 0)) for y in range(ROWS_Y)]]
    select_n x2 -> x0, other arithmetic: 1.99 us -> none  [the longest x1 1.01 us: shards(): jnp.where(core == 0, kept, swapped)]
  transfers between devices with their start and end apart: 8 -> 10, of which waited for: 4 -> 3; matrix products, arithmetic and copies ran while one was open for 1% -> 1% of each run, Pallas kernels for 2% -> 10%
where the time goes in v3:
time: 163 us; the launch traced here: 161 us
  blocking collectives  69.2 us (42%)
  starting transfers between devices  43.4 us (27%)
  Pallas kernels  24 us (15%)
  waiting for transfers between devices  20.1 us (12%)
  local copies, waits for them, and re-layouts  2.84 us (2%)
    all_to_all x1, blocking collectives, shards(): lax.all_to_all(added(terms, tile, examples), ('ex', 'dim'), 0, 0, tiled=T...  43.4 us
    all_to_all x1, blocking collectives, shards(): lax.all_to_all(terms, 'dim', 0, 0, tiled=True, axis_index_groups=near)  25.8 us
    ppermute x4, starting transfers between devices, shards(): others = [lax.ppermute(part, 'ex', shift(1, y, 0)) for y in range(ROWS_Y)]  16.5 us
    pallas_call x2, Pallas kernels, scores_of(): pl.pallas_call(body, grid_spec=pltpu.PrefetchScalarGridSpec(num_scalar_pr...  13.9 us
    ppermute x3, waiting for transfers between devices, shards(): lax.ppermute(own, 'ex', shift(x, 0, c))  11.1 us
    all_to_all x1, starting transfers between devices, shards(): lax.all_to_all(spread(query_grads, tile), 'ex', 0, 0, tiled=True, axis_in...  10.3 us
    ppermute x3, starting transfers between devices, shards(): lax.ppermute(own, 'ex', shift(x, 0, c))  9.36 us
    all_to_all x1, waiting for transfers between devices, shards(): lax.all_to_all(copies, 'ex', 0, 0, tiled=True, axis_index_groups=along_y)  9.02 us
  transfers between devices with their start and end apart: 10, of which 3 were waited for; matrix products, arithmetic and copies ran while one was open for 1% of the time, Pallas kernels for 10%

profile of v3, /device:TPU:1, one launch (start us, length us, event | category | flops | bytes accessed | tf_op | source)
XLA Modules:
  0.0 160.6 jit_solution(3674150388858248654)
XLA Ops:
  0.0 0.0 copy-start.1
  0.0 0.9 copy-done.1
  1.0 1.0 shard_map.46
  2.0 10.3 %all-to-all-start = ((bf16[8,32,2048]{2,1,0:T(8,128)(2,1)}), bf16[8,32,2048]{2,1,0:T(8,128)(2,1)S(1)}, u32[]{:S(2)}, u32[]{:S(2)}) async-start(bf16[8,32,2048]{2,1,0:T(8,128)(2,1)} %shard_map.46), calls=%async_computation | async-start | bytes 2097152 | tf_op jit(solution)/shard_map/all_to_all | solution.py:252
  12.3 1.9 %collective-permute-start.2 = (bf16[2048,128]{1,0:T(8,128)(2,1)}, bf16[2048,128]{1,0:T(8,128)(2,1)S(1)}, u32[]{:S(2)}, u32[]{:S(2)}) collective-permute-start(bf16[2048,128]{1,0:T(8,128)(2,1)} %bitcast.10), channel_id=1, source_target_pairs={{0,288},{32,256},{64,352},{96,320},{128,416},{160,384},{192,480},{... | collective-permute-start | bytes 1572872 | tf_op jit(solution)/shard_map/ppermute | solution.py:249
  14.2 4.9 %collective-permute-start.1 = (bf16[2048,128]{1,0:T(8,128)(2,1)}, bf16[2048,128]{1,0:T(8,128)(2,1)S(1)}, u32[]{:S(2)}, u32[]{:S(2)}) collective-permute-start(bf16[2048,128]{1,0:T(8,128)(2,1)} %bitcast.11), channel_id=1, source_target_pairs={{0,256},{32,288},{64,320},{96,352},{128,384},{160,416},{192,448},{... | collective-permute-start | bytes 1572872 | tf_op jit(solution)/shard_map/ppermute | solution.py:249
  19.1 2.6 %collective-permute-start = (bf16[2048,128]{1,0:T(8,128)(2,1)}, bf16[2048,128]{1,0:T(8,128)(2,1)S(1)}, u32[]{:S(2)}, u32[]{:S(2)}) collective-permute-start(bf16[2048,128]{1,0:T(8,128)(2,1)} %bitcast.12), channel_id=1, source_target_pairs={{0,32},{32,0},{64,96},{96,64},{128,160},{160,128},{192,224},{224,1... | collective-permute-start | bytes 1572872 | tf_op jit(solution)/shard_map/ppermute | solution.py:249
  21.7 1.9 %copy.6.scales_ref = f32[1024,16]{1,0:T(8,128)} copy(f32[1024,16]{0,1:T(8,128)} %param.7) | data formatting | bytes 131072 | tf_op args[3]
  23.6 0.0 copy-start
  23.6 6.0 %shard_map.47.refs_4_ = bf16[1024,2048]{1,0:T(8,128)(2,1)} custom-call(bf16[1024,2048]{1,0:T(8,128)(2,1)} %codes_ref.1, f32[1024,16]{1,0:T(8,128)} %copy.6.scales_ref), custom_call_target="tpu_custom_call" | custom-call | flops 2097152 | bytes 8388608 | tf_op jit(solution)/shard_map/pallas_call | solution.py:27
  29.6 0.5 collective-permute-done.2.refs_4_
  30.1 10.6 %collective-permute-done.1.refs_3_ = bf16[2048,128]{1,0:T(8,128)(2,1)S(1)} collective-permute-done((bf16[2048,128]{1,0:T(8,128)(2,1)}, bf16[2048,128]{1,0:T(8,128)(2,1)S(1)}, u32[]{:S(2)}, u32[]{:S(2)}) %collective-permute-start.1) | collective-permute-done | bytes 524320 | tf_op jit(solution)/shard_map/ppermute | solution.py:249
  40.7 0.0 collective-permute-done.refs_2_
  40.7 0.0 all-to-all-done
  40.7 2.8 %collective-permute-start.3 = (bf16[1024,2048]{1,0:T(8,128)(2,1)}, bf16[1024,2048]{1,0:T(8,128)(2,1)}, u32[]{:S(2)}, u32[]{:S(2)}) collective-permute-start(bf16[1024,2048]{1,0:T(8,128)(2,1)} %shard_map.47.refs_4_), channel_id=1, source_target_pairs={{0,32},{32,0},{64,96},{96,64},{128,160},{160,128},{192,224},{224,1... | collective-permute-start | bytes 12582920 | tf_op jit(solution)/shard_map/ppermute | solution.py:260
  43.5 0.1 pad_add_fusion.place_ref
  43.6 0.0 copy-done
  43.6 2.7 %shard_map.48 = (bf16[256,512]{1,0:T(8,128)(2,1)S(1)}, bf16[4,256,512]{2,1,0:T(8,128)(2,1)}) custom-call(s32[3]{0:T(128)S(1)} %pad_add_fusion.place_ref, bf16[256,2048]{1,0:T(8,128)(2,1)S(1)} %bitcast.9, bf16[2048,128]{1,0:T(8,128)(2,1)S(1)} %bitcast.13, bf16[2048,128]{1,0:T(8,128)(2,1)S(1)} %collective-permute-done.refs_2_, ...), custom_call_target="tpu_custom_call" | custom-call | flops 536870912 | bytes 4456448 | tf_op jit(solution)/shard_map/pallas_call | solution.py:87
  46.3 4.4 %all-to-all-start.1 = ((bf16[4,256,512]{2,1,0:T(8,128)(2,1)}), bf16[4,256,512]{2,1,0:T(8,128)(2,1)S(1)}, u32[]{:S(2)}, u32[]{:S(2)}) async-start(bf16[4,256,512]{2,1,0:T(8,128)(2,1)} %get-tuple-element.18), calls=%async_computation.1 | async-start | bytes 2097152 | tf_op jit(solution)/shard_map/all_to_all | solution.py:262
  50.7 4.1 %collective-permute-start.7 = (bf16[256,512]{1,0:T(8,128)(2,1)S(1)}, bf16[256,512]{1,0:T(8,128)(2,1)S(1)}, u32[]{:S(2)}, u32[]{:S(2)}) collective-permute-start(bf16[256,512]{1,0:T(8,128)(2,1)S(1)} %get-tuple-element.20), channel_id=1, source_target_pairs={{0,448},{32,480},{64,256},{96,288},{128,320},{160,352},{192,384},{... | collective-permute-start | bytes 786440 | tf_op jit(solution)/shard_map/ppermute | solution.py:263
  54.7 5.4 %collective-permute-start.6 = (bf16[256,512]{1,0:T(8,128)(2,1)S(1)}, bf16[256,512]{1,0:T(8,128)(2,1)S(1)}, u32[]{:S(2)}, u32[]{:S(2)}) collective-permute-start(bf16[256,512]{1,0:T(8,128)(2,1)S(1)} %get-tuple-element.20), channel_id=1, source_target_pairs={{0,384},{32,416},{64,448},{96,480},{128,256},{160,288},{192,320},{... | collective-permute-start | bytes 786440 | tf_op jit(solution)/shard_map/ppermute | solution.py:263
  60.1 2.0 %collective-permute-start.5 = (bf16[256,512]{1,0:T(8,128)(2,1)S(1)}, bf16[256,512]{1,0:T(8,128)(2,1)S(1)}, u32[]{:S(2)}, u32[]{:S(2)}) collective-permute-start(bf16[256,512]{1,0:T(8,128)(2,1)S(1)} %get-tuple-element.20), channel_id=1, source_target_pairs={{0,320},{32,352},{64,384},{96,416},{128,448},{160,480},{192,256},{... | collective-permute-start | bytes 786440 | tf_op jit(solution)/shard_map/ppermute | solution.py:263
  62.1 5.1 %collective-permute-start.4 = (bf16[256,512]{1,0:T(8,128)(2,1)S(1)}, bf16[256,512]{1,0:T(8,128)(2,1)S(1)}, u32[]{:S(2)}, u32[]{:S(2)}) collective-permute-start(bf16[256,512]{1,0:T(8,128)(2,1)S(1)} %get-tuple-element.20), channel_id=1, source_target_pairs={{0,256},{32,288},{64,320},{96,352},{128,384},{160,416},{192,448},{... | collective-permute-start | bytes 786440 | tf_op jit(solution)/shard_map/ppermute | solution.py:263
  67.2 9.0 %all-to-all-done.1.refs_0_.refs_1_.refs_2_.refs_3_ = bf16[4,256,512]{2,1,0:T(8,128)(2,1)S(1)} async-done(((bf16[4,256,512]{2,1,0:T(8,128)(2,1)}), bf16[4,256,512]{2,1,0:T(8,128)(2,1)S(1)}, u32[]{:S(2)}, u32[]{:S(2)}) %all-to-all-start.1) | async-done | bytes 1048608 | tf_op jit(solution)/shard_map/all_to_all | solution.py:262
  76.2 0.0 collective-permute-done.3.refs_5_
  76.3 6.9 %shard_map.49.before_ref = bf16[4,128,2048]{2,1,0:T(8,128)(2,1)S(1)} custom-call(s32[3]{0:T(128)S(1)} %pad_add_fusion.place_ref, bf16[4,256,512]{2,1,0:T(8,128)(2,1)S(1)} %all-to-all-done.1.refs_0_.refs_1_.refs_2_.refs_3_, bf16[4,256,512]{2,1,0:T(8,128)(2,1)S(1)} %all-to-all-done.1.refs_0_.refs_1_.refs_2_.refs_3_, ...), custom_call_target="tpu_custom_call" | custom-call | flops 2147483648 | bytes 10485760 | tf_op jit(solution)/shard_map/pallas_call | solution.py:159
  83.2 0.0 collective-permute-done.7.refs_3_
  83.2 0.0 collective-permute-done.6.refs_2_
  83.2 0.0 collective-permute-done.5.refs_1_
  83.2 0.0 collective-permute-done.4.refs_0_
  83.2 6.9 %shard_map.50 = bf16[4,128,2048]{2,1,0:T(8,128)(2,1)S(1)} custom-call(s32[3]{0:T(128)S(1)} %pad_add_fusion.place_ref, bf16[4,128,2048]{2,1,0:T(8,128)(2,1)S(1)} %shard_map.49.before_ref, bf16[256,512]{1,0:T(8,128)(2,1)S(1)} %collective-permute-done.4.refs_0_, bf16[256,512]{1,0:T(8,128)(2,1)S(1)} %collective-permute-done.5.refs_1_, ...), custom_call_target="tpu_custom_call", output_to_operand_aliasing={{}: (1, {})} | custom-call | flops 2147483648 | bytes 10485760 | tf_op jit(solution)/shard_map/pallas_call | solution.py:159
  90.2 25.8 %all_to_all.20.terms_ref = bf16[4,128,2048]{2,1,0:T(8,128)(2,1)S(1)} all-to-all(bf16[4,128,2048]{2,1,0:T(8,128)(2,1)S(1)} %shard_map.50), channel_id=1, replica_groups={{0,1,2,3},{4,5,6,7},{8,9,10,11},{12,13,14,15},{16,17,18,19},{20,21,22,2..., dimensions={0} | all-to-all | bytes 4194304 | tf_op jit(solution)/shard_map/all_to_all | solution.py:267
  116.0 0.5 shard_map.51
  116.5 43.4 %all_to_all.21 = bf16[16,16,1024]{2,1,0:T(8,128)(2,1)S(1)} all-to-all(bf16[16,16,1024]{2,1,0:T(8,128)(2,1)S(1)} %shard_map.51), channel_id=1, replica_groups={{0,32,4,36,8,40,12,44,16,48,20,52,24,56,28,60},{1,33,5,37,9,41,13,45,17..., dimensions={0} | all-to-all | bytes 1048576 | tf_op jit(solution)/shard_map/all_to_all | solution.py:268
  159.9 0.1 convert_reduce_fusion
  160.0 0.7 broadcast_multiply_fusion
Async XLA Ops:
  0.0 0.9 copy-start.1
  2.0 38.7 %all-to-all-start = ((bf16[8,32,2048]{2,1,0:T(8,128)(2,1)}), bf16[8,32,2048]{2,1,0:T(8,128)(2,1)S(1)}, u32[]{:S(2)}, u32[]{:S(2)}) async-start(bf16[8,32,2048]{2,1,0:T(8,128)(2,1)} %shard_map.46), calls=%async_computation | async-start | bytes 2097152 | tf_op jit(solution)/shard_map/all_to_all | solution.py:252
  12.3 17.8 %collective-permute-start.2 = (bf16[2048,128]{1,0:T(8,128)(2,1)}, bf16[2048,128]{1,0:T(8,128)(2,1)S(1)}, u32[]{:S(2)}, u32[]{:S(2)}) collective-permute-start(bf16[2048,128]{1,0:T(8,128)(2,1)} %bitcast.10), channel_id=1, source_target_pairs={{0,288},{32,256},{64,352},{96,320},{128,416},{160,384},{192,480},{... | collective-permute-start | bytes 1572872 | tf_op jit(solution)/shard_map/ppermute | solution.py:249
  14.2 26.4 %collective-permute-start.1 = (bf16[2048,128]{1,0:T(8,128)(2,1)}, bf16[2048,128]{1,0:T(8,128)(2,1)S(1)}, u32[]{:S(2)}, u32[]{:S(2)}) collective-permute-start(bf16[2048,128]{1,0:T(8,128)(2,1)} %bitcast.11), channel_id=1, source_target_pairs={{0,256},{32,288},{64,320},{96,352},{128,384},{160,416},{192,448},{... | collective-permute-start | bytes 1572872 | tf_op jit(solution)/shard_map/ppermute | solution.py:249
  19.1 21.5 %collective-permute-start = (bf16[2048,128]{1,0:T(8,128)(2,1)}, bf16[2048,128]{1,0:T(8,128)(2,1)S(1)}, u32[]{:S(2)}, u32[]{:S(2)}) collective-permute-start(bf16[2048,128]{1,0:T(8,128)(2,1)} %bitcast.12), channel_id=1, source_target_pairs={{0,32},{32,0},{64,96},{96,64},{128,160},{160,128},{192,224},{224,1... | collective-permute-start | bytes 1572872 | tf_op jit(solution)/shard_map/ppermute | solution.py:249
  23.6 20.0 %copy-start = (bf16[1,2048,128]{2,1,0:T(8,128)(2,1)S(1)}, bf16[1,2048,128]{2,1,0:T(8,128)(2,1)}, u32[]{:S(2)}) copy-start(bf16[1,2048,128]{2,1,0:T(8,128)(2,1)} %param.5) | copy-start | bytes 1572868
  40.7 35.6 %collective-permute-start.3 = (bf16[1024,2048]{1,0:T(8,128)(2,1)}, bf16[1024,2048]{1,0:T(8,128)(2,1)}, u32[]{:S(2)}, u32[]{:S(2)}) collective-permute-start(bf16[1024,2048]{1,0:T(8,128)(2,1)} %shard_map.47.refs_4_), channel_id=1, source_target_pairs={{0,32},{32,0},{64,96},{96,64},{128,160},{160,128},{192,224},{224,1... | collective-permute-start | bytes 12582920 | tf_op jit(solution)/shard_map/ppermute | solution.py:260
  46.3 30.0 %all-to-all-start.1 = ((bf16[4,256,512]{2,1,0:T(8,128)(2,1)}), bf16[4,256,512]{2,1,0:T(8,128)(2,1)S(1)}, u32[]{:S(2)}, u32[]{:S(2)}) async-start(bf16[4,256,512]{2,1,0:T(8,128)(2,1)} %get-tuple-element.18), calls=%async_computation.1 | async-start | bytes 2097152 | tf_op jit(solution)/shard_map/all_to_all | solution.py:262
  50.7 32.5 %collective-permute-start.7 = (bf16[256,512]{1,0:T(8,128)(2,1)S(1)}, bf16[256,512]{1,0:T(8,128)(2,1)S(1)}, u32[]{:S(2)}, u32[]{:S(2)}) collective-permute-start(bf16[256,512]{1,0:T(8,128)(2,1)S(1)} %get-tuple-element.20), channel_id=1, source_target_pairs={{0,448},{32,480},{64,256},{96,288},{128,320},{160,352},{192,384},{... | collective-permute-start | bytes 786440 | tf_op jit(solution)/shard_map/ppermute | solution.py:263
  54.7 28.5 %collective-permute-start.6 = (bf16[256,512]{1,0:T(8,128)(2,1)S(1)}, bf16[256,512]{1,0:T(8,128)(2,1)S(1)}, u32[]{:S(2)}, u32[]{:S(2)}) collective-permute-start(bf16[256,512]{1,0:T(8,128)(2,1)S(1)} %get-tuple-element.20), channel_id=1, source_target_pairs={{0,384},{32,416},{64,448},{96,480},{128,256},{160,288},{192,320},{... | collective-permute-start | bytes 786440 | tf_op jit(solution)/shard_map/ppermute | solution.py:263
  60.1 23.1 %collective-permute-start.5 = (bf16[256,512]{1,0:T(8,128)(2,1)S(1)}, bf16[256,512]{1,0:T(8,128)(2,1)S(1)}, u32[]{:S(2)}, u32[]{:S(2)}) collective-permute-start(bf16[256,512]{1,0:T(8,128)(2,1)S(1)} %get-tuple-element.20), channel_id=1, source_target_pairs={{0,320},{32,352},{64,384},{96,416},{128,448},{160,480},{192,256},{... | collective-permute-start | bytes 786440 | tf_op jit(solution)/shard_map/ppermute | solution.py:263
  62.1 21.1 %collective-permute-start.4 = (bf16[256,512]{1,0:T(8,128)(2,1)S(1)}, bf16[256,512]{1,0:T(8,128)(2,1)S(1)}, u32[]{:S(2)}, u32[]{:S(2)}) collective-permute-start(bf16[256,512]{1,0:T(8,128)(2,1)S(1)} %get-tuple-element.20), channel_id=1, source_target_pairs={{0,256},{32,288},{64,320},{96,352},{128,384},{160,416},{192,448},{... | collective-permute-start | bytes 786440 | tf_op jit(solution)/shard_map/ppermute | solution.py:263

commit v4 on v3

v4 whole, which is shorter than its diff:
```python
import jax
import jax.numpy as jnp
from jax import lax
from jax.experimental import pallas as pl
from jax.experimental.pallas import tpu as pltpu
from jax.sharding import PartitionSpec as P

CORES, ROWS_Y, ROWS_X = 2, 4, 2
PAIRS, SIDES = 8, 2
NEAR = 2 * SIDES
MIB = 1 << 20


def dequantize(codes_ref, scales_ref, out_ref):
    block = codes_ref.shape[1] // scales_ref.shape[1]
    for b in range(scales_ref.shape[1]):
        columns = slice(b * block, (b + 1) * block)
        entries = codes_ref[:, columns].astype(jnp.float32) * scales_ref[:, b : b + 1]
        out_ref[:, columns] = entries.astype(out_ref.dtype)


def dequantized(codes, scales):
    rows, width = codes.shape
    tile = 256
    return pl.pallas_call(
        dequantize,
        grid=(rows // tile,),
        in_specs=[
            pl.BlockSpec((tile, width), lambda r: (r, 0)),
            pl.BlockSpec((tile, scales.shape[1]), lambda r: (r, 0)),
        ],
        out_specs=pl.BlockSpec((tile, width), lambda r: (r, 0)),
        out_shape=jax.ShapeDtypeStruct(codes.shape, jnp.bfloat16),
        compiler_params=pltpu.CompilerParams(vmem_limit_bytes=56 * MIB),
        cost_estimate=pl.CostEstimate(
            flops=rows * width, bytes_accessed=4 * rows * width, transcendentals=0
        ),
    )(codes, scales)


def copy_halves(grads_ref, out_ref):
    tile = out_ref.shape[1] // 2
    for b in range(2):
        for core in range(CORES):
            row = (b * CORES + core) * tile
            entries = grads_ref[row : row + tile, :]
            for y in range(ROWS_Y):
                out_ref[y * CORES + core, b * tile : (b + 1) * tile, :] = entries


def spread(grads, tile):
    rows, width = grads.shape
    return pl.pallas_call(
        copy_halves,
        in_specs=[pl.BlockSpec(memory_space=pltpu.VMEM)],
        out_specs=pl.BlockSpec(memory_space=pltpu.VMEM),
        out_shape=jax.ShapeDtypeStruct((ROWS_Y * CORES, 2 * tile, width), grads.dtype),
        compiler_params=pltpu.CompilerParams(vmem_limit_bytes=8 * MIB),
        cost_estimate=pl.CostEstimate(
            flops=0, bytes_accessed=2 * (1 + ROWS_Y) * rows * width, transcendentals=0
        ),
    )(grads)


def condition(place_ref, *refs):
    grads_ref, column_refs, (parts_ref, weights) = refs[0], refs[1:-2], refs[-2:]
    columns = column_refs[0].shape[1]
    for core in range(CORES):

        @pl.when(place_ref[0] == core)
        def _():
            for i, ref in enumerate(column_refs):
                at = (i ^ core) * columns
                weights[:, at : at + columns] = ref[...]

    part = jnp.dot(grads_ref[...], weights[...], preferred_element_type=jnp.float32)
    for chip in range(parts_ref.shape[0]):
        parts_ref[chip] = part.astype(parts_ref.dtype)


def conditioned_for(place, chips, grads, columns):
    rows, width = grads.shape
    out = len(columns) * columns[0].shape[1]
    return pl.pallas_call(
        condition,
        in_specs=[pl.BlockSpec(memory_space=pltpu.SMEM)]
        + [pl.BlockSpec(memory_space=pltpu.VMEM)] * (1 + len(columns)),
        out_specs=pl.BlockSpec(memory_space=pltpu.VMEM),
        out_shape=jax.ShapeDtypeStruct((chips, rows, out), jnp.bfloat16),
        scratch_shapes=[pltpu.VMEM((width, out), jnp.bfloat16)],
        compiler_params=pltpu.CompilerParams(vmem_limit_bytes=16 * MIB),
        cost_estimate=pl.CostEstimate(
            flops=2 * rows * width * out,
            bytes_accessed=2 * (rows * width + width * out + chips * rows * out),
            transcendentals=0,
        ),
    )(place, grads, *columns)


def score(place_ref, parts_ref, store_ref, *refs):
    out_refs, queries = refs[:NEAR], refs[NEAR]
    block_rows, columns = parts_ref.shape[1], parts_ref.shape[2] // ROWS_X
    rows = block_rows // ROWS_Y
    tile = rows // NEAR

    @pl.when(pl.program_id(0) == 0)
    def _():
        for x in range(ROWS_X):
            for pair in range(ROWS_Y):
                for near in range(NEAR):
                    to = (near ^ place_ref[1]) * (PAIRS * tile) + (x * ROWS_Y + pair) * tile
                    to = pl.multiple_of(to, tile)
                    row = pair * rows + near * tile
                    for y in range(ROWS_Y):
                        for k in range(ROWS_X):
                            at = ((x ^ k) * ROWS_Y + y) * columns
                            queries[pl.ds(to, tile), at : at + columns] = parts_ref[
                                x * ROWS_Y + y, row : row + tile, k * columns : (k + 1) * columns
                            ]

    term = lax.dot_general(
        queries[...], store_ref[...], (((1,), (1,)), ((), ())),
        preferred_element_type=jnp.float32,
    )
    for k, ref in enumerate(out_refs):
        ref[...] = term[k * PAIRS * tile : (k + 1) * PAIRS * tile].astype(ref.dtype)


def scores_of(place, parts, store):
    chips, block_rows, columns = parts.shape
    rows = ROWS_X * block_rows
    examples, width = store.shape
    tile = 256
    return pl.pallas_call(
        score,
        grid_spec=pltpu.PrefetchScalarGridSpec(
            num_scalar_prefetch=1,
            grid=(examples // tile,),
            in_specs=[
                pl.BlockSpec((chips, block_rows, columns), lambda n, place_ref: (0, 0, 0)),
                pl.BlockSpec((tile, width), lambda n, place_ref: (n, 0)),
            ],
            out_specs=[pl.BlockSpec((rows // NEAR, tile), lambda n, place_ref: (0, n))] * NEAR,
            scratch_shapes=[pltpu.VMEM((rows, width), jnp.bfloat16)],
        ),
        out_shape=[jax.ShapeDtypeStruct((rows // NEAR, examples), jnp.bfloat16)] * NEAR,
        compiler_params=pltpu.CompilerParams(vmem_limit_bytes=32 * MIB),
        cost_estimate=pl.CostEstimate(
            flops=2 * rows * width * examples,
            bytes_accessed=2 * (rows * width + (width + rows) * examples),
            transcendentals=0,
        ),
    )(place, parts, store)


def add(place_ref, *refs):
    out_ref = refs[-1]
    tile = out_ref.shape[1]
    for i in range(CORES):
        total = refs[i * NEAR][...].astype(jnp.float32)
        for ref in refs[i * NEAR + 1 : (i + 1) * NEAR]:
            total += ref[...].astype(jnp.float32)
        for p in range(out_ref.shape[0] // CORES):
            at = p * CORES + (place_ref[0] ^ i)
            out_ref[at] = total[p * tile : (p + 1) * tile].astype(out_ref.dtype)


def added(place, tile, terms):
    steps = 4
    rows, examples = terms[0].shape
    return pl.pallas_call(
        add,
        grid_spec=pltpu.PrefetchScalarGridSpec(
            num_scalar_prefetch=1,
            grid=(steps,),
            in_specs=[pl.BlockSpec((rows // steps, examples), lambda s, place_ref: (s, 0))] * len(terms),
            out_specs=pl.BlockSpec(
                (PAIRS * CORES // steps, tile, examples), lambda s, place_ref: (s, 0, 0)
            ),
        ),
        out_shape=jax.ShapeDtypeStruct((PAIRS * CORES, tile, examples), jnp.bfloat16),
        compiler_params=pltpu.CompilerParams(vmem_limit_bytes=16 * MIB),
        cost_estimate=pl.CostEstimate(
            flops=len(terms) * rows * examples,
            bytes_accessed=3 * len(terms) * rows * examples,
            transcendentals=0,
        ),
    )(place, *terms)


def shards(query_grads, precond, codes, scales):
    own_queries, width = query_grads.shape
    examples = codes.shape[0]
    ex_size, slots = lax.axis_size("ex"), lax.axis_size("dim")
    tile = own_queries * ex_size // slots // CORES
    chips = ROWS_X * ROWS_Y
    position = lax.axis_index("ex")
    near_here = lax.axis_index("dim") % NEAR
    place = jnp.stack([position % CORES, near_here])
    spots = [(x, y, c) for x in range(ROWS_X) for y in range(ROWS_Y) for c in range(CORES)]

    def shift(x_by, y_by, core_by):
        return [
            (e, ((x + x_by) % ROWS_X * ROWS_Y + (y + y_by) % ROWS_Y) * CORES + (c + core_by) % CORES)
            for e, (x, y, c) in enumerate(spots)
        ]

    chip_group = ROWS_Y * CORES
    beside = [list(range(x * chip_group, (x + 1) * chip_group)) for x in range(ROWS_X)]
    same_core = [[chip * CORES + c for chip in range(chips)] for c in range(CORES)]
    far = [
        [(chip * CORES + c) * slots + pair * NEAR + i for pair in range(PAIRS) for c in range(CORES)]
        for chip in range(chips)
        for i in range(NEAR)
    ]

    own = precond[0]
    own_other = lax.ppermute(own, "ex", shift(0, 0, 1))
    across = lax.ppermute(own, "ex", shift(1, 0, 0))
    across_other = lax.ppermute(across, "ex", shift(0, 0, 1))

    grads = lax.all_to_all(
        spread(query_grads, tile), "ex", 0, 0, tiled=True, axis_index_groups=beside
    ).reshape(ROWS_Y * CORES * 2 * tile, width)

    mine = dequantized(codes, scales)
    grads, mine, own_other, across, across_other = lax.optimization_barrier(
        (grads, mine, own_other, across, across_other)
    )
    copies = conditioned_for(place, chips, grads, [own, own_other, across, across_other])
    mine, copies = lax.optimization_barrier((mine, copies))
    theirs = lax.ppermute(mine, "ex", shift(0, 0, 1))
    parts = lax.all_to_all(copies, "ex", 0, 0, tiled=True, axis_index_groups=same_core)

    terms = []
    for store in (mine, theirs):
        here, *away = scores_of(place, parts, store)
        terms += [here] + [
            lax.ppermute(term, "dim", [(d, d ^ k) for d in range(slots)])
            for k, term in enumerate(away, 1)
        ]
    sums = lax.all_to_all(
        added(place, tile, terms), ("ex", "dim"), 0, 0, tiled=True, axis_index_groups=far
    )
    total = jnp.sum(sums.astype(jnp.float32).reshape(PAIRS, CORES * tile, examples), axis=0)
    return total * float(width * slots) ** (-0.5)


def solution(mesh):
    placed = (P("ex", "dim"), P("dim", None, "ex"), P("ex", "dim"), P("ex", "dim"))
    return jax.shard_map(
        shards, mesh=mesh, in_specs=placed, out_specs=P("dim", "ex"), check_vma=False
    )
```

time: 163 us -> 149 us (0.914)
  waiting for transfers between devices: 20.1 us -> 8.07 us
  blocking collectives: 69.2 us -> 79.4 us
  Pallas kernels: 24 us -> 17.3 us
  starting transfers between devices: 43.4 us -> 39 us
    all_to_all x2, blocking collectives: 69.2 us -> 79.4 us  [the longest x1 47.6 us: shards(): lax.all_to_all(added(place, tile, terms), ('ex', 'dim'), 0, 0, tiled=True...]
    all_to_all x1 -> x0, waiting for transfers between devices: 9.02 us -> none  [shards(): lax.all_to_all(copies, 'ex', 0, 0, tiled=True, axis_index_groups=along_y)]
    pallas_call x3, Pallas kernels: 14.3 us -> 8.58 us  [the longest x2 7.69 us: scores_of(): pl.pallas_call(score, grid_spec=pltpu.PrefetchScalarGridSpec(num_scalar_p...]
    all_to_all x1 -> x0, starting transfers between devices: 4.39 us -> none  [shards(): lax.all_to_all(copies, 'ex', 0, 0, tiled=True, axis_index_groups=along_y)]
    ppermute x7 -> x9, starting transfers between devices: 25.9 us -> 29.6 us  [the longest x6 16.9 us: shards(): lax.ppermute(term, 'dim', [(d, d ^ k) for d in range(slots)])]
    all_to_all x1, starting transfers between devices: 10.3 us -> 6.78 us  [shards(): lax.all_to_all(spread(query_grads, tile), 'ex', 0, 0, tiled=True, axis_in...]
    ppermute x7 -> x9, waiting for transfers between devices: 11.1 us -> 8.07 us  [the longest x6 8.06 us: shards(): lax.ppermute(term, 'dim', [(d, d ^ k) for d in range(slots)])]
    unnamed x5 -> x7, local copies, waits for them, and re-layouts: 2.84 us -> 3.3 us
  transfers between devices with their start and end apart: 10 -> 11, of which waited for: 3 -> 2; matrix products, arithmetic and copies ran while one was open for 1% -> 1% of each run, Pallas kernels for 10% -> 10%
where the time goes in v4:
time: 149 us; the launch traced here: 148 us
  blocking collectives  79.4 us (53%)
  starting transfers between devices  39 us (26%)
  Pallas kernels  17.3 us (12%)
  waiting for transfers between devices  8.07 us (5%)
  local copies, waits for them, and re-layouts  3.3 us (2%)
    all_to_all x1, blocking collectives, shards(): lax.all_to_all(added(place, tile, terms), ('ex', 'dim'), 0, 0, tiled=True...  47.6 us
    all_to_all x1, blocking collectives, shards(): lax.all_to_all(copies, 'ex', 0, 0, tiled=True, axis_index_groups=same_core)  31.8 us
    ppermute x6, starting transfers between devices, shards(): lax.ppermute(term, 'dim', [(d, d ^ k) for d in range(slots)])  16.9 us
    ppermute x6, waiting for transfers between devices, shards(): lax.ppermute(term, 'dim', [(d, d ^ k) for d in range(slots)])  8.06 us
    pallas_call x2, Pallas kernels, scores_of(): pl.pallas_call(score, grid_spec=pltpu.PrefetchScalarGridSpec(num_scalar_p...  7.69 us
    all_to_all x1, starting transfers between devices, shards(): lax.all_to_all(spread(query_grads, tile), 'ex', 0, 0, tiled=True, axis_in...  6.78 us
    pallas_call x1, Pallas kernels, dequantized(): pl.pallas_call(dequantize, grid=(rows // tile,), in_specs=[pl.BlockSpec((...  5.98 us
    ppermute x1, starting transfers between devices, shards(): across = lax.ppermute(own, 'ex', shift(1, 0, 0))  5.47 us
  transfers between devices with their start and end apart: 11, of which 2 were waited for; matrix products, arithmetic and copies ran while one was open for 1% of the time, Pallas kernels for 10%

profile of v4, /device:TPU:1, one launch (start us, length us, event | category | flops | bytes accessed | tf_op | source)
XLA Modules:
  0.0 148.1 jit_solution(8940772632767664935)
XLA Ops:
  0.0 5.5 %collective-permute-start.1 = (bf16[2048,128]{1,0:T(8,128)(2,1)}, bf16[2048,128]{1,0:T(8,128)(2,1)S(1)}, u32[]{:S(2)}, u32[]{:S(2)}) collective-permute-start(bf16[2048,128]{1,0:T(8,128)(2,1)} %bitcast.9), channel_id=1, source_target_pairs={{0,256},{32,288},{64,320},{96,352},{128,384},{160,416},{192,448},{... | collective-permute-start | bytes 1572872 | tf_op jit(solution)/shard_map/ppermute | solution.py:219
  5.5 0.0 copy-start.2
  5.5 0.9 copy-done.2
  6.4 1.0 shard_map.46
  7.5 6.8 %all-to-all-start = ((bf16[8,32,2048]{2,1,0:T(8,128)(2,1)}), bf16[8,32,2048]{2,1,0:T(8,128)(2,1)S(1)}, u32[]{:S(2)}, u32[]{:S(2)}) async-start(bf16[8,32,2048]{2,1,0:T(8,128)(2,1)} %shard_map.46), calls=%async_computation | async-start | bytes 2097152 | tf_op jit(solution)/shard_map/all_to_all | solution.py:222
  14.2 2.0 %collective-permute-start = (bf16[2048,128]{1,0:T(8,128)(2,1)}, bf16[2048,128]{1,0:T(8,128)(2,1)S(1)}, u32[]{:S(2)}, u32[]{:S(2)}) collective-permute-start(bf16[2048,128]{1,0:T(8,128)(2,1)} %bitcast.10), channel_id=1, source_target_pairs={{0,32},{32,0},{64,96},{96,64},{128,160},{160,128},{192,224},{224,1... | collective-permute-start | bytes 1572872 | tf_op jit(solution)/shard_map/ppermute | solution.py:218
  16.3 0.0 collective-permute-done.1.refs_3_
  16.3 5.3 %collective-permute-start.2 = (bf16[2048,128]{1,0:T(8,128)(2,1)S(1)}, bf16[2048,128]{1,0:T(8,128)(2,1)S(1)}, u32[]{:S(2)}, u32[]{:S(2)}) collective-permute-start(bf16[2048,128]{1,0:T(8,128)(2,1)S(1)} %collective-permute-done.1.refs_3_), channel_id=1, source_target_pairs={{0,32},{32,0},{64,96},{96,64},{128,160},{160,128},{192,224},{224,1... | collective-permute-start | bytes 1572872 | tf_op jit(solution)/shard_map/ppermute | solution.py:220
  21.6 1.9 %copy.5.scales_ref = f32[1024,16]{1,0:T(8,128)} copy(f32[1024,16]{0,1:T(8,128)} %param.7) | data formatting | bytes 131072 | tf_op args[3]
  23.5 0.0 copy-start.1
  23.5 6.0 %shard_map.47.store_ref = bf16[1024,2048]{1,0:T(8,128)(2,1)} custom-call(bf16[1024,2048]{1,0:T(8,128)(2,1)} %codes_ref.1, f32[1024,16]{1,0:T(8,128)} %copy.5.scales_ref), custom_call_target="tpu_custom_call" | custom-call | flops 2097152 | bytes 8388608 | tf_op jit(solution)/shard_map/pallas_call | solution.py:25
  29.4 0.1 pad_add_fusion.place_ref
  29.5 0.0 collective-permute-done.refs_2_
  29.5 0.0 all-to-all-done
  29.5 0.0 copy-start
  29.5 0.0 collective-permute-done.2.refs_4_
  29.5 0.0 copy-done.1
  29.5 1.7 %shard_map.48 = bf16[8,256,512]{2,1,0:T(8,128)(2,1)S(1)} custom-call(s32[2]{0:T(128)S(1)} %pad_add_fusion.place_ref, bf16[256,2048]{1,0:T(8,128)(2,1)S(1)} %bitcast.8, bf16[2048,128]{1,0:T(8,128)(2,1)S(1)} %bitcast.11, bf16[2048,128]{1,0:T(8,128)(2,1)S(1)} %collective-permute-done.refs_2_, bf16[2048,128]{1,0:T(8,128)(2,1)S(1)} %collective-permute-done.1.refs_3_, ...), custom_call_target="tpu_custom_call" | custom-call | flops 536870912 | bytes 5242880 | tf_op jit(solution)/shard_map/pallas_call | solution.py:84
  31.2 0.5 copy-done
  31.7 2.6 %collective-permute-start.6 = (bf16[1024,2048]{1,0:T(8,128)(2,1)S(1)}, bf16[1024,2048]{1,0:T(8,128)(2,1)S(1)}, u32[]{:S(2)}, u32[]{:S(2)}) collective-permute-start(bf16[1024,2048]{1,0:T(8,128)(2,1)S(1)} %copy-done), channel_id=1, source_target_pairs={{0,32},{32,0},{64,96},{96,64},{128,160},{160,128},{192,224},{224,1... | collective-permute-start | bytes 12582920 | tf_op jit(solution)/shard_map/ppermute | solution.py:232
  34.3 31.8 %all_to_all.15.parts_ref = bf16[8,256,512]{2,1,0:T(8,128)(2,1)S(1)} all-to-all(bf16[8,256,512]{2,1,0:T(8,128)(2,1)S(1)} %shard_map.48), channel_id=1, replica_groups={{0,64,128,192,256,320,384,448},{32,96,160,224,288,352,416,480},{1,65,12..., dimensions={0} | all-to-all | bytes 4194304 | tf_op jit(solution)/shard_map/all_to_all | solution.py:233
  66.1 3.8 %shard_map.49 = (bf16[128,1024]{1,0:T(8,128)(2,1)S(1)}, bf16[128,1024]{1,0:T(8,128)(2,1)S(1)}, bf16[128,1024]{1,0:T(8,128)(2,1)S(1)}, bf16[128,1024]{1,0:T(8,128)(2,1)S(1)}) custom-call(s32[2]{0:T(128)S(1)} %pad_add_fusion.place_ref, bf16[8,256,512]{2,1,0:T(8,128)(2,1)S(1)} %all_to_all.15.parts_ref, bf16[1024,2048]{1,0:T(8,128)(2,1)S(1)} %copy-done), custom_call_target="tpu_custom_call" | custom-call | flops 2147483648 | bytes 7340032 | tf_op jit(solution)/shard_map/pallas_call | solution.py:134
  70.0 2.4 %collective-permute-start.3 = (bf16[128,1024]{1,0:T(8,128)(2,1)S(1)}, bf16[128,1024]{1,0:T(8,128)(2,1)S(1)}, u32[]{:S(2)}, u32[]{:S(2)}) collective-permute-start(bf16[128,1024]{1,0:T(8,128)(2,1)S(1)} %get-tuple-element.28), channel_id=1, source_target_pairs={{0,1},{1,0},{2,3},{3,2},{4,5},{5,4},{6,7},{7,6},{8,9},{9,8},{10,11... | collective-permute-start | bytes 786440 | tf_op jit(solution)/shard_map/ppermute | solution.py:239
  72.4 3.6 %collective-permute-start.4 = (bf16[128,1024]{1,0:T(8,128)(2,1)S(1)}, bf16[128,1024]{1,0:T(8,128)(2,1)S(1)}, u32[]{:S(2)}, u32[]{:S(2)}) collective-permute-start(bf16[128,1024]{1,0:T(8,128)(2,1)S(1)} %get-tuple-element.29), channel_id=1, source_target_pairs={{0,2},{1,3},{2,0},{3,1},{4,6},{5,7},{6,4},{7,5},{8,10},{9,11},{10,... | collective-permute-start | bytes 786440 | tf_op jit(solution)/shard_map/ppermute | solution.py:239
  76.0 2.5 %collective-permute-start.5 = (bf16[128,1024]{1,0:T(8,128)(2,1)S(1)}, bf16[128,1024]{1,0:T(8,128)(2,1)S(1)}, u32[]{:S(2)}, u32[]{:S(2)}) collective-permute-start(bf16[128,1024]{1,0:T(8,128)(2,1)S(1)} %get-tuple-element.30), channel_id=1, source_target_pairs={{0,3},{1,2},{2,1},{3,0},{4,7},{5,6},{6,5},{7,4},{8,11},{9,10},{10,... | collective-permute-start | bytes 786440 | tf_op jit(solution)/shard_map/ppermute | solution.py:239
  78.5 0.0 collective-permute-done.6.store_ref
  78.5 3.8 %shard_map.50 = (bf16[128,1024]{1,0:T(8,128)(2,1)S(1)}, bf16[128,1024]{1,0:T(8,128)(2,1)S(1)}, bf16[128,1024]{1,0:T(8,128)(2,1)S(1)}, bf16[128,1024]{1,0:T(8,128)(2,1)S(1)}) custom-call(s32[2]{0:T(128)S(1)} %pad_add_fusion.place_ref, bf16[8,256,512]{2,1,0:T(8,128)(2,1)S(1)} %all_to_all.15.parts_ref, bf16[1024,2048]{1,0:T(8,128)(2,1)S(1)} %collective-permute-done.6.store_ref), custom_call_target="tpu_custom_call" | custom-call | flops 2147483648 | bytes 7340032 | tf_op jit(solution)/shard_map/pallas_call | solution.py:134
  82.4 2.5 %collective-permute-start.7 = (bf16[128,1024]{1,0:T(8,128)(2,1)S(1)}, bf16[128,1024]{1,0:T(8,128)(2,1)S(1)}, u32[]{:S(2)}, u32[]{:S(2)}) collective-permute-start(bf16[128,1024]{1,0:T(8,128)(2,1)S(1)} %get-tuple-element.32), channel_id=1, source_target_pairs={{0,1},{1,0},{2,3},{3,2},{4,5},{5,4},{6,7},{7,6},{8,9},{9,8},{10,11... | collective-permute-start | bytes 786440 | tf_op jit(solution)/shard_map/ppermute | solution.py:239
  84.9 3.4 %collective-permute-start.8 = (bf16[128,1024]{1,0:T(8,128)(2,1)S(1)}, bf16[128,1024]{1,0:T(8,128)(2,1)S(1)}, u32[]{:S(2)}, u32[]{:S(2)}) collective-permute-start(bf16[128,1024]{1,0:T(8,128)(2,1)S(1)} %get-tuple-element.33), channel_id=1, source_target_pairs={{0,2},{1,3},{2,0},{3,1},{4,6},{5,7},{6,4},{7,5},{8,10},{9,11},{10,... | collective-permute-start | bytes 786440 | tf_op jit(solution)/shard_map/ppermute | solution.py:239
  88.2 0.0 collective-permute-done.3.refs_1_
  88.2 2.5 %collective-permute-start.9 = (bf16[128,1024]{1,0:T(8,128)(2,1)S(1)}, bf16[128,1024]{1,0:T(8,128)(2,1)S(1)}, u32[]{:S(2)}, u32[]{:S(2)}) collective-permute-start(bf16[128,1024]{1,0:T(8,128)(2,1)S(1)} %get-tuple-element.34), channel_id=1, source_target_pairs={{0,3},{1,2},{2,1},{3,0},{4,7},{5,6},{6,5},{7,4},{8,11},{9,10},{10,... | collective-permute-start | bytes 786440 | tf_op jit(solution)/shard_map/ppermute | solution.py:239
  90.8 0.0 collective-permute-done.4.refs_2_
  90.8 0.0 collective-permute-done.5.refs_3_
  90.8 2.8 %collective-permute-done.7.refs_5_ = bf16[128,1024]{1,0:T(8,128)(2,1)S(1)} collective-permute-done((bf16[128,1024]{1,0:T(8,128)(2,1)S(1)}, bf16[128,1024]{1,0:T(8,128)(2,1)S(1)}, u32[]{:S(2)}, u32[]{:S(2)}) %collective-permute-start.7) | collective-permute-done | bytes 262176 | tf_op jit(solution)/shard_map/ppermute | solution.py:239
  93.5 0.0 collective-permute-done.8.refs_6_
  93.5 5.3 %collective-permute-done.9.refs_7_ = bf16[128,1024]{1,0:T(8,128)(2,1)S(1)} collective-permute-done((bf16[128,1024]{1,0:T(8,128)(2,1)S(1)}, bf16[128,1024]{1,0:T(8,128)(2,1)S(1)}, u32[]{:S(2)}, u32[]{:S(2)}) %collective-permute-start.9) | collective-permute-done | bytes 262176 | tf_op jit(solution)/shard_map/ppermute | solution.py:239
  98.8 0.9 shard_map.51
  99.7 47.6 %all_to_all.16 = bf16[16,16,1024]{2,1,0:T(8,128)(2,1)S(1)} all-to-all(bf16[16,16,1024]{2,1,0:T(8,128)(2,1)S(1)} %shard_map.51), channel_id=1, replica_groups={{0,32,4,36,8,40,12,44,16,48,20,52,24,56,28,60},{1,33,5,37,9,41,13,45,17..., dimensions={0} | all-to-all | bytes 1048576 | tf_op jit(solution)/shard_map/all_to_all | solution.py:242
  147.4 0.1 convert_reduce_fusion
  147.4 0.7 broadcast_multiply_fusion
Async XLA Ops:
  0.0 16.3 %collective-permute-start.1 = (bf16[2048,128]{1,0:T(8,128)(2,1)}, bf16[2048,128]{1,0:T(8,128)(2,1)S(1)}, u32[]{:S(2)}, u32[]{:S(2)}) collective-permute-start(bf16[2048,128]{1,0:T(8,128)(2,1)} %bitcast.9), channel_id=1, source_target_pairs={{0,256},{32,288},{64,320},{96,352},{128,384},{160,416},{192,448},{... | collective-permute-start | bytes 1572872 | tf_op jit(solution)/shard_map/ppermute | solution.py:219
  5.5 1.0 copy-start.2
  7.5 22.0 %all-to-all-start = ((bf16[8,32,2048]{2,1,0:T(8,128)(2,1)}), bf16[8,32,2048]{2,1,0:T(8,128)(2,1)S(1)}, u32[]{:S(2)}, u32[]{:S(2)}) async-start(bf16[8,32,2048]{2,1,0:T(8,128)(2,1)} %shard_map.46), calls=%async_computation | async-start | bytes 2097152 | tf_op jit(solution)/shard_map/all_to_all | solution.py:222
  14.2 15.3 %collective-permute-start = (bf16[2048,128]{1,0:T(8,128)(2,1)}, bf16[2048,128]{1,0:T(8,128)(2,1)S(1)}, u32[]{:S(2)}, u32[]{:S(2)}) collective-permute-start(bf16[2048,128]{1,0:T(8,128)(2,1)} %bitcast.10), channel_id=1, source_target_pairs={{0,32},{32,0},{64,96},{96,64},{128,160},{160,128},{192,224},{224,1... | collective-permute-start | bytes 1572872 | tf_op jit(solution)/shard_map/ppermute | solution.py:218
  16.3 13.2 %collective-permute-start.2 = (bf16[2048,128]{1,0:T(8,128)(2,1)S(1)}, bf16[2048,128]{1,0:T(8,128)(2,1)S(1)}, u32[]{:S(2)}, u32[]{:S(2)}) collective-permute-start(bf16[2048,128]{1,0:T(8,128)(2,1)S(1)} %collective-permute-done.1.refs_3_), channel_id=1, source_target_pairs={{0,32},{32,0},{64,96},{96,64},{128,160},{160,128},{192,224},{224,1... | collective-permute-start | bytes 1572872 | tf_op jit(solution)/shard_map/ppermute | solution.py:220
  23.5 6.1 %copy-start.1 = (bf16[1,2048,128]{2,1,0:T(8,128)(2,1)S(1)}, bf16[1,2048,128]{2,1,0:T(8,128)(2,1)}, u32[]{:S(2)}) copy-start(bf16[1,2048,128]{2,1,0:T(8,128)(2,1)} %param.5) | copy-start | bytes 1572868
  29.5 2.2 %copy-start = (bf16[1024,2048]{1,0:T(8,128)(2,1)S(1)}, bf16[1024,2048]{1,0:T(8,128)(2,1)}, u32[]{:S(2)}) copy-start(bf16[1024,2048]{1,0:T(8,128)(2,1)} %shard_map.47.store_ref) | copy-start | bytes 12582916
  31.7 46.8 %collective-permute-start.6 = (bf16[1024,2048]{1,0:T(8,128)(2,1)S(1)}, bf16[1024,2048]{1,0:T(8,128)(2,1)S(1)}, u32[]{:S(2)}, u32[]{:S(2)}) collective-permute-start(bf16[1024,2048]{1,0:T(8,128)(2,1)S(1)} %copy-done), channel_id=1, source_target_pairs={{0,32},{32,0},{64,96},{96,64},{128,160},{160,128},{192,224},{224,1... | collective-permute-start | bytes 12582920 | tf_op jit(solution)/shard_map/ppermute | solution.py:232
  70.0 18.3 %collective-permute-start.3 = (bf16[128,1024]{1,0:T(8,128)(2,1)S(1)}, bf16[128,1024]{1,0:T(8,128)(2,1)S(1)}, u32[]{:S(2)}, u32[]{:S(2)}) collective-permute-start(bf16[128,1024]{1,0:T(8,128)(2,1)S(1)} %get-tuple-element.28), channel_id=1, source_target_pairs={{0,1},{1,0},{2,3},{3,2},{4,5},{5,4},{6,7},{7,6},{8,9},{9,8},{10,11... | collective-permute-start | bytes 786440 | tf_op jit(solution)/shard_map/ppermute | solution.py:239
  72.4 18.4 %collective-permute-start.4 = (bf16[128,1024]{1,0:T(8,128)(2,1)S(1)}, bf16[128,1024]{1,0:T(8,128)(2,1)S(1)}, u32[]{:S(2)}, u32[]{:S(2)}) collective-permute-start(bf16[128,1024]{1,0:T(8,128)(2,1)S(1)} %get-tuple-element.29), channel_id=1, source_target_pairs={{0,2},{1,3},{2,0},{3,1},{4,6},{5,7},{6,4},{7,5},{8,10},{9,11},{10,... | collective-permute-start | bytes 786440 | tf_op jit(solution)/shard_map/ppermute | solution.py:239
  76.0 14.8 %collective-permute-start.5 = (bf16[128,1024]{1,0:T(8,128)(2,1)S(1)}, bf16[128,1024]{1,0:T(8,128)(2,1)S(1)}, u32[]{:S(2)}, u32[]{:S(2)}) collective-permute-start(bf16[128,1024]{1,0:T(8,128)(2,1)S(1)} %get-tuple-element.30), channel_id=1, source_target_pairs={{0,3},{1,2},{2,1},{3,0},{4,7},{5,6},{6,5},{7,4},{8,11},{9,10},{10,... | collective-permute-start | bytes 786440 | tf_op jit(solution)/shard_map/ppermute | solution.py:239
  82.4 11.2 %collective-permute-start.7 = (bf16[128,1024]{1,0:T(8,128)(2,1)S(1)}, bf16[128,1024]{1,0:T(8,128)(2,1)S(1)}, u32[]{:S(2)}, u32[]{:S(2)}) collective-permute-start(bf16[128,1024]{1,0:T(8,128)(2,1)S(1)} %get-tuple-element.32), channel_id=1, source_target_pairs={{0,1},{1,0},{2,3},{3,2},{4,5},{5,4},{6,7},{7,6},{8,9},{9,8},{10,11... | collective-permute-start | bytes 786440 | tf_op jit(solution)/shard_map/ppermute | solution.py:239
  84.9 8.7 %collective-permute-start.8 = (bf16[128,1024]{1,0:T(8,128)(2,1)S(1)}, bf16[128,1024]{1,0:T(8,128)(2,1)S(1)}, u32[]{:S(2)}, u32[]{:S(2)}) collective-permute-start(bf16[128,1024]{1,0:T(8,128)(2,1)S(1)} %get-tuple-element.33), channel_id=1, source_target_pairs={{0,2},{1,3},{2,0},{3,1},{4,6},{5,7},{6,4},{7,5},{8,10},{9,11},{10,... | collective-permute-start | bytes 786440 | tf_op jit(solution)/shard_map/ppermute | solution.py:239
  88.2 10.6 %collective-permute-start.9 = (bf16[128,1024]{1,0:T(8,128)(2,1)S(1)}, bf16[128,1024]{1,0:T(8,128)(2,1)S(1)}, u32[]{:S(2)}, u32[]{:S(2)}) collective-permute-start(bf16[128,1024]{1,0:T(8,128)(2,1)S(1)} %get-tuple-element.34), channel_id=1, source_target_pairs={{0,3},{1,2},{2,1},{3,0},{4,7},{5,6},{6,5},{7,4},{8,11},{9,10},{10,... | collective-permute-start | bytes 786440 | tf_op jit(solution)/shard_map/ppermute | solution.py:239

commit v5 on v4

--- a/solution.py
+++ b/solution.py
@@ -1,3 +1,5 @@
+import functools
+
 import jax
 import jax.numpy as jnp
 from jax import lax
@@ -97,8 +99,8 @@
     )(place, grads, *columns)
 
 
-def score(place_ref, parts_ref, store_ref, *refs):
-    out_refs, queries = refs[:NEAR], refs[NEAR]
+def score(apart, place_ref, parts_ref, store_ref, *refs):
+    out_refs, queries = refs[:-1], refs[-1]
     block_rows, columns = parts_ref.shape[1], parts_ref.shape[2] // ROWS_X
     rows = block_rows // ROWS_Y
     tile = rows // NEAR
@@ -108,8 +110,11 @@
         for x in range(ROWS_X):
             for pair in range(ROWS_Y):
                 for near in range(NEAR):
-                    to = (near ^ place_ref[1]) * (PAIRS * tile) + (x * ROWS_Y + pair) * tile
-                    to = pl.multiple_of(to, tile)
+                    to = (x * ROWS_Y + pair) * tile
+                    if apart:
+                        to = pl.multiple_of((near ^ place_ref[1]) * (PAIRS * tile) + to, tile)
+                    else:
+                        to += near * PAIRS * tile
                     row = pair * rows + near * tile
                     for y in range(ROWS_Y):
                         for k in range(ROWS_X):
@@ -122,17 +127,26 @@
         queries[...], store_ref[...], (((1,), (1,)), ((), ())),
         preferred_element_type=jnp.float32,
     )
-    for k, ref in enumerate(out_refs):
-        ref[...] = term[k * PAIRS * tile : (k + 1) * PAIRS * tile].astype(ref.dtype)
-
-
-def scores_of(place, parts, store):
+    for k in range(NEAR):
+        entries = term[k * PAIRS * tile : (k + 1) * PAIRS * tile].astype(out_refs[0].dtype)
+        if apart:
+            out_refs[k][...] = entries
+        else:
+            out_refs[0][k] = entries
+
+
+def scores_of(apart, place, parts, store):
     chips, block_rows, columns = parts.shape
     rows = ROWS_X * block_rows
     examples, width = store.shape
     tile = 256
-    return pl.pallas_call(
-        score,
+    if apart:
+        block, index, shape, count = (rows // NEAR, tile), lambda n, place_ref: (0, n), (rows // NEAR, examples), NEAR
+    else:
+        block, index = (NEAR, rows // NEAR, tile), lambda n, place_ref: (0, 0, n)
+        shape, count = (NEAR, rows // NEAR, examples), 1
+    return pl.pallas_call(
+        functools.partial(score, apart),
         grid_spec=pltpu.PrefetchScalarGridSpec(
             num_scalar_prefetch=1,
             grid=(examples // tile,),
@@ -140,11 +154,11 @@
                 pl.BlockSpec((chips, block_rows, columns), lambda n, place_ref: (0, 0, 0)),
                 pl.BlockSpec((tile, width), lambda n, place_ref: (n, 0)),
             ],
-            out_specs=[pl.BlockSpec((rows // NEAR, tile), lambda n, place_ref: (0, n))] * NEAR,
+            out_specs=[pl.BlockSpec(block, index)] * count,
             scratch_shapes=[pltpu.VMEM((rows, width), jnp.bfloat16)],
         ),
-        out_shape=[jax.ShapeDtypeStruct((rows // NEAR, examples), jnp.bfloat16)] * NEAR,
-        compiler_params=pltpu.CompilerParams(vmem_limit_bytes=32 * MIB),
+        out_shape=[jax.ShapeDtypeStruct(shape, jnp.bfloat16) if apart else pltpu.HBM(shape, jnp.bfloat16)] * count,
+        compiler_params=pltpu.CompilerParams(vmem_limit_bytes=50 * MIB),
         cost_estimate=pl.CostEstimate(
             flops=2 * rows * width * examples,
             bytes_accessed=2 * (rows * width + (width + rows) * examples),
@@ -153,27 +167,31 @@
     )(place, parts, store)
 
 
-def add(place_ref, *refs):
-    out_ref = refs[-1]
+def add(place_ref, gathered_ref, *refs):
+    other_refs, out_ref = refs[:-1], refs[-1]
     tile = out_ref.shape[1]
-    for i in range(CORES):
-        total = refs[i * NEAR][...].astype(jnp.float32)
-        for ref in refs[i * NEAR + 1 : (i + 1) * NEAR]:
-            total += ref[...].astype(jnp.float32)
+    sums = gathered_ref[0].astype(jnp.float32), other_refs[0][...].astype(jnp.float32)
+    for k in range(1, NEAR):
+        sums = (
+            sums[0] + gathered_ref[k].astype(jnp.float32),
+            sums[1] + other_refs[k][...].astype(jnp.float32),
+        )
+    for i, total in enumerate(sums):
         for p in range(out_ref.shape[0] // CORES):
             at = p * CORES + (place_ref[0] ^ i)
             out_ref[at] = total[p * tile : (p + 1) * tile].astype(out_ref.dtype)
 
 
-def added(place, tile, terms):
+def added(place, tile, gathered, others):
     steps = 4
-    rows, examples = terms[0].shape
+    rows, examples = others[0].shape
     return pl.pallas_call(
         add,
         grid_spec=pltpu.PrefetchScalarGridSpec(
             num_scalar_prefetch=1,
             grid=(steps,),
-            in_specs=[pl.BlockSpec((rows // steps, examples), lambda s, place_ref: (s, 0))] * len(terms),
+            in_specs=[pl.BlockSpec((NEAR, rows // steps, examples), lambda s, place_ref: (0, s, 0))]
+            + [pl.BlockSpec((rows // steps, examples), lambda s, place_ref: (s, 0))] * NEAR,
             out_specs=pl.BlockSpec(
                 (PAIRS * CORES // steps, tile, examples), lambda s, place_ref: (s, 0, 0)
             ),
@@ -181,11 +199,11 @@
         out_shape=jax.ShapeDtypeStruct((PAIRS * CORES, tile, examples), jnp.bfloat16),
         compiler_params=pltpu.CompilerParams(vmem_limit_bytes=16 * MIB),
         cost_estimate=pl.CostEstimate(
-            flops=len(terms) * rows * examples,
-            bytes_accessed=3 * len(terms) * rows * examples,
+            flops=2 * NEAR * rows * examples,
+            bytes_accessed=6 * NEAR * rows * examples,
             transcendentals=0,
         ),
-    )(place, *terms)
+    )(place, gathered, *others)
 
 
 def shards(query_grads, precond, codes, scales):
@@ -208,19 +226,20 @@
     chip_group = ROWS_Y * CORES
     beside = [list(range(x * chip_group, (x + 1) * chip_group)) for x in range(ROWS_X)]
     same_core = [[chip * CORES + c for chip in range(chips)] for c in range(CORES)]
+    near = [[pair * NEAR + i for i in range(NEAR)] for pair in range(PAIRS)]
     far = [
         [(chip * CORES + c) * slots + pair * NEAR + i for pair in range(PAIRS) for c in range(CORES)]
         for chip in range(chips)
         for i in range(NEAR)
     ]
 
-    own = precond[0]
+    own, halves = precond[0], spread(query_grads, tile)
     own_other = lax.ppermute(own, "ex", shift(0, 0, 1))
     across = lax.ppermute(own, "ex", shift(1, 0, 0))
     across_other = lax.ppermute(across, "ex", shift(0, 0, 1))
 
     grads = lax.all_to_all(
-        spread(query_grads, tile), "ex", 0, 0, tiled=True, axis_index_groups=beside
+        halves, "ex", 0, 0, tiled=True, axis_index_groups=beside
     ).reshape(ROWS_Y * CORES * 2 * tile, width)
 
     mine = dequantized(codes, scales)
@@ -232,15 +251,14 @@
     theirs = lax.ppermute(mine, "ex", shift(0, 0, 1))
     parts = lax.all_to_all(copies, "ex", 0, 0, tiled=True, axis_index_groups=same_core)
 
-    terms = []
-    for store in (mine, theirs):
-        here, *away = scores_of(place, parts, store)
-        terms += [here] + [
-            lax.ppermute(term, "dim", [(d, d ^ k) for d in range(slots)])
-            for k, term in enumerate(away, 1)
-        ]
+    (terms,) = scores_of(False, place, parts, mine)
+    gathered = lax.all_to_all(terms, "dim", 0, 0, tiled=True, axis_index_groups=near)
+    here, *away = scores_of(True, place, parts, theirs)
+    others = [here] + [
+        lax.ppermute(term, "dim", [(d, d ^ k) for d in range(slots)]) for k, term in enumerate(away, 1)
+    ]
     sums = lax.all_to_all(
-        added(place, tile, terms), ("ex", "dim"), 0, 0, tiled=True, axis_index_groups=far
+        added(place, tile, gathered, others), ("ex", "dim"), 0, 0, tiled=True, axis_index_groups=far
     )
     total = jnp.sum(sums.astype(jnp.float32).reshape(PAIRS, CORES * tile, examples), axis=0)
     return total * float(width * slots) ** (-0.5)

time: 149 us -> 151 us (1.013)
  blocking collectives: 79.4 us -> 49 us
  waiting for transfers between devices: 8.07 us -> 34.6 us
  Pallas kernels: 17.3 us -> 22.9 us
    all_to_all x2 -> x1, blocking collectives: 79.4 us -> 49 us  [shards(): lax.all_to_all(added(place, tile, gathered, others), ('ex', 'dim'), 0, 0,...]
    all_to_all x1 -> x3, waiting for transfers between devices: 0.01 us -> 24 us  [the longest x1 24 us: shards(): lax.all_to_all(copies, 'ex', 0, 0, tiled=True, axis_index_groups=same_core)]
    all_to_all x1 -> x3, starting transfers between devices: 6.78 us -> 16 us  [the longest x1 6.78 us: shards(): lax.all_to_all(halves, 'ex', 0, 0, tiled=True, axis_index_groups=beside)]
    ppermute x6 -> x3, starting transfers between devices: 16.9 us -> 8.56 us  [shards(): lax.ppermute(term, 'dim', [(d, d ^ k) for d in range(slots)])]
    pallas_call x2, Pallas kernels: 7.69 us -> 11.9 us  [scores_of(): pl.pallas_call(functools.partial(score, apart), grid_spec=pltpu.PrefetchS...]
    ppermute x6 -> x3, waiting for transfers between devices: 8.06 us -> 10.6 us  [shards(): lax.ppermute(term, 'dim', [(d, d ^ k) for d in range(slots)])]
    unnamed x7 -> x5, local copies, waits for them, and re-layouts: 3.3 us -> 2.83 us
  transfers between devices with their start and end apart: 11 -> 10, of which waited for: 2 -> 3; matrix products, arithmetic and copies ran while one was open for 1% -> 1% of each run, Pallas kernels for 10% -> 13%
where the time goes in v5:
time: 151 us; the launch traced here: 150 us
  blocking collectives  49 us (32%)
  starting transfers between devices  39.6 us (26%)
  waiting for transfers between devices  34.6 us (23%)
  Pallas kernels  22.9 us (15%)
  local copies, waits for them, and re-layouts  2.83 us (2%)
    all_to_all x1, blocking collectives, shards(): lax.all_to_all(added(place, tile, gathered, others), ('ex', 'dim'), 0, 0,...  49 us
    all_to_all x1, waiting for transfers between devices, shards(): lax.all_to_all(copies, 'ex', 0, 0, tiled=True, axis_index_groups=same_core)  24 us
    pallas_call x2, Pallas kernels, scores_of(): pl.pallas_call(functools.partial(score, apart), grid_spec=pltpu.PrefetchS...  11.9 us
    ppermute x3, waiting for transfers between devices, shards(): lax.ppermute(term, 'dim', [(d, d ^ k) for d in range(slots)])  10.6 us
    ppermute x3, starting transfers between devices, shards(): lax.ppermute(term, 'dim', [(d, d ^ k) for d in range(slots)])  8.56 us
    all_to_all x1, starting transfers between devices, shards(): lax.all_to_all(halves, 'ex', 0, 0, tiled=True, axis_index_groups=beside)  6.78 us
    pallas_call x1, Pallas kernels, dequantized(): pl.pallas_call(dequantize, grid=(rows // tile,), in_specs=[pl.BlockSpec((...  5.99 us
    all_to_all x1, starting transfers between devices, shards(): lax.all_to_all(copies, 'ex', 0, 0, tiled=True, axis_index_groups=same_core)  5.76 us
  transfers between devices with their start and end apart: 10, of which 3 were waited for; matrix products, arithmetic and copies ran while one was open for 1% of the time, Pallas kernels for 13%

profile of v5, /device:TPU:1, one launch (start us, length us, event | category | flops | bytes accessed | tf_op | source)
XLA Modules:
  0.0 150.0 jit_solution(10598146099428118220)
XLA Ops:
  0.0 5.5 %collective-permute-start.1 = (bf16[2048,128]{1,0:T(8,128)(2,1)}, bf16[2048,128]{1,0:T(8,128)(2,1)S(1)}, u32[]{:S(2)}, u32[]{:S(2)}) collective-permute-start(bf16[2048,128]{1,0:T(8,128)(2,1)} %bitcast.9), channel_id=1, source_target_pairs={{0,256},{32,288},{64,320},{96,352},{128,384},{160,416},{192,448},{... | collective-permute-start | bytes 1572872 | tf_op jit(solution)/shard_map/ppermute | solution.py:238
  5.5 0.0 copy-start.1
  5.5 0.9 copy-done.1
  6.4 1.0 shard_map.46
  7.5 6.8 %all-to-all-start = ((bf16[8,32,2048]{2,1,0:T(8,128)(2,1)}), bf16[8,32,2048]{2,1,0:T(8,128)(2,1)S(1)}, u32[]{:S(2)}, u32[]{:S(2)}) async-start(bf16[8,32,2048]{2,1,0:T(8,128)(2,1)} %shard_map.46), calls=%async_computation | async-start | bytes 2097152 | tf_op jit(solution)/shard_map/all_to_all | solution.py:241
  14.2 2.0 %collective-permute-start = (bf16[2048,128]{1,0:T(8,128)(2,1)}, bf16[2048,128]{1,0:T(8,128)(2,1)S(1)}, u32[]{:S(2)}, u32[]{:S(2)}) collective-permute-start(bf16[2048,128]{1,0:T(8,128)(2,1)} %bitcast.10), channel_id=1, source_target_pairs={{0,32},{32,0},{64,96},{96,64},{128,160},{160,128},{192,224},{224,1... | collective-permute-start | bytes 1572872 | tf_op jit(solution)/shard_map/ppermute | solution.py:237
  16.3 0.0 collective-permute-done.1.refs_3_
  16.3 5.3 %collective-permute-start.2 = (bf16[2048,128]{1,0:T(8,128)(2,1)S(1)}, bf16[2048,128]{1,0:T(8,128)(2,1)S(1)}, u32[]{:S(2)}, u32[]{:S(2)}) collective-permute-start(bf16[2048,128]{1,0:T(8,128)(2,1)S(1)} %collective-permute-done.1.refs_3_), channel_id=1, source_target_pairs={{0,32},{32,0},{64,96},{96,64},{128,160},{160,128},{192,224},{224,1... | collective-permute-start | bytes 1572872 | tf_op jit(solution)/shard_map/ppermute | solution.py:239
  21.6 1.9 %copy.5.scales_ref = f32[1024,16]{1,0:T(8,128)} copy(f32[1024,16]{0,1:T(8,128)} %param.7) | data formatting | bytes 131072 | tf_op args[3]
  23.5 0.0 copy-start
  23.5 6.0 %shard_map.47.store_ref = bf16[1024,2048]{1,0:T(8,128)(2,1)} custom-call(bf16[1024,2048]{1,0:T(8,128)(2,1)} %codes_ref.1, f32[1024,16]{1,0:T(8,128)} %copy.5.scales_ref), custom_call_target="tpu_custom_call" | custom-call | flops 2097152 | bytes 8388608 | tf_op jit(solution)/shard_map/pallas_call | solution.py:27
  29.5 0.1 pad_add_fusion.place_ref
  29.5 0.0 collective-permute-done.refs_2_
  29.5 0.0 all-to-all-done
  29.5 0.0 collective-permute-done.2.refs_4_
  29.5 0.0 copy-done
  29.5 3.1 %shard_map.48 = bf16[8,256,512]{2,1,0:T(8,128)(2,1)} custom-call(s32[2]{0:T(128)S(1)} %pad_add_fusion.place_ref, bf16[256,2048]{1,0:T(8,128)(2,1)S(1)} %bitcast.8, bf16[2048,128]{1,0:T(8,128)(2,1)S(1)} %bitcast.11, bf16[2048,128]{1,0:T(8,128)(2,1)S(1)} %collective-permute-done.refs_2_, bf16[2048,128]{1,0:T(8,128)(2,1)S(1)} %collective-permute-done.1.refs_3_, ...), custom_call_target="tpu_custom_call" | custom-call | flops 536870912 | bytes 5242880 | tf_op jit(solution)/shard_map/pallas_call | solution.py:86
  32.6 5.8 %all-to-all-start.1 = ((bf16[8,256,512]{2,1,0:T(8,128)(2,1)}), bf16[8,256,512]{2,1,0:T(8,128)(2,1)S(1)}, u32[]{:S(2)}, u32[]{:S(2)}) async-start(bf16[8,256,512]{2,1,0:T(8,128)(2,1)} %shard_map.48), calls=%async_computation.1 | async-start | bytes 4194304 | tf_op jit(solution)/shard_map/all_to_all | solution.py:252
  38.4 2.2 %collective-permute-start.3 = (bf16[1024,2048]{1,0:T(8,128)(2,1)}, bf16[1024,2048]{1,0:T(8,128)(2,1)}, u32[]{:S(2)}, u32[]{:S(2)}) collective-permute-start(bf16[1024,2048]{1,0:T(8,128)(2,1)} %shard_map.47.store_ref), channel_id=1, source_target_pairs={{0,32},{32,0},{64,96},{96,64},{128,160},{160,128},{192,224},{224,1... | collective-permute-start | bytes 12582920 | tf_op jit(solution)/shard_map/ppermute | solution.py:251
  40.6 24.0 %all-to-all-done.1.parts_ref = bf16[8,256,512]{2,1,0:T(8,128)(2,1)S(1)} async-done(((bf16[8,256,512]{2,1,0:T(8,128)(2,1)}), bf16[8,256,512]{2,1,0:T(8,128)(2,1)S(1)}, u32[]{:S(2)}, u32[]{:S(2)}) %all-to-all-start.1) | async-done | bytes 2097184 | tf_op jit(solution)/shard_map/all_to_all | solution.py:252
  64.6 6.3 %shard_map.49 = bf16[4,128,1024]{2,1,0:T(8,128)(2,1)} custom-call(s32[2]{0:T(128)S(1)} %pad_add_fusion.place_ref, bf16[8,256,512]{2,1,0:T(8,128)(2,1)S(1)} %all-to-all-done.1.parts_ref, bf16[1024,2048]{1,0:T(8,128)(2,1)} %shard_map.47.store_ref), custom_call_target="tpu_custom_call" | custom-call | flops 2147483648 | bytes 7340032 | tf_op jit(solution)/shard_map/pallas_call | solution.py:148
  70.9 3.5 %all-to-all-start.2 = ((bf16[4,128,1024]{2,1,0:T(8,128)(2,1)}), bf16[4,128,1024]{2,1,0:T(8,128)(2,1)S(1)}, u32[]{:S(2)}, u32[]{:S(2)}) async-start(bf16[4,128,1024]{2,1,0:T(8,128)(2,1)} %shard_map.49), calls=%async_computation.2 | async-start | bytes 2097152 | tf_op jit(solution)/shard_map/all_to_all | solution.py:255
  74.4 0.0 collective-permute-done.3.store_ref
  74.4 5.6 %shard_map.50 = (bf16[128,1024]{1,0:T(8,128)(2,1)S(1)}, bf16[128,1024]{1,0:T(8,128)(2,1)S(1)}, bf16[128,1024]{1,0:T(8,128)(2,1)S(1)}, bf16[128,1024]{1,0:T(8,128)(2,1)S(1)}) custom-call(s32[2]{0:T(128)S(1)} %pad_add_fusion.place_ref, bf16[8,256,512]{2,1,0:T(8,128)(2,1)S(1)} %all-to-all-done.1.parts_ref, bf16[1024,2048]{1,0:T(8,128)(2,1)} %collective-permute-done.3.store_ref), custom_call_target="tpu_custom_call" | custom-call | flops 2147483648 | bytes 7340032 | tf_op jit(solution)/shard_map/pallas_call | solution.py:148
  80.0 3.3 %collective-permute-start.4 = (bf16[128,1024]{1,0:T(8,128)(2,1)S(1)}, bf16[128,1024]{1,0:T(8,128)(2,1)S(1)}, u32[]{:S(2)}, u32[]{:S(2)}) collective-permute-start(bf16[128,1024]{1,0:T(8,128)(2,1)S(1)} %get-tuple-element.24), channel_id=1, source_target_pairs={{0,1},{1,0},{2,3},{3,2},{4,5},{5,4},{6,7},{7,6},{8,9},{9,8},{10,11... | collective-permute-start | bytes 786440 | tf_op jit(solution)/shard_map/ppermute | solution.py:258
  83.4 3.1 %collective-permute-start.5 = (bf16[128,1024]{1,0:T(8,128)(2,1)S(1)}, bf16[128,1024]{1,0:T(8,128)(2,1)S(1)}, u32[]{:S(2)}, u32[]{:S(2)}) collective-permute-start(bf16[128,1024]{1,0:T(8,128)(2,1)S(1)} %get-tuple-element.25), channel_id=1, source_target_pairs={{0,2},{1,3},{2,0},{3,1},{4,6},{5,7},{6,4},{7,5},{8,10},{9,11},{10,... | collective-permute-start | bytes 786440 | tf_op jit(solution)/shard_map/ppermute | solution.py:258
  86.5 2.1 %collective-permute-start.6 = (bf16[128,1024]{1,0:T(8,128)(2,1)S(1)}, bf16[128,1024]{1,0:T(8,128)(2,1)S(1)}, u32[]{:S(2)}, u32[]{:S(2)}) collective-permute-start(bf16[128,1024]{1,0:T(8,128)(2,1)S(1)} %get-tuple-element.26), channel_id=1, source_target_pairs={{0,3},{1,2},{2,1},{3,0},{4,7},{5,6},{6,5},{7,4},{8,11},{9,10},{10,... | collective-permute-start | bytes 786440 | tf_op jit(solution)/shard_map/ppermute | solution.py:258
  88.6 4.5 %collective-permute-done.4.refs_1_ = bf16[128,1024]{1,0:T(8,128)(2,1)S(1)} collective-permute-done((bf16[128,1024]{1,0:T(8,128)(2,1)S(1)}, bf16[128,1024]{1,0:T(8,128)(2,1)S(1)}, u32[]{:S(2)}, u32[]{:S(2)}) %collective-permute-start.4) | collective-permute-done | bytes 262176 | tf_op jit(solution)/shard_map/ppermute | solution.py:258
  93.1 0.0 collective-permute-done.5.refs_2_
  93.1 6.1 %collective-permute-done.6.refs_3_ = bf16[128,1024]{1,0:T(8,128)(2,1)S(1)} collective-permute-done((bf16[128,1024]{1,0:T(8,128)(2,1)S(1)}, bf16[128,1024]{1,0:T(8,128)(2,1)S(1)}, u32[]{:S(2)}, u32[]{:S(2)}) %collective-permute-start.6) | collective-permute-done | bytes 262176 | tf_op jit(solution)/shard_map/ppermute | solution.py:258
  99.2 0.0 all-to-all-done.2.gathered_ref
  99.2 1.0 shard_map.51
  100.2 49.0 %all_to_all.20 = bf16[16,16,1024]{2,1,0:T(8,128)(2,1)S(1)} all-to-all(bf16[16,16,1024]{2,1,0:T(8,128)(2,1)S(1)} %shard_map.51), channel_id=1, replica_groups={{0,32,4,36,8,40,12,44,16,48,20,52,24,56,28,60},{1,33,5,37,9,41,13,45,17..., dimensions={0} | all-to-all | bytes 1048576 | tf_op jit(solution)/shard_map/all_to_all | solution.py:260
  149.2 0.1 convert_reduce_fusion
  149.3 0.7 broadcast_multiply_fusion
Async XLA Ops:
  0.0 16.3 %collective-permute-start.1 = (bf16[2048,128]{1,0:T(8,128)(2,1)}, bf16[2048,128]{1,0:T(8,128)(2,1)S(1)}, u32[]{:S(2)}, u32[]{:S(2)}) collective-permute-start(bf16[2048,128]{1,0:T(8,128)(2,1)} %bitcast.9), channel_id=1, source_target_pairs={{0,256},{32,288},{64,320},{96,352},{128,384},{160,416},{192,448},{... | collective-permute-start | bytes 1572872 | tf_op jit(solution)/shard_map/ppermute | solution.py:238
  5.5 1.0 copy-start.1
  7.5 22.1 %all-to-all-start = ((bf16[8,32,2048]{2,1,0:T(8,128)(2,1)}), bf16[8,32,2048]{2,1,0:T(8,128)(2,1)S(1)}, u32[]{:S(2)}, u32[]{:S(2)}) async-start(bf16[8,32,2048]{2,1,0:T(8,128)(2,1)} %shard_map.46), calls=%async_computation | async-start | bytes 2097152 | tf_op jit(solution)/shard_map/all_to_all | solution.py:241
  14.2 15.3 %collective-permute-start = (bf16[2048,128]{1,0:T(8,128)(2,1)}, bf16[2048,128]{1,0:T(8,128)(2,1)S(1)}, u32[]{:S(2)}, u32[]{:S(2)}) collective-permute-start(bf16[2048,128]{1,0:T(8,128)(2,1)} %bitcast.10), channel_id=1, source_target_pairs={{0,32},{32,0},{64,96},{96,64},{128,160},{160,128},{192,224},{224,1... | collective-permute-start | bytes 1572872 | tf_op jit(solution)/shard_map/ppermute | solution.py:237
  16.3 13.3 %collective-permute-start.2 = (bf16[2048,128]{1,0:T(8,128)(2,1)S(1)}, bf16[2048,128]{1,0:T(8,128)(2,1)S(1)}, u32[]{:S(2)}, u32[]{:S(2)}) collective-permute-start(bf16[2048,128]{1,0:T(8,128)(2,1)S(1)} %collective-permute-done.1.refs_3_), channel_id=1, source_target_pairs={{0,32},{32,0},{64,96},{96,64},{128,160},{160,128},{192,224},{224,1... | collective-permute-start | bytes 1572872 | tf_op jit(solution)/shard_map/ppermute | solution.py:239
  23.5 6.1 %copy-start = (bf16[1,2048,128]{2,1,0:T(8,128)(2,1)S(1)}, bf16[1,2048,128]{2,1,0:T(8,128)(2,1)}, u32[]{:S(2)}) copy-start(bf16[1,2048,128]{2,1,0:T(8,128)(2,1)} %param.5) | copy-start | bytes 1572868
  32.6 32.0 %all-to-all-start.1 = ((bf16[8,256,512]{2,1,0:T(8,128)(2,1)}), bf16[8,256,512]{2,1,0:T(8,128)(2,1)S(1)}, u32[]{:S(2)}, u32[]{:S(2)}) async-start(bf16[8,256,512]{2,1,0:T(8,128)(2,1)} %shard_map.48), calls=%async_computation.1 | async-start | bytes 4194304 | tf_op jit(solution)/shard_map/all_to_all | solution.py:252
  38.4 36.1 %collective-permute-start.3 = (bf16[1024,2048]{1,0:T(8,128)(2,1)}, bf16[1024,2048]{1,0:T(8,128)(2,1)}, u32[]{:S(2)}, u32[]{:S(2)}) collective-permute-start(bf16[1024,2048]{1,0:T(8,128)(2,1)} %shard_map.47.store_ref), channel_id=1, source_target_pairs={{0,32},{32,0},{64,96},{96,64},{128,160},{160,128},{192,224},{224,1... | collective-permute-start | bytes 12582920 | tf_op jit(solution)/shard_map/ppermute | solution.py:251
  70.9 28.3 %all-to-all-start.2 = ((bf16[4,128,1024]{2,1,0:T(8,128)(2,1)}), bf16[4,128,1024]{2,1,0:T(8,128)(2,1)S(1)}, u32[]{:S(2)}, u32[]{:S(2)}) async-start(bf16[4,128,1024]{2,1,0:T(8,128)(2,1)} %shard_map.49), calls=%async_computation.2 | async-start | bytes 2097152 | tf_op jit(solution)/shard_map/all_to_all | solution.py:255
  80.0 13.1 %collective-permute-start.4 = (bf16[128,1024]{1,0:T(8,128)(2,1)S(1)}, bf16[128,1024]{1,0:T(8,128)(2,1)S(1)}, u32[]{:S(2)}, u32[]{:S(2)}) collective-permute-start(bf16[128,1024]{1,0:T(8,128)(2,1)S(1)} %get-tuple-element.24), channel_id=1, source_target_pairs={{0,1},{1,0},{2,3},{3,2},{4,5},{5,4},{6,7},{7,6},{8,9},{9,8},{10,11... | collective-permute-start | bytes 786440 | tf_op jit(solution)/shard_map/ppermute | solution.py:258
  83.4 9.7 %collective-permute-start.5 = (bf16[128,1024]{1,0:T(8,128)(2,1)S(1)}, bf16[128,1024]{1,0:T(8,128)(2,1)S(1)}, u32[]{:S(2)}, u32[]{:S(2)}) collective-permute-start(bf16[128,1024]{1,0:T(8,128)(2,1)S(1)} %get-tuple-element.25), channel_id=1, source_target_pairs={{0,2},{1,3},{2,0},{3,1},{4,6},{5,7},{6,4},{7,5},{8,10},{9,11},{10,... | collective-permute-start | bytes 786440 | tf_op jit(solution)/shard_map/ppermute | solution.py:258
  86.5 12.7 %collective-permute-start.6 = (bf16[128,1024]{1,0:T(8,128)(2,1)S(1)}, bf16[128,1024]{1,0:T(8,128)(2,1)S(1)}, u32[]{:S(2)}, u32[]{:S(2)}) collective-permute-start(bf16[128,1024]{1,0:T(8,128)(2,1)S(1)} %get-tuple-element.26), channel_id=1, source_target_pairs={{0,3},{1,2},{2,1},{3,0},{4,7},{5,6},{6,5},{7,4},{8,11},{9,10},{10,... | collective-permute-start | bytes 786440 | tf_op jit(solution)/shard_map/ppermute | solution.py:258

commit v6 on v5

--- a/solution.py
+++ b/solution.py
@@ -40,24 +40,38 @@
     )(codes, scales)
 
 
-def copy_halves(grads_ref, out_ref):
+def copy_all(copies):
+    for copy in copies:
+        copy.start()
+    for copy in copies:
+        copy.wait()
+
+
+def copy_halves(grads_ref, out_ref, sems):
     tile = out_ref.shape[1] // 2
-    for b in range(2):
+    copies = []
+    for y in range(ROWS_Y):
         for core in range(CORES):
-            row = (b * CORES + core) * tile
-            entries = grads_ref[row : row + tile, :]
-            for y in range(ROWS_Y):
-                out_ref[y * CORES + core, b * tile : (b + 1) * tile, :] = entries
+            for b in range(2):
+                copies.append(
+                    pltpu.make_async_copy(
+                        grads_ref.at[pl.ds((b * CORES + core) * tile, tile)],
+                        out_ref.at[y * CORES + core, pl.ds(b * tile, tile)],
+                        sems.at[len(copies)],
+                    )
+                )
+    copy_all(copies)
 
 
 def spread(grads, tile):
     rows, width = grads.shape
     return pl.pallas_call(
         copy_halves,
-        in_specs=[pl.BlockSpec(memory_space=pltpu.VMEM)],
-        out_specs=pl.BlockSpec(memory_space=pltpu.VMEM),
-        out_shape=jax.ShapeDtypeStruct((ROWS_Y * CORES, 2 * tile, width), grads.dtype),
-        compiler_params=pltpu.CompilerParams(vmem_limit_bytes=8 * MIB),
+        in_specs=[pl.BlockSpec(memory_space=pltpu.HBM)],
+        out_specs=pl.BlockSpec(memory_space=pltpu.HBM),
+        out_shape=pltpu.HBM((ROWS_Y * CORES, 2 * tile, width), grads.dtype),
+        scratch_shapes=[pltpu.SemaphoreType.DMA((ROWS_Y * CORES * 2,))],
+        compiler_params=pltpu.CompilerParams(vmem_limit_bytes=60 * MIB),
         cost_estimate=pl.CostEstimate(
             flops=0, bytes_accessed=2 * (1 + ROWS_Y) * rows * width, transcendentals=0
         ),
@@ -65,7 +79,7 @@
 
 
 def condition(place_ref, *refs):
-    grads_ref, column_refs, (parts_ref, weights) = refs[0], refs[1:-2], refs[-2:]
+    grads_ref, column_refs, (parts_ref, weights, block, sems) = refs[0], refs[1:-4], refs[-4:]
     columns = column_refs[0].shape[1]
     for core in range(CORES):
 
@@ -76,8 +90,13 @@
                 weights[:, at : at + columns] = ref[...]
 
     part = jnp.dot(grads_ref[...], weights[...], preferred_element_type=jnp.float32)
-    for chip in range(parts_ref.shape[0]):
-        parts_ref[chip] = part.astype(parts_ref.dtype)
+    block[...] = part.astype(block.dtype)
+    copy_all(
+        [
+            pltpu.make_async_copy(block, parts_ref.at[chip], sems.at[chip])
+            for chip in range(parts_ref.shape[0])
+        ]
+    )
 
 
 def conditioned_for(place, chips, grads, columns):
@@ -87,9 +106,13 @@
         condition,
         in_specs=[pl.BlockSpec(memory_space=pltpu.SMEM)]
         + [pl.BlockSpec(memory_space=pltpu.VMEM)] * (1 + len(columns)),
-        out_specs=pl.BlockSpec(memory_space=pltpu.VMEM),
-        out_shape=jax.ShapeDtypeStruct((chips, rows, out), jnp.bfloat16),
-        scratch_shapes=[pltpu.VMEM((width, out), jnp.bfloat16)],
+        out_specs=pl.BlockSpec(memory_space=pltpu.HBM),
+        out_shape=pltpu.HBM((chips, rows, out), jnp.bfloat16),
+        scratch_shapes=[
+            pltpu.VMEM((width, out), jnp.bfloat16),
+            pltpu.VMEM((rows, out), jnp.bfloat16),
+            pltpu.SemaphoreType.DMA((chips,)),
+        ],
         compiler_params=pltpu.CompilerParams(vmem_limit_bytes=16 * MIB),
         cost_estimate=pl.CostEstimate(
             flops=2 * rows * width * out,
@@ -100,64 +123,89 @@
 
 
 def score(apart, place_ref, parts_ref, store_ref, *refs):
-    out_refs, queries = refs[:-1], refs[-1]
+    out_refs, (queries, held, ready, terms, sent) = refs[:-5], refs[-5:]
     block_rows, columns = parts_ref.shape[1], parts_ref.shape[2] // ROWS_X
     rows = block_rows // ROWS_Y
     tile = rows // NEAR
-
-    @pl.when(pl.program_id(0) == 0)
-    def _():
-        for x in range(ROWS_X):
-            for pair in range(ROWS_Y):
-                for near in range(NEAR):
-                    to = (x * ROWS_Y + pair) * tile
-                    if apart:
-                        to = pl.multiple_of((near ^ place_ref[1]) * (PAIRS * tile) + to, tile)
-                    else:
-                        to += near * PAIRS * tile
-                    row = pair * rows + near * tile
-                    for y in range(ROWS_Y):
-                        for k in range(ROWS_X):
-                            at = ((x ^ k) * ROWS_Y + y) * columns
-                            queries[pl.ds(to, tile), at : at + columns] = parts_ref[
-                                x * ROWS_Y + y, row : row + tile, k * columns : (k + 1) * columns
-                            ]
-
-    term = lax.dot_general(
-        queries[...], store_ref[...], (((1,), (1,)), ((), ())),
-        preferred_element_type=jnp.float32,
-    )
-    for k in range(NEAR):
-        entries = term[k * PAIRS * tile : (k + 1) * PAIRS * tile].astype(out_refs[0].dtype)
-        if apart:
-            out_refs[k][...] = entries
-        else:
-            out_refs[0][k] = entries
+    steps = ready.shape[0]
+    examples = held.shape[0] // steps
+    copies = [
+        pltpu.make_async_copy(
+            store_ref.at[pl.ds(n * examples, examples)], held.at[pl.ds(n * examples, examples)], ready.at[n]
+        )
+        for n in range(steps)
+    ]
+    for copy in copies:
+        copy.start()
+
+    for x in range(ROWS_X):
+        for pair in range(ROWS_Y):
+            for near in range(NEAR):
+                to = (x * ROWS_Y + pair) * tile
+                if apart:
+                    to = pl.multiple_of((near ^ place_ref[1]) * (PAIRS * tile) + to, tile)
+                else:
+                    to += near * PAIRS * tile
+                row = pair * rows + near * tile
+                for y in range(ROWS_Y):
+                    for k in range(ROWS_X):
+                        at = ((x ^ k) * ROWS_Y + y) * columns
+                        queries[pl.ds(to, tile), at : at + columns] = parts_ref[
+                            x * ROWS_Y + y, row : row + tile, k * columns : (k + 1) * columns
+                        ]
+
+    out_copies = []
+    for n, copy in enumerate(copies):
+        copy.wait()
+        span = slice(n * examples, (n + 1) * examples)
+        term = lax.dot_general(
+            queries[...], held[span, :], (((1,), (1,)), ((), ())),
+            preferred_element_type=jnp.float32,
+        ).astype(terms.dtype)
+        for k in range(NEAR):
+            entries = term[k * PAIRS * tile : (k + 1) * PAIRS * tile]
+            if apart:
+                out_refs[k][:, span] = entries
+            else:
+                terms[k, :, span] = entries
+        if not apart:
+            span = pl.ds(n * examples, examples)
+            out_copies.append(
+                pltpu.make_async_copy(terms.at[:, :, span], out_refs[0].at[:, :, span], sent.at[n])
+            )
+            out_copies[-1].start()
+    for copy in out_copies:
+        copy.wait()
 
 
 def scores_of(apart, place, parts, store):
     chips, block_rows, columns = parts.shape
     rows = ROWS_X * block_rows
     examples, width = store.shape
-    tile = 256
+    steps = 4
+    whole = (NEAR, rows // NEAR, examples)
     if apart:
-        block, index, shape, count = (rows // NEAR, tile), lambda n, place_ref: (0, n), (rows // NEAR, examples), NEAR
+        out_specs = [pl.BlockSpec(memory_space=pltpu.VMEM)] * NEAR
+        out_shape = [jax.ShapeDtypeStruct(whole[1:], jnp.bfloat16)] * NEAR
     else:
-        block, index = (NEAR, rows // NEAR, tile), lambda n, place_ref: (0, 0, n)
-        shape, count = (NEAR, rows // NEAR, examples), 1
+        out_specs = [pl.BlockSpec(memory_space=pltpu.HBM)]
+        out_shape = [pltpu.HBM(whole, jnp.bfloat16)]
     return pl.pallas_call(
         functools.partial(score, apart),
-        grid_spec=pltpu.PrefetchScalarGridSpec(
-            num_scalar_prefetch=1,
-            grid=(examples // tile,),
-            in_specs=[
-                pl.BlockSpec((chips, block_rows, columns), lambda n, place_ref: (0, 0, 0)),
-                pl.BlockSpec((tile, width), lambda n, place_ref: (n, 0)),
-            ],
-            out_specs=[pl.BlockSpec(block, index)] * count,
-            scratch_shapes=[pltpu.VMEM((rows, width), jnp.bfloat16)],
-        ),
-        out_shape=[jax.ShapeDtypeStruct(shape, jnp.bfloat16) if apart else pltpu.HBM(shape, jnp.bfloat16)] * count,
+        in_specs=[
+            pl.BlockSpec(memory_space=pltpu.SMEM),
+            pl.BlockSpec(memory_space=pltpu.VMEM),
+            pl.BlockSpec(memory_space=pltpu.HBM),
+        ],
+        out_specs=out_specs,
+        out_shape=out_shape,
+        scratch_shapes=[
+            pltpu.VMEM((rows, width), jnp.bfloat16),
+            pltpu.VMEM((examples, width), jnp.bfloat16),
+            pltpu.SemaphoreType.DMA((steps,)),
+            pltpu.VMEM((NEAR, 16, 128) if apart else whole, jnp.bfloat16),
+            pltpu.SemaphoreType.DMA((steps,)),
+        ],
         compiler_params=pltpu.CompilerParams(vmem_limit_bytes=50 * MIB),
         cost_estimate=pl.CostEstimate(
             flops=2 * rows * width * examples,
@@ -236,13 +284,14 @@
     own, halves = precond[0], spread(query_grads, tile)
     own_other = lax.ppermute(own, "ex", shift(0, 0, 1))
     across = lax.ppermute(own, "ex", shift(1, 0, 0))
+    mine = dequantized(codes, scales)
+    across, mine = lax.optimization_barrier((across, mine))
     across_other = lax.ppermute(across, "ex", shift(0, 0, 1))
 
     grads = lax.all_to_all(
         halves, "ex", 0, 0, tiled=True, axis_index_groups=beside
     ).reshape(ROWS_Y * CORES * 2 * tile, width)
 
-    mine = dequantized(codes, scales)
     grads, mine, own_other, across, across_other = lax.optimization_barrier(
         (grads, mine, own_other, across, across_other)
     )

time: 151 us -> 177 us (1.17)
  Pallas kernels: 22.9 us -> 57.6 us
  blocking collectives: 49 us -> 42.5 us
  starting transfers between devices: 39.6 us -> 36.8 us
    pallas_call x3, Pallas kernels: 12.9 us -> 47.6 us  [the longest x1 33 us: spread(): pl.pallas_call(copy_halves, in_specs=[pl.BlockSpec(memory_space=pltpu.HBM...]
    all_to_all x1, blocking collectives: 49 us -> 42.5 us  [shards(): lax.all_to_all(added(place, tile, gathered, others), ('ex', 'dim'), 0, 0,...]
    ppermute x1, starting transfers between devices: 5.28 us -> 2.29 us  [shards(): across_other = lax.ppermute(across, 'ex', shift(0, 0, 1))]
    all_to_all x1, waiting for transfers between devices: 0.01 us -> 2.81 us  [shards(): lax.all_to_all(halves, 'ex', 0, 0, tiled=True, axis_index_groups=beside)]
  transfers between devices with their start and end apart: 10 -> 10, of which waited for: 3 -> 4; matrix products, arithmetic and copies ran while one was open for 1% -> 1% of each run, Pallas kernels for 13% -> 30%
where the time goes in v6:
time: 177 us; the launch traced here: 176 us
  Pallas kernels  57.6 us (33%)
  blocking collectives  42.5 us (24%)
  starting transfers between devices  36.8 us (21%)
  waiting for transfers between devices  36.1 us (20%)
  local copies, waits for them, and re-layouts  1.89 us (1%)
    all_to_all x1, blocking collectives, shards(): lax.all_to_all(added(place, tile, gathered, others), ('ex', 'dim'), 0, 0,...  42.5 us
    pallas_call x1, Pallas kernels, spread(): pl.pallas_call(copy_halves, in_specs=[pl.BlockSpec(memory_space=pltpu.HBM...  33 us
    all_to_all x1, waiting for transfers between devices, shards(): lax.all_to_all(copies, 'ex', 0, 0, tiled=True, axis_index_groups=same_core)  23.9 us
    pallas_call x2, Pallas kernels, scores_of(): pl.pallas_call(functools.partial(score, apart), in_specs=[pl.BlockSpec(me...  14.6 us
    ppermute x3, waiting for transfers between devices, shards(): lax.ppermute(term, 'dim', [(d, d ^ k) for d in range(slots)])  9.42 us
    ppermute x3, starting transfers between devices, shards(): lax.ppermute(term, 'dim', [(d, d ^ k) for d in range(slots)])  8.37 us
    all_to_all x1, starting transfers between devices, shards(): lax.all_to_all(halves, 'ex', 0, 0, tiled=True, axis_index_groups=beside)  6.79 us
    pallas_call x1, Pallas kernels, dequantized(): pl.pallas_call(dequantize, grid=(rows // tile,), in_specs=[pl.BlockSpec((...  5.99 us
  transfers between devices with their start and end apart: 10, of which 4 were waited for; matrix products, arithmetic and copies ran while one was open for 1% of the time, Pallas kernels for 30%

profile of v6, /device:TPU:1, one launch (start us, length us, event | category | flops | bytes accessed | tf_op | source)
XLA Modules:
  0.0 175.9 jit_solution(1061480757185297701)
XLA Ops:
  0.0 5.5 %collective-permute-start = (bf16[2048,128]{1,0:T(8,128)(2,1)}, bf16[2048,128]{1,0:T(8,128)(2,1)S(1)}, u32[]{:S(2)}, u32[]{:S(2)}) collective-permute-start(bf16[2048,128]{1,0:T(8,128)(2,1)} %bitcast.9), channel_id=1, source_target_pairs={{0,256},{32,288},{64,320},{96,352},{128,384},{160,416},{192,448},{... | collective-permute-start | bytes 1572872 | tf_op jit(solution)/shard_map/ppermute | solution.py:286
  5.5 33.0 %shard_map.46 = bf16[8,32,2048]{2,1,0:T(8,128)(2,1)} custom-call(bf16[64,2048]{1,0:T(8,128)(2,1)} %grads_ref.1), custom_call_target="tpu_custom_call" | custom-call | bytes 1310720 | tf_op jit(solution)/shard_map/pallas_call | solution.py:68
  38.5 6.8 %all-to-all-start = ((bf16[8,32,2048]{2,1,0:T(8,128)(2,1)}), bf16[8,32,2048]{2,1,0:T(8,128)(2,1)S(1)}, u32[]{:S(2)}, u32[]{:S(2)}) async-start(bf16[8,32,2048]{2,1,0:T(8,128)(2,1)} %shard_map.46), calls=%async_computation | async-start | bytes 2097152 | tf_op jit(solution)/shard_map/all_to_all | solution.py:291
  45.3 2.0 %collective-permute-start.1 = (bf16[2048,128]{1,0:T(8,128)(2,1)}, bf16[2048,128]{1,0:T(8,128)(2,1)S(1)}, u32[]{:S(2)}, u32[]{:S(2)}) collective-permute-start(bf16[2048,128]{1,0:T(8,128)(2,1)} %bitcast.10), channel_id=1, source_target_pairs={{0,32},{32,0},{64,96},{96,64},{128,160},{160,128},{192,224},{224,1... | collective-permute-start | bytes 1572872 | tf_op jit(solution)/shard_map/ppermute | solution.py:285
  47.3 1.9 %copy.5.scales_ref = f32[1024,16]{1,0:T(8,128)} copy(f32[1024,16]{0,1:T(8,128)} %param.7) | data formatting | bytes 131072 | tf_op args[3]
  49.2 0.0 copy-start
  49.2 6.0 %shard_map.47.store_ref = bf16[1024,2048]{1,0:T(8,128)(2,1)} custom-call(bf16[1024,2048]{1,0:T(8,128)(2,1)} %codes_ref.1, f32[1024,16]{1,0:T(8,128)} %copy.5.scales_ref), custom_call_target="tpu_custom_call" | custom-call | flops 2097152 | bytes 8388608 | tf_op jit(solution)/shard_map/pallas_call | solution.py:27
  55.2 0.0 collective-permute-done.refs_3_
  55.2 2.3 %collective-permute-start.2 = (bf16[2048,128]{1,0:T(8,128)(2,1)S(1)}, bf16[2048,128]{1,0:T(8,128)(2,1)S(1)}, u32[]{:S(2)}, u32[]{:S(2)}) collective-permute-start(bf16[2048,128]{1,0:T(8,128)(2,1)S(1)} %collective-permute-done.refs_3_), channel_id=1, source_target_pairs={{0,32},{32,0},{64,96},{96,64},{128,160},{160,128},{192,224},{224,1... | collective-permute-start | bytes 1572872 | tf_op jit(solution)/shard_map/ppermute | solution.py:289
  57.5 0.1 pad_add_fusion.place_ref
  57.6 0.0 collective-permute-done.1.refs_2_
  57.6 2.8 %all-to-all-done = bf16[8,32,2048]{2,1,0:T(8,128)(2,1)S(1)} async-done(((bf16[8,32,2048]{2,1,0:T(8,128)(2,1)}), bf16[8,32,2048]{2,1,0:T(8,128)(2,1)S(1)}, u32[]{:S(2)}, u32[]{:S(2)}) %all-to-all-start) | async-done | bytes 1048608 | tf_op jit(solution)/shard_map/all_to_all | solution.py:291
  60.4 0.0 collective-permute-done.2.refs_4_
  60.4 0.0 copy-done
  60.4 3.1 %shard_map.48 = bf16[8,256,512]{2,1,0:T(8,128)(2,1)} custom-call(s32[2]{0:T(128)S(1)} %pad_add_fusion.place_ref, bf16[256,2048]{1,0:T(8,128)(2,1)S(1)} %bitcast.8, bf16[2048,128]{1,0:T(8,128)(2,1)S(1)} %bitcast.11, bf16[2048,128]{1,0:T(8,128)(2,1)S(1)} %collective-permute-done.1.refs_2_, bf16[2048,128]{1,0:T(8,128)(2,1)S(1)} %collective-permute-done.refs_3_, ...), custom_call_target="tpu_custom_call" | custom-call | flops 536870912 | bytes 5242880 | tf_op jit(solution)/shard_map/pallas_call | solution.py:105
  63.5 6.0 %all-to-all-start.1 = ((bf16[8,256,512]{2,1,0:T(8,128)(2,1)}), bf16[8,256,512]{2,1,0:T(8,128)(2,1)S(1)}, u32[]{:S(2)}, u32[]{:S(2)}) async-start(bf16[8,256,512]{2,1,0:T(8,128)(2,1)} %shard_map.48), calls=%async_computation.1 | async-start | bytes 4194304 | tf_op jit(solution)/shard_map/all_to_all | solution.py:301
  69.4 2.3 %collective-permute-start.3 = (bf16[1024,2048]{1,0:T(8,128)(2,1)}, bf16[1024,2048]{1,0:T(8,128)(2,1)}, u32[]{:S(2)}, u32[]{:S(2)}) collective-permute-start(bf16[1024,2048]{1,0:T(8,128)(2,1)} %shard_map.47.store_ref), channel_id=1, source_target_pairs={{0,32},{32,0},{64,96},{96,64},{128,160},{160,128},{192,224},{224,1... | collective-permute-start | bytes 12582920 | tf_op jit(solution)/shard_map/ppermute | solution.py:300
  71.8 23.9 %all-to-all-done.1.parts_ref = bf16[8,256,512]{2,1,0:T(8,128)(2,1)S(1)} async-done(((bf16[8,256,512]{2,1,0:T(8,128)(2,1)}), bf16[8,256,512]{2,1,0:T(8,128)(2,1)S(1)}, u32[]{:S(2)}, u32[]{:S(2)}) %all-to-all-start.1) | async-done | bytes 2097184 | tf_op jit(solution)/shard_map/all_to_all | solution.py:301
  95.7 7.6 %shard_map.49 = bf16[4,128,1024]{2,1,0:T(8,128)(2,1)} custom-call(s32[2]{0:T(128)S(1)} %pad_add_fusion.place_ref, bf16[8,256,512]{2,1,0:T(8,128)(2,1)S(1)} %all-to-all-done.1.parts_ref, bf16[1024,2048]{1,0:T(8,128)(2,1)} %shard_map.47.store_ref), custom_call_target="tpu_custom_call" | custom-call | flops 2147483648 | bytes 7340032 | tf_op jit(solution)/shard_map/pallas_call | solution.py:193
  103.3 3.5 %all-to-all-start.2 = ((bf16[4,128,1024]{2,1,0:T(8,128)(2,1)}), bf16[4,128,1024]{2,1,0:T(8,128)(2,1)S(1)}, u32[]{:S(2)}, u32[]{:S(2)}) async-start(bf16[4,128,1024]{2,1,0:T(8,128)(2,1)} %shard_map.49), calls=%async_computation.2 | async-start | bytes 2097152 | tf_op jit(solution)/shard_map/all_to_all | solution.py:304
  106.8 0.0 collective-permute-done.3.store_ref
  106.9 6.9 %shard_map.50 = (bf16[128,1024]{1,0:T(8,128)(2,1)S(1)}, bf16[128,1024]{1,0:T(8,128)(2,1)S(1)}, bf16[128,1024]{1,0:T(8,128)(2,1)S(1)}, bf16[128,1024]{1,0:T(8,128)(2,1)S(1)}) custom-call(s32[2]{0:T(128)S(1)} %pad_add_fusion.place_ref, bf16[8,256,512]{2,1,0:T(8,128)(2,1)S(1)} %all-to-all-done.1.parts_ref, bf16[1024,2048]{1,0:T(8,128)(2,1)} %collective-permute-done.3.store_ref), custom_call_target="tpu_custom_call" | custom-call | flops 2147483648 | bytes 7340032 | tf_op jit(solution)/shard_map/pallas_call | solution.py:193
  113.8 3.3 %collective-permute-start.4 = (bf16[128,1024]{1,0:T(8,128)(2,1)S(1)}, bf16[128,1024]{1,0:T(8,128)(2,1)S(1)}, u32[]{:S(2)}, u32[]{:S(2)}) collective-permute-start(bf16[128,1024]{1,0:T(8,128)(2,1)S(1)} %get-tuple-element.28), channel_id=1, source_target_pairs={{0,1},{1,0},{2,3},{3,2},{4,5},{5,4},{6,7},{7,6},{8,9},{9,8},{10,11... | collective-permute-start | bytes 786440 | tf_op jit(solution)/shard_map/ppermute | solution.py:307
  117.1 3.1 %collective-permute-start.5 = (bf16[128,1024]{1,0:T(8,128)(2,1)S(1)}, bf16[128,1024]{1,0:T(8,128)(2,1)S(1)}, u32[]{:S(2)}, u32[]{:S(2)}) collective-permute-start(bf16[128,1024]{1,0:T(8,128)(2,1)S(1)} %get-tuple-element.29), channel_id=1, source_target_pairs={{0,2},{1,3},{2,0},{3,1},{4,6},{5,7},{6,4},{7,5},{8,10},{9,11},{10,... | collective-permute-start | bytes 786440 | tf_op jit(solution)/shard_map/ppermute | solution.py:307
  120.2 1.9 %collective-permute-start.6 = (bf16[128,1024]{1,0:T(8,128)(2,1)S(1)}, bf16[128,1024]{1,0:T(8,128)(2,1)S(1)}, u32[]{:S(2)}, u32[]{:S(2)}) collective-permute-start(bf16[128,1024]{1,0:T(8,128)(2,1)S(1)} %get-tuple-element.30), channel_id=1, source_target_pairs={{0,3},{1,2},{2,1},{3,0},{4,7},{5,6},{6,5},{7,4},{8,11},{9,10},{10,... | collective-permute-start | bytes 786440 | tf_op jit(solution)/shard_map/ppermute | solution.py:307
  122.2 3.3 %collective-permute-done.4.refs_1_ = bf16[128,1024]{1,0:T(8,128)(2,1)S(1)} collective-permute-done((bf16[128,1024]{1,0:T(8,128)(2,1)S(1)}, bf16[128,1024]{1,0:T(8,128)(2,1)S(1)}, u32[]{:S(2)}, u32[]{:S(2)}) %collective-permute-start.4) | collective-permute-done | bytes 262176 | tf_op jit(solution)/shard_map/ppermute | solution.py:307
  125.5 0.0 collective-permute-done.5.refs_2_
  125.5 6.1 %collective-permute-done.6.refs_3_ = bf16[128,1024]{1,0:T(8,128)(2,1)S(1)} collective-permute-done((bf16[128,1024]{1,0:T(8,128)(2,1)S(1)}, bf16[128,1024]{1,0:T(8,128)(2,1)S(1)}, u32[]{:S(2)}, u32[]{:S(2)}) %collective-permute-start.6) | collective-permute-done | bytes 262176 | tf_op jit(solution)/shard_map/ppermute | solution.py:307
  131.6 0.0 all-to-all-done.2.gathered_ref
  131.6 1.0 shard_map.51
  132.6 42.5 %all_to_all.20 = bf16[16,16,1024]{2,1,0:T(8,128)(2,1)S(1)} all-to-all(bf16[16,16,1024]{2,1,0:T(8,128)(2,1)S(1)} %shard_map.51), channel_id=1, replica_groups={{0,32,4,36,8,40,12,44,16,48,20,52,24,56,28,60},{1,33,5,37,9,41,13,45,17..., dimensions={0} | all-to-all | bytes 1048576 | tf_op jit(solution)/shard_map/all_to_all | solution.py:309
  175.1 0.1 convert_reduce_fusion
  175.2 0.7 broadcast_multiply_fusion
Async XLA Ops:
  0.0 55.2 %collective-permute-start = (bf16[2048,128]{1,0:T(8,128)(2,1)}, bf16[2048,128]{1,0:T(8,128)(2,1)S(1)}, u32[]{:S(2)}, u32[]{:S(2)}) collective-permute-start(bf16[2048,128]{1,0:T(8,128)(2,1)} %bitcast.9), channel_id=1, source_target_pairs={{0,256},{32,288},{64,320},{96,352},{128,384},{160,416},{192,448},{... | collective-permute-start | bytes 1572872 | tf_op jit(solution)/shard_map/ppermute | solution.py:286
  38.5 21.9 %all-to-all-start = ((bf16[8,32,2048]{2,1,0:T(8,128)(2,1)}), bf16[8,32,2048]{2,1,0:T(8,128)(2,1)S(1)}, u32[]{:S(2)}, u32[]{:S(2)}) async-start(bf16[8,32,2048]{2,1,0:T(8,128)(2,1)} %shard_map.46), calls=%async_computation | async-start | bytes 2097152 | tf_op jit(solution)/shard_map/all_to_all | solution.py:291
  45.3 12.3 %collective-permute-start.1 = (bf16[2048,128]{1,0:T(8,128)(2,1)}, bf16[2048,128]{1,0:T(8,128)(2,1)S(1)}, u32[]{:S(2)}, u32[]{:S(2)}) collective-permute-start(bf16[2048,128]{1,0:T(8,128)(2,1)} %bitcast.10), channel_id=1, source_target_pairs={{0,32},{32,0},{64,96},{96,64},{128,160},{160,128},{192,224},{224,1... | collective-permute-start | bytes 1572872 | tf_op jit(solution)/shard_map/ppermute | solution.py:285
  49.2 11.2 %copy-start = (bf16[1,2048,128]{2,1,0:T(8,128)(2,1)S(1)}, bf16[1,2048,128]{2,1,0:T(8,128)(2,1)}, u32[]{:S(2)}) copy-start(bf16[1,2048,128]{2,1,0:T(8,128)(2,1)} %param.5) | copy-start | bytes 1572868
  55.2 5.2 %collective-permute-start.2 = (bf16[2048,128]{1,0:T(8,128)(2,1)S(1)}, bf16[2048,128]{1,0:T(8,128)(2,1)S(1)}, u32[]{:S(2)}, u32[]{:S(2)}) collective-permute-start(bf16[2048,128]{1,0:T(8,128)(2,1)S(1)} %collective-permute-done.refs_3_), channel_id=1, source_target_pairs={{0,32},{32,0},{64,96},{96,64},{128,160},{160,128},{192,224},{224,1... | collective-permute-start | bytes 1572872 | tf_op jit(solution)/shard_map/ppermute | solution.py:289
  63.5 32.2 %all-to-all-start.1 = ((bf16[8,256,512]{2,1,0:T(8,128)(2,1)}), bf16[8,256,512]{2,1,0:T(8,128)(2,1)S(1)}, u32[]{:S(2)}, u32[]{:S(2)}) async-start(bf16[8,256,512]{2,1,0:T(8,128)(2,1)} %shard_map.48), calls=%async_computation.1 | async-start | bytes 4194304 | tf_op jit(solution)/shard_map/all_to_all | solution.py:301
  69.4 37.4 %collective-permute-start.3 = (bf16[1024,2048]{1,0:T(8,128)(2,1)}, bf16[1024,2048]{1,0:T(8,128)(2,1)}, u32[]{:S(2)}, u32[]{:S(2)}) collective-permute-start(bf16[1024,2048]{1,0:T(8,128)(2,1)} %shard_map.47.store_ref), channel_id=1, source_target_pairs={{0,32},{32,0},{64,96},{96,64},{128,160},{160,128},{192,224},{224,1... | collective-permute-start | bytes 12582920 | tf_op jit(solution)/shard_map/ppermute | solution.py:300
  103.3 28.3 %all-to-all-start.2 = ((bf16[4,128,1024]{2,1,0:T(8,128)(2,1)}), bf16[4,128,1024]{2,1,0:T(8,128)(2,1)S(1)}, u32[]{:S(2)}, u32[]{:S(2)}) async-start(bf16[4,128,1024]{2,1,0:T(8,128)(2,1)} %shard_map.49), calls=%async_computation.2 | async-start | bytes 2097152 | tf_op jit(solution)/shard_map/all_to_all | solution.py:304
  113.8 11.7 %collective-permute-start.4 = (bf16[128,1024]{1,0:T(8,128)(2,1)S(1)}, bf16[128,1024]{1,0:T(8,128)(2,1)S(1)}, u32[]{:S(2)}, u32[]{:S(2)}) collective-permute-start(bf16[128,1024]{1,0:T(8,128)(2,1)S(1)} %get-tuple-element.28), channel_id=1, source_target_pairs={{0,1},{1,0},{2,3},{3,2},{4,5},{5,4},{6,7},{7,6},{8,9},{9,8},{10,11... | collective-permute-start | bytes 786440 | tf_op jit(solution)/shard_map/ppermute | solution.py:307
  117.1 8.4 %collective-permute-start.5 = (bf16[128,1024]{1,0:T(8,128)(2,1)S(1)}, bf16[128,1024]{1,0:T(8,128)(2,1)S(1)}, u32[]{:S(2)}, u32[]{:S(2)}) collective-permute-start(bf16[128,1024]{1,0:T(8,128)(2,1)S(1)} %get-tuple-element.29), channel_id=1, source_target_pairs={{0,2},{1,3},{2,0},{3,1},{4,6},{5,7},{6,4},{7,5},{8,10},{9,11},{10,... | collective-permute-start | bytes 786440 | tf_op jit(solution)/shard_map/ppermute | solution.py:307
  120.2 11.4 %collective-permute-start.6 = (bf16[128,1024]{1,0:T(8,128)(2,1)S(1)}, bf16[128,1024]{1,0:T(8,128)(2,1)S(1)}, u32[]{:S(2)}, u32[]{:S(2)}) collective-permute-start(bf16[128,1024]{1,0:T(8,128)(2,1)S(1)} %get-tuple-element.30), channel_id=1, source_target_pairs={{0,3},{1,2},{2,1},{3,0},{4,7},{5,6},{6,5},{7,4},{8,11},{9,10},{10,... | collective-permute-start | bytes 786440 | tf_op jit(solution)/shard_map/ppermute | solution.py:307

commit v7 on v5

--- a/solution.py
+++ b/solution.py
@@ -236,13 +236,14 @@
     own, halves = precond[0], spread(query_grads, tile)
     own_other = lax.ppermute(own, "ex", shift(0, 0, 1))
     across = lax.ppermute(own, "ex", shift(1, 0, 0))
+    mine = dequantized(codes, scales)
+    across, mine = lax.optimization_barrier((across, mine))
     across_other = lax.ppermute(across, "ex", shift(0, 0, 1))
 
     grads = lax.all_to_all(
         halves, "ex", 0, 0, tiled=True, axis_index_groups=beside
     ).reshape(ROWS_Y * CORES * 2 * tile, width)
 
-    mine = dequantized(codes, scales)
     grads, mine, own_other, across, across_other = lax.optimization_barrier(
         (grads, mine, own_other, across, across_other)
     )
@@ -255,7 +256,10 @@
     gathered = lax.all_to_all(terms, "dim", 0, 0, tiled=True, axis_index_groups=near)
     here, *away = scores_of(True, place, parts, theirs)
     others = [here] + [
-        lax.ppermute(term, "dim", [(d, d ^ k) for d in range(slots)]) for k, term in enumerate(away, 1)
+        lax.ppermute(
+            term, "dim", [(d, (((d + SIDES) ^ k) - SIDES) % slots if k & SIDES else d ^ k) for d in range(slots)]
+        )
+        for k, term in enumerate(away, 1)
     ]
     sums = lax.all_to_all(
         added(place, tile, gathered, others), ("ex", "dim"), 0, 0, tiled=True, axis_index_groups=far

time: 151 us -> 146 us (0.967)
  blocking collectives: 49 us -> 41.4 us
  starting transfers between devices: 39.6 us -> 41.3 us
    all_to_all x1, blocking collectives: 49 us -> 41.4 us  [shards(): lax.all_to_all(added(place, tile, gathered, others), ('ex', 'dim'), 0, 0,...]
    ppermute x3, starting transfers between devices: 8.56 us -> 13 us  [shards(): lax.ppermute(term, 'dim', [(d, ((d + SIDES ^ k) - SIDES) % slots if k & S...]
    ppermute x1, starting transfers between devices: 5.28 us -> 2.29 us  [shards(): across_other = lax.ppermute(across, 'ex', shift(0, 0, 1))]
    all_to_all x1, waiting for transfers between devices: 0.01 us -> 2.82 us  [shards(): lax.all_to_all(halves, 'ex', 0, 0, tiled=True, axis_index_groups=beside)]
    ppermute x3, waiting for transfers between devices: 10.6 us -> 8.08 us  [shards(): lax.ppermute(term, 'dim', [(d, ((d + SIDES ^ k) - SIDES) % slots if k & S...]
  transfers between devices with their start and end apart: 10 -> 10, of which waited for: 3 -> 5; matrix products, arithmetic and copies ran while one was open for 1% -> 1% of each run, Pallas kernels for 13% -> 13%
where the time goes in v7:
time: 146 us; the launch traced here: 144 us
  blocking collectives  41.4 us (28%)
  starting transfers between devices  41.3 us (28%)
  waiting for transfers between devices  34.8 us (24%)
  Pallas kernels  22.9 us (16%)
  local copies, waits for them, and re-layouts  2.83 us (2%)
    all_to_all x1, blocking collectives, shards(): lax.all_to_all(added(place, tile, gathered, others), ('ex', 'dim'), 0, 0,...  41.4 us
    all_to_all x1, waiting for transfers between devices, shards(): lax.all_to_all(copies, 'ex', 0, 0, tiled=True, axis_index_groups=same_core)  23.9 us
    ppermute x3, starting transfers between devices, shards(): lax.ppermute(term, 'dim', [(d, ((d + SIDES ^ k) - SIDES) % slots if k & S...  13 us
    pallas_call x2, Pallas kernels, scores_of(): pl.pallas_call(functools.partial(score, apart), grid_spec=pltpu.PrefetchS...  11.9 us
    ppermute x3, waiting for transfers between devices, shards(): lax.ppermute(term, 'dim', [(d, ((d + SIDES ^ k) - SIDES) % slots if k & S...  8.08 us
    all_to_all x1, starting transfers between devices, shards(): lax.all_to_all(halves, 'ex', 0, 0, tiled=True, axis_index_groups=beside)  6.78 us
    pallas_call x1, Pallas kernels, dequantized(): pl.pallas_call(dequantize, grid=(rows // tile,), in_specs=[pl.BlockSpec((...  5.99 us
    all_to_all x1, starting transfers between devices, shards(): lax.all_to_all(copies, 'ex', 0, 0, tiled=True, axis_index_groups=same_core)  5.96 us
  transfers between devices with their start and end apart: 10, of which 5 were waited for; matrix products, arithmetic and copies ran while one was open for 1% of the time, Pallas kernels for 13%

profile of v7, /device:TPU:1, one launch (start us, length us, event | category | flops | bytes accessed | tf_op | source)
XLA Modules:
  0.0 144.2 jit_solution(15340542480985393643)
XLA Ops:
  0.0 5.5 %collective-permute-start = (bf16[2048,128]{1,0:T(8,128)(2,1)}, bf16[2048,128]{1,0:T(8,128)(2,1)S(1)}, u32[]{:S(2)}, u32[]{:S(2)}) collective-permute-start(bf16[2048,128]{1,0:T(8,128)(2,1)} %bitcast.9), channel_id=1, source_target_pairs={{0,256},{32,288},{64,320},{96,352},{128,384},{160,416},{192,448},{... | collective-permute-start | bytes 1572872 | tf_op jit(solution)/shard_map/ppermute | solution.py:238
  5.5 0.0 copy-start.1
  5.5 0.9 copy-done.1
  6.4 1.0 shard_map.46
  7.5 6.8 %all-to-all-start = ((bf16[8,32,2048]{2,1,0:T(8,128)(2,1)}), bf16[8,32,2048]{2,1,0:T(8,128)(2,1)S(1)}, u32[]{:S(2)}, u32[]{:S(2)}) async-start(bf16[8,32,2048]{2,1,0:T(8,128)(2,1)} %shard_map.46), calls=%async_computation | async-start | bytes 2097152 | tf_op jit(solution)/shard_map/all_to_all | solution.py:243
  14.2 2.0 %collective-permute-start.1 = (bf16[2048,128]{1,0:T(8,128)(2,1)}, bf16[2048,128]{1,0:T(8,128)(2,1)S(1)}, u32[]{:S(2)}, u32[]{:S(2)}) collective-permute-start(bf16[2048,128]{1,0:T(8,128)(2,1)} %bitcast.10), channel_id=1, source_target_pairs={{0,32},{32,0},{64,96},{96,64},{128,160},{160,128},{192,224},{224,1... | collective-permute-start | bytes 1572872 | tf_op jit(solution)/shard_map/ppermute | solution.py:237
  16.3 1.9 %copy.5.scales_ref = f32[1024,16]{1,0:T(8,128)} copy(f32[1024,16]{0,1:T(8,128)} %param.7) | data formatting | bytes 131072 | tf_op args[3]
  18.1 0.0 copy-start
  18.1 6.0 %shard_map.47.store_ref = bf16[1024,2048]{1,0:T(8,128)(2,1)} custom-call(bf16[1024,2048]{1,0:T(8,128)(2,1)} %codes_ref.1, f32[1024,16]{1,0:T(8,128)} %copy.5.scales_ref), custom_call_target="tpu_custom_call" | custom-call | flops 2097152 | bytes 8388608 | tf_op jit(solution)/shard_map/pallas_call | solution.py:27
  24.1 0.0 collective-permute-done.refs_3_
  24.1 2.3 %collective-permute-start.2 = (bf16[2048,128]{1,0:T(8,128)(2,1)S(1)}, bf16[2048,128]{1,0:T(8,128)(2,1)S(1)}, u32[]{:S(2)}, u32[]{:S(2)}) collective-permute-start(bf16[2048,128]{1,0:T(8,128)(2,1)S(1)} %collective-permute-done.refs_3_), channel_id=1, source_target_pairs={{0,32},{32,0},{64,96},{96,64},{128,160},{160,128},{192,224},{224,1... | collective-permute-start | bytes 1572872 | tf_op jit(solution)/shard_map/ppermute | solution.py:241
  26.5 0.1 pad_add_fusion.place_ref
  26.5 0.0 collective-permute-done.1.refs_2_
  26.5 2.8 %all-to-all-done = bf16[8,32,2048]{2,1,0:T(8,128)(2,1)S(1)} async-done(((bf16[8,32,2048]{2,1,0:T(8,128)(2,1)}), bf16[8,32,2048]{2,1,0:T(8,128)(2,1)S(1)}, u32[]{:S(2)}, u32[]{:S(2)}) %all-to-all-start) | async-done | bytes 1048608 | tf_op jit(solution)/shard_map/all_to_all | solution.py:243
  29.4 0.0 collective-permute-done.2.refs_4_
  29.4 0.0 copy-done
  29.4 3.1 %shard_map.48 = bf16[8,256,512]{2,1,0:T(8,128)(2,1)} custom-call(s32[2]{0:T(128)S(1)} %pad_add_fusion.place_ref, bf16[256,2048]{1,0:T(8,128)(2,1)S(1)} %bitcast.8, bf16[2048,128]{1,0:T(8,128)(2,1)S(1)} %bitcast.11, bf16[2048,128]{1,0:T(8,128)(2,1)S(1)} %collective-permute-done.1.refs_2_, bf16[2048,128]{1,0:T(8,128)(2,1)S(1)} %collective-permute-done.refs_3_, ...), custom_call_target="tpu_custom_call" | custom-call | flops 536870912 | bytes 5242880 | tf_op jit(solution)/shard_map/pallas_call | solution.py:86
  32.4 6.0 %all-to-all-start.1 = ((bf16[8,256,512]{2,1,0:T(8,128)(2,1)}), bf16[8,256,512]{2,1,0:T(8,128)(2,1)S(1)}, u32[]{:S(2)}, u32[]{:S(2)}) async-start(bf16[8,256,512]{2,1,0:T(8,128)(2,1)} %shard_map.48), calls=%async_computation.1 | async-start | bytes 4194304 | tf_op jit(solution)/shard_map/all_to_all | solution.py:253
  38.4 2.3 %collective-permute-start.3 = (bf16[1024,2048]{1,0:T(8,128)(2,1)}, bf16[1024,2048]{1,0:T(8,128)(2,1)}, u32[]{:S(2)}, u32[]{:S(2)}) collective-permute-start(bf16[1024,2048]{1,0:T(8,128)(2,1)} %shard_map.47.store_ref), channel_id=1, source_target_pairs={{0,32},{32,0},{64,96},{96,64},{128,160},{160,128},{192,224},{224,1... | collective-permute-start | bytes 12582920 | tf_op jit(solution)/shard_map/ppermute | solution.py:252
  40.7 23.9 %all-to-all-done.1.parts_ref = bf16[8,256,512]{2,1,0:T(8,128)(2,1)S(1)} async-done(((bf16[8,256,512]{2,1,0:T(8,128)(2,1)}), bf16[8,256,512]{2,1,0:T(8,128)(2,1)S(1)}, u32[]{:S(2)}, u32[]{:S(2)}) %all-to-all-start.1) | async-done | bytes 2097184 | tf_op jit(solution)/shard_map/all_to_all | solution.py:253
  64.6 6.3 %shard_map.49 = bf16[4,128,1024]{2,1,0:T(8,128)(2,1)} custom-call(s32[2]{0:T(128)S(1)} %pad_add_fusion.place_ref, bf16[8,256,512]{2,1,0:T(8,128)(2,1)S(1)} %all-to-all-done.1.parts_ref, bf16[1024,2048]{1,0:T(8,128)(2,1)} %shard_map.47.store_ref), custom_call_target="tpu_custom_call" | custom-call | flops 2147483648 | bytes 7340032 | tf_op jit(solution)/shard_map/pallas_call | solution.py:148
  70.9 3.5 %all-to-all-start.2 = ((bf16[4,128,1024]{2,1,0:T(8,128)(2,1)}), bf16[4,128,1024]{2,1,0:T(8,128)(2,1)S(1)}, u32[]{:S(2)}, u32[]{:S(2)}) async-start(bf16[4,128,1024]{2,1,0:T(8,128)(2,1)} %shard_map.49), calls=%async_computation.2 | async-start | bytes 2097152 | tf_op jit(solution)/shard_map/all_to_all | solution.py:256
  74.4 0.0 collective-permute-done.3.store_ref
  74.4 5.6 %shard_map.50 = (bf16[128,1024]{1,0:T(8,128)(2,1)S(1)}, bf16[128,1024]{1,0:T(8,128)(2,1)S(1)}, bf16[128,1024]{1,0:T(8,128)(2,1)S(1)}, bf16[128,1024]{1,0:T(8,128)(2,1)S(1)}) custom-call(s32[2]{0:T(128)S(1)} %pad_add_fusion.place_ref, bf16[8,256,512]{2,1,0:T(8,128)(2,1)S(1)} %all-to-all-done.1.parts_ref, bf16[1024,2048]{1,0:T(8,128)(2,1)} %collective-permute-done.3.store_ref), custom_call_target="tpu_custom_call" | custom-call | flops 2147483648 | bytes 7340032 | tf_op jit(solution)/shard_map/pallas_call | solution.py:148
  80.0 3.3 %collective-permute-start.4 = (bf16[128,1024]{1,0:T(8,128)(2,1)S(1)}, bf16[128,1024]{1,0:T(8,128)(2,1)S(1)}, u32[]{:S(2)}, u32[]{:S(2)}) collective-permute-start(bf16[128,1024]{1,0:T(8,128)(2,1)S(1)} %get-tuple-element.28), channel_id=1, source_target_pairs={{0,1},{1,0},{2,3},{3,2},{4,5},{5,4},{6,7},{7,6},{8,9},{9,8},{10,11... | collective-permute-start | bytes 786440 | tf_op jit(solution)/shard_map/ppermute | solution.py:259
  83.3 7.7 %collective-permute-start.5 = (bf16[128,1024]{1,0:T(8,128)(2,1)S(1)}, bf16[128,1024]{1,0:T(8,128)(2,1)S(1)}, u32[]{:S(2)}, u32[]{:S(2)}) collective-permute-start(bf16[128,1024]{1,0:T(8,128)(2,1)S(1)} %get-tuple-element.29), channel_id=1, source_target_pairs={{0,30},{1,31},{2,4},{3,5},{4,2},{5,3},{6,8},{7,9},{8,6},{9,7},{10,... | collective-permute-start | bytes 786440 | tf_op jit(solution)/shard_map/ppermute | solution.py:259
  91.1 1.9 %collective-permute-start.6 = (bf16[128,1024]{1,0:T(8,128)(2,1)S(1)}, bf16[128,1024]{1,0:T(8,128)(2,1)S(1)}, u32[]{:S(2)}, u32[]{:S(2)}) collective-permute-start(bf16[128,1024]{1,0:T(8,128)(2,1)S(1)} %get-tuple-element.30), channel_id=1, source_target_pairs={{0,31},{1,30},{2,5},{3,4},{4,3},{5,2},{6,9},{7,8},{8,7},{9,6},{10,... | collective-permute-start | bytes 786440 | tf_op jit(solution)/shard_map/ppermute | solution.py:259
  93.0 0.1 collective-permute-done.4.refs_1_
  93.1 2.8 %collective-permute-done.5.refs_2_ = bf16[128,1024]{1,0:T(8,128)(2,1)S(1)} collective-permute-done((bf16[128,1024]{1,0:T(8,128)(2,1)S(1)}, bf16[128,1024]{1,0:T(8,128)(2,1)S(1)}, u32[]{:S(2)}, u32[]{:S(2)}) %collective-permute-start.5) | collective-permute-done | bytes 262176 | tf_op jit(solution)/shard_map/ppermute | solution.py:259
  95.9 5.2 %collective-permute-done.6.refs_3_ = bf16[128,1024]{1,0:T(8,128)(2,1)S(1)} collective-permute-done((bf16[128,1024]{1,0:T(8,128)(2,1)S(1)}, bf16[128,1024]{1,0:T(8,128)(2,1)S(1)}, u32[]{:S(2)}, u32[]{:S(2)}) %collective-permute-start.6) | collective-permute-done | bytes 262176 | tf_op jit(solution)/shard_map/ppermute | solution.py:259
  101.1 0.0 all-to-all-done.2.gathered_ref
  101.1 1.0 shard_map.51
  102.1 41.4 %all_to_all.20 = bf16[16,16,1024]{2,1,0:T(8,128)(2,1)S(1)} all-to-all(bf16[16,16,1024]{2,1,0:T(8,128)(2,1)S(1)} %shard_map.51), channel_id=1, replica_groups={{0,32,4,36,8,40,12,44,16,48,20,52,24,56,28,60},{1,33,5,37,9,41,13,45,17..., dimensions={0} | all-to-all | bytes 1048576 | tf_op jit(solution)/shard_map/all_to_all | solution.py:264
  143.5 0.1 convert_reduce_fusion
  143.6 0.7 broadcast_multiply_fusion
Async XLA Ops:
  0.0 24.1 %collective-permute-start = (bf16[2048,128]{1,0:T(8,128)(2,1)}, bf16[2048,128]{1,0:T(8,128)(2,1)S(1)}, u32[]{:S(2)}, u32[]{:S(2)}) collective-permute-start(bf16[2048,128]{1,0:T(8,128)(2,1)} %bitcast.9), channel_id=1, source_target_pairs={{0,256},{32,288},{64,320},{96,352},{128,384},{160,416},{192,448},{... | collective-permute-start | bytes 1572872 | tf_op jit(solution)/shard_map/ppermute | solution.py:238
  5.5 1.0 copy-start.1
  7.5 21.9 %all-to-all-start = ((bf16[8,32,2048]{2,1,0:T(8,128)(2,1)}), bf16[8,32,2048]{2,1,0:T(8,128)(2,1)S(1)}, u32[]{:S(2)}, u32[]{:S(2)}) async-start(bf16[8,32,2048]{2,1,0:T(8,128)(2,1)} %shard_map.46), calls=%async_computation | async-start | bytes 2097152 | tf_op jit(solution)/shard_map/all_to_all | solution.py:243
  14.2 12.3 %collective-permute-start.1 = (bf16[2048,128]{1,0:T(8,128)(2,1)}, bf16[2048,128]{1,0:T(8,128)(2,1)S(1)}, u32[]{:S(2)}, u32[]{:S(2)}) collective-permute-start(bf16[2048,128]{1,0:T(8,128)(2,1)} %bitcast.10), channel_id=1, source_target_pairs={{0,32},{32,0},{64,96},{96,64},{128,160},{160,128},{192,224},{224,1... | collective-permute-start | bytes 1572872 | tf_op jit(solution)/shard_map/ppermute | solution.py:237
  18.1 11.2 %copy-start = (bf16[1,2048,128]{2,1,0:T(8,128)(2,1)S(1)}, bf16[1,2048,128]{2,1,0:T(8,128)(2,1)}, u32[]{:S(2)}) copy-start(bf16[1,2048,128]{2,1,0:T(8,128)(2,1)} %param.5) | copy-start | bytes 1572868
  24.1 5.2 %collective-permute-start.2 = (bf16[2048,128]{1,0:T(8,128)(2,1)S(1)}, bf16[2048,128]{1,0:T(8,128)(2,1)S(1)}, u32[]{:S(2)}, u32[]{:S(2)}) collective-permute-start(bf16[2048,128]{1,0:T(8,128)(2,1)S(1)} %collective-permute-done.refs_3_), channel_id=1, source_target_pairs={{0,32},{32,0},{64,96},{96,64},{128,160},{160,128},{192,224},{224,1... | collective-permute-start | bytes 1572872 | tf_op jit(solution)/shard_map/ppermute | solution.py:241
  32.4 32.2 %all-to-all-start.1 = ((bf16[8,256,512]{2,1,0:T(8,128)(2,1)}), bf16[8,256,512]{2,1,0:T(8,128)(2,1)S(1)}, u32[]{:S(2)}, u32[]{:S(2)}) async-start(bf16[8,256,512]{2,1,0:T(8,128)(2,1)} %shard_map.48), calls=%async_computation.1 | async-start | bytes 4194304 | tf_op jit(solution)/shard_map/all_to_all | solution.py:253
  38.4 36.1 %collective-permute-start.3 = (bf16[1024,2048]{1,0:T(8,128)(2,1)}, bf16[1024,2048]{1,0:T(8,128)(2,1)}, u32[]{:S(2)}, u32[]{:S(2)}) collective-permute-start(bf16[1024,2048]{1,0:T(8,128)(2,1)} %shard_map.47.store_ref), channel_id=1, source_target_pairs={{0,32},{32,0},{64,96},{96,64},{128,160},{160,128},{192,224},{224,1... | collective-permute-start | bytes 12582920 | tf_op jit(solution)/shard_map/ppermute | solution.py:252
  70.9 30.2 %all-to-all-start.2 = ((bf16[4,128,1024]{2,1,0:T(8,128)(2,1)}), bf16[4,128,1024]{2,1,0:T(8,128)(2,1)S(1)}, u32[]{:S(2)}, u32[]{:S(2)}) async-start(bf16[4,128,1024]{2,1,0:T(8,128)(2,1)} %shard_map.49), calls=%async_computation.2 | async-start | bytes 2097152 | tf_op jit(solution)/shard_map/all_to_all | solution.py:256
  80.0 13.1 %collective-permute-start.4 = (bf16[128,1024]{1,0:T(8,128)(2,1)S(1)}, bf16[128,1024]{1,0:T(8,128)(2,1)S(1)}, u32[]{:S(2)}, u32[]{:S(2)}) collective-permute-start(bf16[128,1024]{1,0:T(8,128)(2,1)S(1)} %get-tuple-element.28), channel_id=1, source_target_pairs={{0,1},{1,0},{2,3},{3,2},{4,5},{5,4},{6,7},{7,6},{8,9},{9,8},{10,11... | collective-permute-start | bytes 786440 | tf_op jit(solution)/shard_map/ppermute | solution.py:259
  83.3 12.5 %collective-permute-start.5 = (bf16[128,1024]{1,0:T(8,128)(2,1)S(1)}, bf16[128,1024]{1,0:T(8,128)(2,1)S(1)}, u32[]{:S(2)}, u32[]{:S(2)}) collective-permute-start(bf16[128,1024]{1,0:T(8,128)(2,1)S(1)} %get-tuple-element.29), channel_id=1, source_target_pairs={{0,30},{1,31},{2,4},{3,5},{4,2},{5,3},{6,8},{7,9},{8,6},{9,7},{10,... | collective-permute-start | bytes 786440 | tf_op jit(solution)/shard_map/ppermute | solution.py:259
  91.1 10.0 %collective-permute-start.6 = (bf16[128,1024]{1,0:T(8,128)(2,1)S(1)}, bf16[128,1024]{1,0:T(8,128)(2,1)S(1)}, u32[]{:S(2)}, u32[]{:S(2)}) collective-permute-start(bf16[128,1024]{1,0:T(8,128)(2,1)S(1)} %get-tuple-element.30), channel_id=1, source_target_pairs={{0,31},{1,30},{2,5},{3,4},{4,3},{5,2},{6,9},{7,8},{8,7},{9,6},{10,... | collective-permute-start | bytes 786440 | tf_op jit(solution)/shard_map/ppermute | solution.py:259

commit v8 on v7

--- a/solution.py
+++ b/solution.py
@@ -167,43 +167,75 @@
     )(place, parts, store)
 
 
-def add(place_ref, gathered_ref, *refs):
-    other_refs, out_ref = refs[:-1], refs[-1]
-    tile = out_ref.shape[1]
-    sums = gathered_ref[0].astype(jnp.float32), other_refs[0][...].astype(jnp.float32)
-    for k in range(1, NEAR):
-        sums = (
-            sums[0] + gathered_ref[k].astype(jnp.float32),
-            sums[1] + other_refs[k][...].astype(jnp.float32),
-        )
-    for i, total in enumerate(sums):
-        for p in range(out_ref.shape[0] // CORES):
-            at = p * CORES + (place_ref[0] ^ i)
-            out_ref[at] = total[p * tile : (p + 1) * tile].astype(out_ref.dtype)
-
-
-def added(place, tile, gathered, others):
-    steps = 4
-    rows, examples = others[0].shape
-    return pl.pallas_call(
-        add,
+def split(place_ref, *refs):
+    terms, kept_ref, sent_ref = refs[:-2], refs[-2], refs[-1]
+    for i, out_ref in enumerate((kept_ref, sent_ref)):
+        blocks = terms[i::2]
+        if len(blocks) == 1:
+            blocks = [blocks[0].at[k] for k in range(NEAR)]
+        total = blocks[0][...].astype(jnp.float32)
+        for block in blocks[1:]:
+            total += block[...].astype(jnp.float32)
+        out_ref[...] = total.astype(out_ref.dtype)
+
+
+def split_sums(place, tile, terms):
+    half = PAIRS // 2
+    examples = terms[0].shape[-1]
+
+    def spec(ndim, flip):
+        def rows(j, place_ref):
+            return 2 * j + (1 - place_ref[2] if flip else place_ref[2])
+
+        if ndim == 2:
+            return pl.BlockSpec((tile, examples), lambda j, place_ref: (rows(j, place_ref), 0))
+        return pl.BlockSpec((NEAR, tile, examples), lambda j, place_ref: (0, rows(j, place_ref), 0))
+
+    return pl.pallas_call(
+        split,
         grid_spec=pltpu.PrefetchScalarGridSpec(
             num_scalar_prefetch=1,
-            grid=(steps,),
-            in_specs=[pl.BlockSpec((NEAR, rows // steps, examples), lambda s, place_ref: (0, s, 0))]
-            + [pl.BlockSpec((rows // steps, examples), lambda s, place_ref: (s, 0))] * NEAR,
-            out_specs=pl.BlockSpec(
-                (PAIRS * CORES // steps, tile, examples), lambda s, place_ref: (s, 0, 0)
-            ),
-        ),
-        out_shape=jax.ShapeDtypeStruct((PAIRS * CORES, tile, examples), jnp.bfloat16),
+            grid=(half,),
+            in_specs=[spec(term.ndim, flip) for term in terms for flip in (False, True)],
+            out_specs=[pl.BlockSpec((pl.squeezed, tile, examples), lambda j, place_ref: (j, 0, 0))] * 2,
+        ),
+        out_shape=[
+            jax.ShapeDtypeStruct((half, tile, examples), jnp.float32),
+            jax.ShapeDtypeStruct((half, tile, examples), jnp.bfloat16),
+        ],
         compiler_params=pltpu.CompilerParams(vmem_limit_bytes=16 * MIB),
         cost_estimate=pl.CostEstimate(
-            flops=2 * NEAR * rows * examples,
-            bytes_accessed=6 * NEAR * rows * examples,
+            flops=2 * NEAR * half * tile * examples,
+            bytes_accessed=5 * NEAR * half * tile * examples,
             transcendentals=0,
         ),
-    )(place, gathered, *others)
+    )(place, *[term for term in terms for _ in range(2)])
+
+
+def join(place_ref, *refs):
+    out_ref = refs[-1]
+    for i in range(CORES):
+        kept_ref, came_ref = refs[2 * i], refs[2 * i + 1]
+        for j in range(kept_ref.shape[0]):
+            total = kept_ref[j] + came_ref[j].astype(jnp.float32)
+            out_ref[j * CORES + (place_ref[0] ^ i)] = total.astype(out_ref.dtype)
+
+
+def joined(place, *halves):
+    pairs, tile, examples = halves[0].shape
+    return pl.pallas_call(
+        join,
+        in_specs=[pl.BlockSpec(memory_space=pltpu.SMEM)]
+        + [pl.BlockSpec(memory_space=pltpu.VMEM)] * len(halves),
+        out_specs=pl.BlockSpec(memory_space=pltpu.VMEM),
+        out_shape=jax.ShapeDtypeStruct((pairs * CORES, tile, examples), jnp.bfloat16),
+        compiler_params=pltpu.CompilerParams(vmem_limit_bytes=16 * MIB),
+        cost_estimate=pl.CostEstimate(
+            flops=CORES * pairs * tile * examples,
+            bytes_accessed=8 * CORES * pairs * tile * examples,
+            transcendentals=0,
+        ),
+    )(place, *halves)
 
 
 def shards(query_grads, precond, codes, scales):
@@ -213,8 +245,8 @@
     tile = own_queries * ex_size // slots // CORES
     chips = ROWS_X * ROWS_Y
     position = lax.axis_index("ex")
-    near_here = lax.axis_index("dim") % NEAR
-    place = jnp.stack([position % CORES, near_here])
+    slot = lax.axis_index("dim")
+    place = jnp.stack([position % CORES, slot % NEAR, slot // NEAR % 2])
     spots = [(x, y, c) for x in range(ROWS_X) for y in range(ROWS_Y) for c in range(CORES)]
 
     def shift(x_by, y_by, core_by):
@@ -228,9 +260,10 @@
     same_core = [[chip * CORES + c for chip in range(chips)] for c in range(CORES)]
     near = [[pair * NEAR + i for i in range(NEAR)] for pair in range(PAIRS)]
     far = [
-        [(chip * CORES + c) * slots + pair * NEAR + i for pair in range(PAIRS) for c in range(CORES)]
+        [(chip * CORES + c) * slots + pair * NEAR + i for pair in range(parity, PAIRS, 2) for c in range(CORES)]
         for chip in range(chips)
         for i in range(NEAR)
+        for parity in range(2)
     ]
 
     own, halves = precond[0], spread(query_grads, tile)
@@ -261,10 +294,18 @@
         )
         for k, term in enumerate(away, 1)
     ]
+    kept, sent = split_sums(place, tile, [gathered])
+    came = lax.ppermute(sent, "dim", [(d, d ^ NEAR) for d in range(slots)])
+    *others, sent = lax.optimization_barrier((*others, sent))
+    kept_other, sent_other = split_sums(place, tile, others)
+    came_other = lax.ppermute(
+        sent_other, "dim", [(d, (((d + NEAR) ^ NEAR) - NEAR) % slots) for d in range(slots)]
+    )
     sums = lax.all_to_all(
-        added(place, tile, gathered, others), ("ex", "dim"), 0, 0, tiled=True, axis_index_groups=far
-    )
-    total = jnp.sum(sums.astype(jnp.float32).reshape(PAIRS, CORES * tile, examples), axis=0)
+        joined(place, kept, came, kept_other, came_other),
+        ("ex", "dim"), 0, 0, tiled=True, axis_index_groups=far,
+    )
+    total = jnp.sum(sums.astype(jnp.float32).reshape(PAIRS // 2, CORES * tile, examples), axis=0)
     return total * float(width * slots) ** (-0.5)
 
 

time: 146 us -> 146 us (level)
  the two profiles are of different devices: /device:TPU:1 before, /device:TPU:6 now
where the time goes in v8:
time: 146 us; the launch traced here: 145 us
  starting transfers between devices  50.5 us (35%)
  waiting for transfers between devices  37.2 us (25%)
  blocking collectives  28.8 us (20%)
  Pallas kernels  25 us (17%)
  local copies, waits for them, and re-layouts  2.82 us (2%)
    all_to_all x1, blocking collectives, shards(): lax.all_to_all(joined(place, kept, came, kept_other, came_other), ('ex',...  28.8 us
    all_to_all x1, waiting for transfers between devices, shards(): lax.all_to_all(copies, 'ex', 0, 0, tiled=True, axis_index_groups=same_core)  24 us
    ppermute x3, starting transfers between devices, shards(): lax.ppermute(term, 'dim', [(d, ((d + SIDES ^ k) - SIDES) % slots if k & S...  13.3 us
    pallas_call x2, Pallas kernels, scores_of(): pl.pallas_call(functools.partial(score, apart), grid_spec=pltpu.PrefetchS...  12.6 us
    ppermute x1, starting transfers between devices, shards(): lax.ppermute(sent_other, 'dim', [(d, ((d + NEAR ^ NEAR) - NEAR) % slots)...  7.85 us
    all_to_all x1, starting transfers between devices, shards(): lax.all_to_all(terms, 'dim', 0, 0, tiled=True, axis_index_groups=near)  7.78 us
    ppermute x3, waiting for transfers between devices, shards(): lax.ppermute(term, 'dim', [(d, ((d + SIDES ^ k) - SIDES) % slots if k & S...  6.63 us
    pallas_call x1, Pallas kernels, dequantized(): pl.pallas_call(dequantize, grid=(rows // tile,), in_specs=[pl.BlockSpec((...  6 us
  transfers between devices with their start and end apart: 12, of which 5 were waited for; matrix products, arithmetic and copies ran while one was open for 1% of the time, Pallas kernels for 15%

profile of v8, /device:TPU:6, one launch (start us, length us, event | category | flops | bytes accessed | tf_op | source)
XLA Modules:
  0.0 145.3 jit_solution(5562551335052478362)
XLA Ops:
  0.0 3.3 %collective-permute-start = (bf16[2048,128]{1,0:T(8,128)(2,1)}, bf16[2048,128]{1,0:T(8,128)(2,1)S(1)}, u32[]{:S(2)}, u32[]{:S(2)}) collective-permute-start(bf16[2048,128]{1,0:T(8,128)(2,1)} %bitcast.10), channel_id=1, source_target_pairs={{0,256},{32,288},{64,320},{96,352},{128,384},{160,416},{192,448},{... | collective-permute-start | bytes 1572872 | tf_op jit(solution)/shard_map/ppermute | solution.py:271
  3.3 0.0 copy-start.1
  3.3 0.9 copy-done.1
  4.3 1.0 shard_map.46
  5.3 4.5 %all-to-all-start = ((bf16[8,32,2048]{2,1,0:T(8,128)(2,1)}), bf16[8,32,2048]{2,1,0:T(8,128)(2,1)S(1)}, u32[]{:S(2)}, u32[]{:S(2)}) async-start(bf16[8,32,2048]{2,1,0:T(8,128)(2,1)} %shard_map.46), calls=%async_computation | async-start | bytes 2097152 | tf_op jit(solution)/shard_map/all_to_all | solution.py:276
  9.8 2.4 %collective-permute-start.1 = (bf16[2048,128]{1,0:T(8,128)(2,1)}, bf16[2048,128]{1,0:T(8,128)(2,1)S(1)}, u32[]{:S(2)}, u32[]{:S(2)}) collective-permute-start(bf16[2048,128]{1,0:T(8,128)(2,1)} %bitcast.11), channel_id=1, source_target_pairs={{0,32},{32,0},{64,96},{96,64},{128,160},{160,128},{192,224},{224,1... | collective-permute-start | bytes 1572872 | tf_op jit(solution)/shard_map/ppermute | solution.py:270
  12.2 1.9 %copy.5.scales_ref = f32[1024,16]{1,0:T(8,128)} copy(f32[1024,16]{0,1:T(8,128)} %param.7) | data formatting | bytes 131072 | tf_op args[3]
  14.1 0.0 copy-start
  14.1 6.0 %shard_map.47.store_ref = bf16[1024,2048]{1,0:T(8,128)(2,1)} custom-call(bf16[1024,2048]{1,0:T(8,128)(2,1)} %codes_ref.1, f32[1024,16]{1,0:T(8,128)} %copy.5.scales_ref), custom_call_target="tpu_custom_call" | custom-call | flops 2097152 | bytes 8388608 | tf_op jit(solution)/shard_map/pallas_call | solution.py:27
  20.1 0.0 collective-permute-done.refs_3_
  20.1 1.9 %collective-permute-start.2 = (bf16[2048,128]{1,0:T(8,128)(2,1)S(1)}, bf16[2048,128]{1,0:T(8,128)(2,1)S(1)}, u32[]{:S(2)}, u32[]{:S(2)}) collective-permute-start(bf16[2048,128]{1,0:T(8,128)(2,1)S(1)} %collective-permute-done.refs_3_), channel_id=1, source_target_pairs={{0,32},{32,0},{64,96},{96,64},{128,160},{160,128},{192,224},{224,1... | collective-permute-start | bytes 1572872 | tf_op jit(solution)/shard_map/ppermute | solution.py:274
  22.0 0.1 pad_add_fusion.place_ref
  22.1 0.0 collective-permute-done.1.refs_2_
  22.1 3.6 %all-to-all-done = bf16[8,32,2048]{2,1,0:T(8,128)(2,1)S(1)} async-done(((bf16[8,32,2048]{2,1,0:T(8,128)(2,1)}), bf16[8,32,2048]{2,1,0:T(8,128)(2,1)S(1)}, u32[]{:S(2)}, u32[]{:S(2)}) %all-to-all-start) | async-done | bytes 1048608 | tf_op jit(solution)/shard_map/all_to_all | solution.py:276
  25.7 0.0 collective-permute-done.2.refs_4_
  25.8 0.0 copy-done
  25.8 3.1 %shard_map.48 = bf16[8,256,512]{2,1,0:T(8,128)(2,1)} custom-call(s32[3]{0:T(128)S(1)} %pad_add_fusion.place_ref, bf16[256,2048]{1,0:T(8,128)(2,1)S(1)} %bitcast.9, bf16[2048,128]{1,0:T(8,128)(2,1)S(1)} %bitcast.12, bf16[2048,128]{1,0:T(8,128)(2,1)S(1)} %collective-permute-done.1.refs_2_, bf16[2048,128]{1,0:T(8,128)(2,1)S(1)} %collective-permute-done.refs_3_, ...), custom_call_target="tpu_custom_call" | custom-call | flops 536870912 | bytes 5242880 | tf_op jit(solution)/shard_map/pallas_call | solution.py:86
  28.8 5.6 %all-to-all-start.1 = ((bf16[8,256,512]{2,1,0:T(8,128)(2,1)}), bf16[8,256,512]{2,1,0:T(8,128)(2,1)S(1)}, u32[]{:S(2)}, u32[]{:S(2)}) async-start(bf16[8,256,512]{2,1,0:T(8,128)(2,1)} %shard_map.48), calls=%async_computation.1 | async-start | bytes 4194304 | tf_op jit(solution)/shard_map/all_to_all | solution.py:286
  34.5 1.9 %collective-permute-start.4 = (bf16[1024,2048]{1,0:T(8,128)(2,1)}, bf16[1024,2048]{1,0:T(8,128)(2,1)}, u32[]{:S(2)}, u32[]{:S(2)}) collective-permute-start(bf16[1024,2048]{1,0:T(8,128)(2,1)} %shard_map.47.store_ref), channel_id=1, source_target_pairs={{0,32},{32,0},{64,96},{96,64},{128,160},{160,128},{192,224},{224,1... | collective-permute-start | bytes 12582920 | tf_op jit(solution)/shard_map/ppermute | solution.py:285
  36.4 24.0 %all-to-all-done.1.parts_ref = bf16[8,256,512]{2,1,0:T(8,128)(2,1)S(1)} async-done(((bf16[8,256,512]{2,1,0:T(8,128)(2,1)}), bf16[8,256,512]{2,1,0:T(8,128)(2,1)S(1)}, u32[]{:S(2)}, u32[]{:S(2)}) %all-to-all-start.1) | async-done | bytes 2097184 | tf_op jit(solution)/shard_map/all_to_all | solution.py:286
  60.4 6.3 %shard_map.49 = bf16[4,128,1024]{2,1,0:T(8,128)(2,1)} custom-call(s32[3]{0:T(128)S(1)} %pad_add_fusion.place_ref, bf16[8,256,512]{2,1,0:T(8,128)(2,1)S(1)} %all-to-all-done.1.parts_ref, bf16[1024,2048]{1,0:T(8,128)(2,1)} %shard_map.47.store_ref), custom_call_target="tpu_custom_call" | custom-call | flops 2147483648 | bytes 7340032 | tf_op jit(solution)/shard_map/pallas_call | solution.py:148
  66.7 7.8 %all-to-all-start.2 = ((bf16[4,128,1024]{2,1,0:T(8,128)(2,1)}), bf16[4,128,1024]{2,1,0:T(8,128)(2,1)S(1)}, u32[]{:S(2)}, u32[]{:S(2)}) async-start(bf16[4,128,1024]{2,1,0:T(8,128)(2,1)} %shard_map.49), calls=%async_computation.2 | async-start | bytes 2097152 | tf_op jit(solution)/shard_map/all_to_all | solution.py:289
  74.5 0.0 collective-permute-done.4.store_ref
  74.5 6.3 %shard_map.51 = (bf16[128,1024]{1,0:T(8,128)(2,1)S(1)}, bf16[128,1024]{1,0:T(8,128)(2,1)}, bf16[128,1024]{1,0:T(8,128)(2,1)}, bf16[128,1024]{1,0:T(8,128)(2,1)}) custom-call(s32[3]{0:T(128)S(1)} %pad_add_fusion.place_ref, bf16[8,256,512]{2,1,0:T(8,128)(2,1)S(1)} %all-to-all-done.1.parts_ref, bf16[1024,2048]{1,0:T(8,128)(2,1)} %collective-permute-done.4.store_ref), custom_call_target="tpu_custom_call" | custom-call | flops 2147483648 | bytes 7340032 | tf_op jit(solution)/shard_map/pallas_call | solution.py:148
  80.7 1.9 %collective-permute-start.5 = (bf16[128,1024]{1,0:T(8,128)(2,1)}, bf16[128,1024]{1,0:T(8,128)(2,1)S(1)}, u32[]{:S(2)}, u32[]{:S(2)}) collective-permute-start(bf16[128,1024]{1,0:T(8,128)(2,1)} %get-tuple-element.38), channel_id=1, source_target_pairs={{0,1},{1,0},{2,3},{3,2},{4,5},{5,4},{6,7},{7,6},{8,9},{9,8},{10,11... | collective-permute-start | bytes 786440 | tf_op jit(solution)/shard_map/ppermute | solution.py:292
  82.7 8.6 %collective-permute-start.6 = (bf16[128,1024]{1,0:T(8,128)(2,1)}, bf16[128,1024]{1,0:T(8,128)(2,1)S(1)}, u32[]{:S(2)}, u32[]{:S(2)}) collective-permute-start(bf16[128,1024]{1,0:T(8,128)(2,1)} %get-tuple-element.39), channel_id=1, source_target_pairs={{0,30},{1,31},{2,4},{3,5},{4,2},{5,3},{6,8},{7,9},{8,6},{9,7},{10,... | collective-permute-start | bytes 786440 | tf_op jit(solution)/shard_map/ppermute | solution.py:292
  91.3 2.8 %collective-permute-start.7 = (bf16[128,1024]{1,0:T(8,128)(2,1)}, bf16[128,1024]{1,0:T(8,128)(2,1)S(1)}, u32[]{:S(2)}, u32[]{:S(2)}) collective-permute-start(bf16[128,1024]{1,0:T(8,128)(2,1)} %get-tuple-element.40), channel_id=1, source_target_pairs={{0,31},{1,30},{2,5},{3,4},{4,3},{5,2},{6,9},{7,8},{8,7},{9,6},{10,... | collective-permute-start | bytes 786440 | tf_op jit(solution)/shard_map/ppermute | solution.py:292
  94.1 0.0 all-to-all-done.2.refs_0_.refs_1_
  94.1 0.9 shard_map.50
  95.0 1.9 %collective-permute-start.3 = (bf16[4,16,1024]{2,1,0:T(8,128)(2,1)S(1)}, bf16[4,16,1024]{2,1,0:T(8,128)(2,1)S(1)}, u32[]{:S(2)}, u32[]{:S(2)}) collective-permute-start(bf16[4,16,1024]{2,1,0:T(8,128)(2,1)S(1)} %get-tuple-element.36), channel_id=1, source_target_pairs={{0,4},{1,5},{2,6},{3,7},{4,0},{5,1},{6,2},{7,3},{8,12},{9,13},{10,... | collective-permute-start | bytes 393224 | tf_op jit(solution)/shard_map/ppermute | solution.py:298
  97.0 0.0 collective-permute-done.5.refs_2_.refs_3_
  97.0 1.4 collective-permute-done.6.refs_4_.refs_5_
  98.3 5.3 %collective-permute-done.7.refs_6_.refs_7_ = bf16[128,1024]{1,0:T(8,128)(2,1)S(1)} collective-permute-done((bf16[128,1024]{1,0:T(8,128)(2,1)}, bf16[128,1024]{1,0:T(8,128)(2,1)S(1)}, u32[]{:S(2)}, u32[]{:S(2)}) %collective-permute-start.7) | collective-permute-done | bytes 262176 | tf_op jit(solution)/shard_map/ppermute | solution.py:292
  103.6 0.8 shard_map.52
  104.4 7.8 %collective-permute-start.8 = (bf16[4,16,1024]{2,1,0:T(8,128)(2,1)S(1)}, bf16[4,16,1024]{2,1,0:T(8,128)(2,1)S(1)}, u32[]{:S(2)}, u32[]{:S(2)}) collective-permute-start(bf16[4,16,1024]{2,1,0:T(8,128)(2,1)S(1)} %get-tuple-element.46), channel_id=1, source_target_pairs={{0,28},{1,29},{2,30},{3,31},{4,8},{5,9},{6,10},{7,11},{8,4},{9,5},... | collective-permute-start | bytes 393224 | tf_op jit(solution)/shard_map/ppermute | solution.py:301
  112.2 0.0 collective-permute-done.3.refs_1_
  112.2 2.9 %collective-permute-done.8.refs_3_ = bf16[4,16,1024]{2,1,0:T(8,128)(2,1)S(1)} collective-permute-done((bf16[4,16,1024]{2,1,0:T(8,128)(2,1)S(1)}, bf16[4,16,1024]{2,1,0:T(8,128)(2,1)S(1)}, u32[]{:S(2)}, u32[]{:S(2)}) %collective-permute-start.8) | collective-permute-done | bytes 131104 | tf_op jit(solution)/shard_map/ppermute | solution.py:301
  115.1 0.6 shard_map.53
  115.7 28.8 %all_to_all.20 = bf16[8,16,1024]{2,1,0:T(8,128)(2,1)S(1)} all-to-all(bf16[8,16,1024]{2,1,0:T(8,128)(2,1)S(1)} %shard_map.53), channel_id=1, replica_groups={{0,32,8,40,16,48,24,56},{4,36,12,44,20,52,28,60},{1,33,9,41,17,49,25,57..., dimensions={0} | all-to-all | bytes 524288 | tf_op jit(solution)/shard_map/all_to_all | solution.py:304
  144.6 0.7 broadcast_multiply_fusion
  (1 shorter events, 0.0 us)
Async XLA Ops:
  0.0 20.1 %collective-permute-start = (bf16[2048,128]{1,0:T(8,128)(2,1)}, bf16[2048,128]{1,0:T(8,128)(2,1)S(1)}, u32[]{:S(2)}, u32[]{:S(2)}) collective-permute-start(bf16[2048,128]{1,0:T(8,128)(2,1)} %bitcast.10), channel_id=1, source_target_pairs={{0,256},{32,288},{64,320},{96,352},{128,384},{160,416},{192,448},{... | collective-permute-start | bytes 1572872 | tf_op jit(solution)/shard_map/ppermute | solution.py:271
  3.3 1.0 copy-start.1
  5.3 20.4 %all-to-all-start = ((bf16[8,32,2048]{2,1,0:T(8,128)(2,1)}), bf16[8,32,2048]{2,1,0:T(8,128)(2,1)S(1)}, u32[]{:S(2)}, u32[]{:S(2)}) async-start(bf16[8,32,2048]{2,1,0:T(8,128)(2,1)} %shard_map.46), calls=%async_computation | async-start | bytes 2097152 | tf_op jit(solution)/shard_map/all_to_all | solution.py:276
  9.8 12.3 %collective-permute-start.1 = (bf16[2048,128]{1,0:T(8,128)(2,1)}, bf16[2048,128]{1,0:T(8,128)(2,1)S(1)}, u32[]{:S(2)}, u32[]{:S(2)}) collective-permute-start(bf16[2048,128]{1,0:T(8,128)(2,1)} %bitcast.11), channel_id=1, source_target_pairs={{0,32},{32,0},{64,96},{96,64},{128,160},{160,128},{192,224},{224,1... | collective-permute-start | bytes 1572872 | tf_op jit(solution)/shard_map/ppermute | solution.py:270
  14.1 11.7 %copy-start = (bf16[1,2048,128]{2,1,0:T(8,128)(2,1)S(1)}, bf16[1,2048,128]{2,1,0:T(8,128)(2,1)}, u32[]{:S(2)}) copy-start(bf16[1,2048,128]{2,1,0:T(8,128)(2,1)} %param.5) | copy-start | bytes 1572868
  20.1 5.7 %collective-permute-start.2 = (bf16[2048,128]{1,0:T(8,128)(2,1)S(1)}, bf16[2048,128]{1,0:T(8,128)(2,1)S(1)}, u32[]{:S(2)}, u32[]{:S(2)}) collective-permute-start(bf16[2048,128]{1,0:T(8,128)(2,1)S(1)} %collective-permute-done.refs_3_), channel_id=1, source_target_pairs={{0,32},{32,0},{64,96},{96,64},{128,160},{160,128},{192,224},{224,1... | collective-permute-start | bytes 1572872 | tf_op jit(solution)/shard_map/ppermute | solution.py:274
  28.8 31.5 %all-to-all-start.1 = ((bf16[8,256,512]{2,1,0:T(8,128)(2,1)}), bf16[8,256,512]{2,1,0:T(8,128)(2,1)S(1)}, u32[]{:S(2)}, u32[]{:S(2)}) async-start(bf16[8,256,512]{2,1,0:T(8,128)(2,1)} %shard_map.48), calls=%async_computation.1 | async-start | bytes 4194304 | tf_op jit(solution)/shard_map/all_to_all | solution.py:286
  34.5 40.0 %collective-permute-start.4 = (bf16[1024,2048]{1,0:T(8,128)(2,1)}, bf16[1024,2048]{1,0:T(8,128)(2,1)}, u32[]{:S(2)}, u32[]{:S(2)}) collective-permute-start(bf16[1024,2048]{1,0:T(8,128)(2,1)} %shard_map.47.store_ref), channel_id=1, source_target_pairs={{0,32},{32,0},{64,96},{96,64},{128,160},{160,128},{192,224},{224,1... | collective-permute-start | bytes 12582920 | tf_op jit(solution)/shard_map/ppermute | solution.py:285
  66.7 27.4 %all-to-all-start.2 = ((bf16[4,128,1024]{2,1,0:T(8,128)(2,1)}), bf16[4,128,1024]{2,1,0:T(8,128)(2,1)S(1)}, u32[]{:S(2)}, u32[]{:S(2)}) async-start(bf16[4,128,1024]{2,1,0:T(8,128)(2,1)} %shard_map.49), calls=%async_computation.2 | async-start | bytes 2097152 | tf_op jit(solution)/shard_map/all_to_all | solution.py:289
  80.7 16.2 %collective-permute-start.5 = (bf16[128,1024]{1,0:T(8,128)(2,1)}, bf16[128,1024]{1,0:T(8,128)(2,1)S(1)}, u32[]{:S(2)}, u32[]{:S(2)}) collective-permute-start(bf16[128,1024]{1,0:T(8,128)(2,1)} %get-tuple-element.38), channel_id=1, source_target_pairs={{0,1},{1,0},{2,3},{3,2},{4,5},{5,4},{6,7},{7,6},{8,9},{9,8},{10,11... | collective-permute-start | bytes 786440 | tf_op jit(solution)/shard_map/ppermute | solution.py:292
  82.7 15.6 %collective-permute-start.6 = (bf16[128,1024]{1,0:T(8,128)(2,1)}, bf16[128,1024]{1,0:T(8,128)(2,1)S(1)}, u32[]{:S(2)}, u32[]{:S(2)}) collective-permute-start(bf16[128,1024]{1,0:T(8,128)(2,1)} %get-tuple-element.39), channel_id=1, source_target_pairs={{0,30},{1,31},{2,4},{3,5},{4,2},{5,3},{6,8},{7,9},{8,6},{9,7},{10,... | collective-permute-start | bytes 786440 | tf_op jit(solution)/shard_map/ppermute | solution.py:292
  91.3 12.3 %collective-permute-start.7 = (bf16[128,1024]{1,0:T(8,128)(2,1)}, bf16[128,1024]{1,0:T(8,128)(2,1)S(1)}, u32[]{:S(2)}, u32[]{:S(2)}) collective-permute-start(bf16[128,1024]{1,0:T(8,128)(2,1)} %get-tuple-element.40), channel_id=1, source_target_pairs={{0,31},{1,30},{2,5},{3,4},{4,3},{5,2},{6,9},{7,8},{8,7},{9,6},{10,... | collective-permute-start | bytes 786440 | tf_op jit(solution)/shard_map/ppermute | solution.py:292
  95.0 17.2 %collective-permute-start.3 = (bf16[4,16,1024]{2,1,0:T(8,128)(2,1)S(1)}, bf16[4,16,1024]{2,1,0:T(8,128)(2,1)S(1)}, u32[]{:S(2)}, u32[]{:S(2)}) collective-permute-start(bf16[4,16,1024]{2,1,0:T(8,128)(2,1)S(1)} %get-tuple-element.36), channel_id=1, source_target_pairs={{0,4},{1,5},{2,6},{3,7},{4,0},{5,1},{6,2},{7,3},{8,12},{9,13},{10,... | collective-permute-start | bytes 393224 | tf_op jit(solution)/shard_map/ppermute | solution.py:298
  104.4 10.8 %collective-permute-start.8 = (bf16[4,16,1024]{2,1,0:T(8,128)(2,1)S(1)}, bf16[4,16,1024]{2,1,0:T(8,128)(2,1)S(1)}, u32[]{:S(2)}, u32[]{:S(2)}) collective-permute-start(bf16[4,16,1024]{2,1,0:T(8,128)(2,1)S(1)} %get-tuple-element.46), channel_id=1, source_target_pairs={{0,28},{1,29},{2,30},{3,31},{4,8},{5,9},{6,10},{7,11},{8,4},{9,5},... | collective-permute-start | bytes 393224 | tf_op jit(solution)/shard_map/ppermute | solution.py:301

commit v9 on v7

--- a/solution.py
+++ b/solution.py
@@ -1,5 +1,3 @@
-import functools
-
 import jax
 import jax.numpy as jnp
 from jax import lax
@@ -99,8 +97,8 @@
     )(place, grads, *columns)
 
 
-def score(apart, place_ref, parts_ref, store_ref, *refs):
-    out_refs, queries = refs[:-1], refs[-1]
+def score(place_ref, parts_ref, mine_ref, theirs_ref, out_ref, *refs):
+    apart_refs, queries = refs[:-1], refs[-1]
     block_rows, columns = parts_ref.shape[1], parts_ref.shape[2] // ROWS_X
     rows = block_rows // ROWS_Y
     tile = rows // NEAR
@@ -110,11 +108,8 @@
         for x in range(ROWS_X):
             for pair in range(ROWS_Y):
                 for near in range(NEAR):
-                    to = (x * ROWS_Y + pair) * tile
-                    if apart:
-                        to = pl.multiple_of((near ^ place_ref[1]) * (PAIRS * tile) + to, tile)
-                    else:
-                        to += near * PAIRS * tile
+                    to = (near ^ place_ref[1]) * (PAIRS * tile) + (x * ROWS_Y + pair) * tile
+                    to = pl.multiple_of(to, tile)
                     row = pair * rows + near * tile
                     for y in range(ROWS_Y):
                         for k in range(ROWS_X):
@@ -123,48 +118,49 @@
                                 x * ROWS_Y + y, row : row + tile, k * columns : (k + 1) * columns
                             ]
 
-    term = lax.dot_general(
-        queries[...], store_ref[...], (((1,), (1,)), ((), ())),
-        preferred_element_type=jnp.float32,
-    )
-    for k in range(NEAR):
-        entries = term[k * PAIRS * tile : (k + 1) * PAIRS * tile].astype(out_refs[0].dtype)
-        if apart:
-            out_refs[k][...] = entries
-        else:
-            out_refs[0][k] = entries
-
-
-def scores_of(apart, place, parts, store):
+    def times(store_ref):
+        term = lax.dot_general(
+            queries[...], store_ref[...], (((1,), (1,)), ((), ())),
+            preferred_element_type=jnp.float32,
+        ).astype(out_ref.dtype)
+        return [term[k * PAIRS * tile : (k + 1) * PAIRS * tile] for k in range(NEAR)]
+
+    for k, entries in enumerate(times(mine_ref)):
+        out_ref[k ^ place_ref[1]] = entries
+    for ref, entries in zip(apart_refs, times(theirs_ref), strict=True):
+        ref[...] = entries
+
+
+def scores_of(place, parts, mine, theirs):
     chips, block_rows, columns = parts.shape
     rows = ROWS_X * block_rows
-    examples, width = store.shape
+    examples, width = mine.shape
     tile = 256
-    if apart:
-        block, index, shape, count = (rows // NEAR, tile), lambda n, place_ref: (0, n), (rows // NEAR, examples), NEAR
-    else:
-        block, index = (NEAR, rows // NEAR, tile), lambda n, place_ref: (0, 0, n)
-        shape, count = (NEAR, rows // NEAR, examples), 1
-    return pl.pallas_call(
-        functools.partial(score, apart),
+    shape = (NEAR, rows // NEAR, examples)
+    store_spec = pl.BlockSpec((tile, width), lambda n, place_ref: (n, 0))
+    return pl.pallas_call(
+        score,
         grid_spec=pltpu.PrefetchScalarGridSpec(
             num_scalar_prefetch=1,
             grid=(examples // tile,),
             in_specs=[
                 pl.BlockSpec((chips, block_rows, columns), lambda n, place_ref: (0, 0, 0)),
-                pl.BlockSpec((tile, width), lambda n, place_ref: (n, 0)),
+                store_spec,
+                store_spec,
             ],
-            out_specs=[pl.BlockSpec(block, index)] * count,
+            out_specs=[pl.BlockSpec((NEAR, rows // NEAR, tile), lambda n, place_ref: (0, 0, n))]
+            + [pl.BlockSpec((rows // NEAR, tile), lambda n, place_ref: (0, n))] * NEAR,
             scratch_shapes=[pltpu.VMEM((rows, width), jnp.bfloat16)],
         ),
-        out_shape=[jax.ShapeDtypeStruct(shape, jnp.bfloat16) if apart else pltpu.HBM(shape, jnp.bfloat16)] * count,
-        compiler_params=pltpu.CompilerParams(vmem_limit_bytes=50 * MIB),
-        cost_estimate=pl.CostEstimate(
-            flops=2 * rows * width * examples,
-            bytes_accessed=2 * (rows * width + (width + rows) * examples),
+        out_shape=[pltpu.HBM(shape, jnp.bfloat16)]
+        + [jax.ShapeDtypeStruct(shape[1:], jnp.bfloat16)] * NEAR,
+        compiler_params=pltpu.CompilerParams(vmem_limit_bytes=32 * MIB),
+        cost_estimate=pl.CostEstimate(
+            flops=2 * CORES * rows * width * examples,
+            bytes_accessed=2 * (rows * width + CORES * (width + rows) * examples),
             transcendentals=0,
         ),
-    )(place, parts, store)
+    )(place, parts, mine, theirs)
 
 
 def add(place_ref, gathered_ref, *refs):
@@ -252,9 +248,8 @@
     theirs = lax.ppermute(mine, "ex", shift(0, 0, 1))
     parts = lax.all_to_all(copies, "ex", 0, 0, tiled=True, axis_index_groups=same_core)
 
-    (terms,) = scores_of(False, place, parts, mine)
+    terms, here, *away = scores_of(place, parts, mine, theirs)
     gathered = lax.all_to_all(terms, "dim", 0, 0, tiled=True, axis_index_groups=near)
-    here, *away = scores_of(True, place, parts, theirs)
     others = [here] + [
         lax.ppermute(
             term, "dim", [(d, (((d + SIDES) ^ k) - SIDES) % slots if k & SIDES else d ^ k) for d in range(slots)]

time: 146 us -> 146 us (level)
  blocking collectives: 41.4 us -> 76.6 us
  waiting for transfers between devices: 34.8 us -> 11.1 us
  Pallas kernels: 22.9 us -> 16.4 us
  starting transfers between devices: 41.3 us -> 36.5 us
    all_to_all x0 -> x1, blocking collectives: none -> 32.2 us  [shards(): lax.all_to_all(copies, 'ex', 0, 0, tiled=True, axis_index_groups=same_core)]
    all_to_all x1 -> x0, waiting for transfers between devices: 23.9 us -> none  [shards(): lax.all_to_all(copies, 'ex', 0, 0, tiled=True, axis_index_groups=same_core)]
    all_to_all x1 -> x0, starting transfers between devices: 5.96 us -> none  [shards(): lax.all_to_all(copies, 'ex', 0, 0, tiled=True, axis_index_groups=same_core)]
    pallas_call x2 -> x1, Pallas kernels: 11.9 us -> 6.73 us  [scores_of(): pl.pallas_call(score, grid_spec=pltpu.PrefetchScalarGridSpec(num_scalar_p...]
    all_to_all x1, blocking collectives: 41.4 us -> 44.5 us  [shards(): lax.all_to_all(added(place, tile, gathered, others), ('ex', 'dim'), 0, 0,...]
    unnamed x5 -> x7, local copies, waits for them, and re-layouts: 2.83 us -> 3.32 us
  transfers between devices with their start and end apart: 10 -> 9, of which waited for: 5 -> 3; matrix products, arithmetic and copies ran while one was open for 1% -> 1% of each run, Pallas kernels for 13% -> 5%
where the time goes in v9:
time: 146 us; the launch traced here: 145 us
  blocking collectives  76.6 us (52%)
  starting transfers between devices  36.5 us (25%)
  Pallas kernels  16.4 us (11%)
  waiting for transfers between devices  11.1 us (8%)
  local copies, waits for them, and re-layouts  3.32 us (2%)
    all_to_all x1, blocking collectives, shards(): lax.all_to_all(added(place, tile, gathered, others), ('ex', 'dim'), 0, 0,...  44.5 us
    all_to_all x1, blocking collectives, shards(): lax.all_to_all(copies, 'ex', 0, 0, tiled=True, axis_index_groups=same_core)  32.2 us
    ppermute x3, starting transfers between devices, shards(): lax.ppermute(term, 'dim', [(d, ((d + SIDES ^ k) - SIDES) % slots if k & S...  13.6 us
    ppermute x3, waiting for transfers between devices, shards(): lax.ppermute(term, 'dim', [(d, ((d + SIDES ^ k) - SIDES) % slots if k & S...  8.24 us
    all_to_all x1, starting transfers between devices, shards(): lax.all_to_all(halves, 'ex', 0, 0, tiled=True, axis_index_groups=beside)  6.78 us
    pallas_call x1, Pallas kernels, scores_of(): pl.pallas_call(score, grid_spec=pltpu.PrefetchScalarGridSpec(num_scalar_p...  6.73 us
    pallas_call x1, Pallas kernels, dequantized(): pl.pallas_call(dequantize, grid=(rows // tile,), in_specs=[pl.BlockSpec((...  5.99 us
    ppermute x1, starting transfers between devices, shards(): across = lax.ppermute(own, 'ex', shift(1, 0, 0))  5.47 us
  transfers between devices with their start and end apart: 9, of which 3 were waited for; matrix products, arithmetic and copies ran while one was open for 1% of the time, Pallas kernels for 5%

profile of v9, /device:TPU:1, one launch (start us, length us, event | category | flops | bytes accessed | tf_op | source)
XLA Modules:
  0.0 144.8 jit_solution(4016366261448659244)
XLA Ops:
  0.0 5.5 %collective-permute-start = (bf16[2048,128]{1,0:T(8,128)(2,1)}, bf16[2048,128]{1,0:T(8,128)(2,1)S(1)}, u32[]{:S(2)}, u32[]{:S(2)}) collective-permute-start(bf16[2048,128]{1,0:T(8,128)(2,1)} %bitcast.9), channel_id=1, source_target_pairs={{0,256},{32,288},{64,320},{96,352},{128,384},{160,416},{192,448},{... | collective-permute-start | bytes 1572872 | tf_op jit(solution)/shard_map/ppermute | solution.py:234
  5.5 0.0 copy-start.2
  5.5 0.9 copy-done.2
  6.4 1.0 shard_map.46
  7.5 6.8 %all-to-all-start = ((bf16[8,32,2048]{2,1,0:T(8,128)(2,1)}), bf16[8,32,2048]{2,1,0:T(8,128)(2,1)S(1)}, u32[]{:S(2)}, u32[]{:S(2)}) async-start(bf16[8,32,2048]{2,1,0:T(8,128)(2,1)} %shard_map.46), calls=%async_computation | async-start | bytes 2097152 | tf_op jit(solution)/shard_map/all_to_all | solution.py:239
  14.2 2.0 %collective-permute-start.1 = (bf16[2048,128]{1,0:T(8,128)(2,1)}, bf16[2048,128]{1,0:T(8,128)(2,1)S(1)}, u32[]{:S(2)}, u32[]{:S(2)}) collective-permute-start(bf16[2048,128]{1,0:T(8,128)(2,1)} %bitcast.10), channel_id=1, source_target_pairs={{0,32},{32,0},{64,96},{96,64},{128,160},{160,128},{192,224},{224,1... | collective-permute-start | bytes 1572872 | tf_op jit(solution)/shard_map/ppermute | solution.py:233
  16.3 1.9 %copy.5.scales_ref = f32[1024,16]{1,0:T(8,128)} copy(f32[1024,16]{0,1:T(8,128)} %param.7) | data formatting | bytes 131072 | tf_op args[3]
  18.2 0.0 copy-start.1
  18.2 6.0 %shard_map.47.mine_ref = bf16[1024,2048]{1,0:T(8,128)(2,1)} custom-call(bf16[1024,2048]{1,0:T(8,128)(2,1)} %codes_ref.1, f32[1024,16]{1,0:T(8,128)} %copy.5.scales_ref), custom_call_target="tpu_custom_call" | custom-call | flops 2097152 | bytes 8388608 | tf_op jit(solution)/shard_map/pallas_call | solution.py:25
  24.1 0.0 collective-permute-done.refs_3_
  24.1 2.3 %collective-permute-start.2 = (bf16[2048,128]{1,0:T(8,128)(2,1)S(1)}, bf16[2048,128]{1,0:T(8,128)(2,1)S(1)}, u32[]{:S(2)}, u32[]{:S(2)}) collective-permute-start(bf16[2048,128]{1,0:T(8,128)(2,1)S(1)} %collective-permute-done.refs_3_), channel_id=1, source_target_pairs={{0,32},{32,0},{64,96},{96,64},{128,160},{160,128},{192,224},{224,1... | collective-permute-start | bytes 1572872 | tf_op jit(solution)/shard_map/ppermute | solution.py:237
  26.5 0.1 pad_add_fusion.place_ref
  26.5 0.0 collective-permute-done.1.refs_2_
  26.5 2.8 %all-to-all-done = bf16[8,32,2048]{2,1,0:T(8,128)(2,1)S(1)} async-done(((bf16[8,32,2048]{2,1,0:T(8,128)(2,1)}), bf16[8,32,2048]{2,1,0:T(8,128)(2,1)S(1)}, u32[]{:S(2)}, u32[]{:S(2)}) %all-to-all-start) | async-done | bytes 1048608 | tf_op jit(solution)/shard_map/all_to_all | solution.py:239
  29.4 0.0 copy-start
  29.4 0.0 collective-permute-done.2.refs_4_
  29.4 0.0 copy-done.1
  29.4 1.7 %shard_map.48 = bf16[8,256,512]{2,1,0:T(8,128)(2,1)S(1)} custom-call(s32[2]{0:T(128)S(1)} %pad_add_fusion.place_ref, bf16[256,2048]{1,0:T(8,128)(2,1)S(1)} %bitcast.8, bf16[2048,128]{1,0:T(8,128)(2,1)S(1)} %bitcast.11, bf16[2048,128]{1,0:T(8,128)(2,1)S(1)} %collective-permute-done.1.refs_2_, bf16[2048,128]{1,0:T(8,128)(2,1)S(1)} %collective-permute-done.refs_3_, ...), custom_call_target="tpu_custom_call" | custom-call | flops 536870912 | bytes 5242880 | tf_op jit(solution)/shard_map/pallas_call | solution.py:84
  31.1 0.5 copy-done
  31.5 2.8 %collective-permute-start.3 = (bf16[1024,2048]{1,0:T(8,128)(2,1)S(1)}, bf16[1024,2048]{1,0:T(8,128)(2,1)S(1)}, u32[]{:S(2)}, u32[]{:S(2)}) collective-permute-start(bf16[1024,2048]{1,0:T(8,128)(2,1)S(1)} %copy-done), channel_id=1, source_target_pairs={{0,32},{32,0},{64,96},{96,64},{128,160},{160,128},{192,224},{224,1... | collective-permute-start | bytes 12582920 | tf_op jit(solution)/shard_map/ppermute | solution.py:248
  34.3 32.2 %all_to_all.20.parts_ref = bf16[8,256,512]{2,1,0:T(8,128)(2,1)S(1)} all-to-all(bf16[8,256,512]{2,1,0:T(8,128)(2,1)S(1)} %shard_map.48), channel_id=1, replica_groups={{0,64,128,192,256,320,384,448},{32,96,160,224,288,352,416,480},{1,65,12..., dimensions={0} | all-to-all | bytes 4194304 | tf_op jit(solution)/shard_map/all_to_all | solution.py:249
  66.5 0.0 collective-permute-done.3.theirs_ref
  66.5 6.7 %shard_map.49 = (bf16[4,128,1024]{2,1,0:T(8,128)(2,1)}, bf16[128,1024]{1,0:T(8,128)(2,1)S(1)}, bf16[128,1024]{1,0:T(8,128)(2,1)S(1)}, bf16[128,1024]{1,0:T(8,128)(2,1)S(1)}, bf16[128,1024]{1,0:T(8,128)(2,1)S(1)}) custom-call(s32[2]{0:T(128)S(1)} %pad_add_fusion.place_ref, bf16[8,256,512]{2,1,0:T(8,128)(2,1)S(1)} %all_to_all.20.parts_ref, ...), custom_call_target="tpu_custom_call" | custom-call | flops 4294967296 | bytes 12582912 | tf_op jit(solution)/shard_map/pallas_call | solution.py:141
  73.2 3.5 %all-to-all-start.2 = ((bf16[4,128,1024]{2,1,0:T(8,128)(2,1)}), bf16[4,128,1024]{2,1,0:T(8,128)(2,1)S(1)}, u32[]{:S(2)}, u32[]{:S(2)}) async-start(bf16[4,128,1024]{2,1,0:T(8,128)(2,1)} %get-tuple-element.28), calls=%async_computation.2 | async-start | bytes 2097152 | tf_op jit(solution)/shard_map/all_to_all | solution.py:252
  76.8 3.3 %collective-permute-start.4 = (bf16[128,1024]{1,0:T(8,128)(2,1)S(1)}, bf16[128,1024]{1,0:T(8,128)(2,1)S(1)}, u32[]{:S(2)}, u32[]{:S(2)}) collective-permute-start(bf16[128,1024]{1,0:T(8,128)(2,1)S(1)} %get-tuple-element.30), channel_id=1, source_target_pairs={{0,1},{1,0},{2,3},{3,2},{4,5},{5,4},{6,7},{7,6},{8,9},{9,8},{10,11... | collective-permute-start | bytes 786440 | tf_op jit(solution)/shard_map/ppermute | solution.py:254
  80.1 8.4 %collective-permute-start.5 = (bf16[128,1024]{1,0:T(8,128)(2,1)S(1)}, bf16[128,1024]{1,0:T(8,128)(2,1)S(1)}, u32[]{:S(2)}, u32[]{:S(2)}) collective-permute-start(bf16[128,1024]{1,0:T(8,128)(2,1)S(1)} %get-tuple-element.31), channel_id=1, source_target_pairs={{0,30},{1,31},{2,4},{3,5},{4,2},{5,3},{6,8},{7,9},{8,6},{9,7},{10,... | collective-permute-start | bytes 786440 | tf_op jit(solution)/shard_map/ppermute | solution.py:254
  88.5 1.9 %collective-permute-start.6 = (bf16[128,1024]{1,0:T(8,128)(2,1)S(1)}, bf16[128,1024]{1,0:T(8,128)(2,1)S(1)}, u32[]{:S(2)}, u32[]{:S(2)}) collective-permute-start(bf16[128,1024]{1,0:T(8,128)(2,1)S(1)} %get-tuple-element.32), channel_id=1, source_target_pairs={{0,31},{1,30},{2,5},{3,4},{4,3},{5,2},{6,9},{7,8},{8,7},{9,6},{10,... | collective-permute-start | bytes 786440 | tf_op jit(solution)/shard_map/ppermute | solution.py:254
  90.4 5.1 %collective-permute-done.4.refs_1_ = bf16[128,1024]{1,0:T(8,128)(2,1)S(1)} collective-permute-done((bf16[128,1024]{1,0:T(8,128)(2,1)S(1)}, bf16[128,1024]{1,0:T(8,128)(2,1)S(1)}, u32[]{:S(2)}, u32[]{:S(2)}) %collective-permute-start.4) | collective-permute-done | bytes 262176 | tf_op jit(solution)/shard_map/ppermute | solution.py:254
  95.5 0.0 collective-permute-done.5.refs_2_
  95.5 3.1 %collective-permute-done.6.refs_3_ = bf16[128,1024]{1,0:T(8,128)(2,1)S(1)} collective-permute-done((bf16[128,1024]{1,0:T(8,128)(2,1)S(1)}, bf16[128,1024]{1,0:T(8,128)(2,1)S(1)}, u32[]{:S(2)}, u32[]{:S(2)}) %collective-permute-start.6) | collective-permute-done | bytes 262176 | tf_op jit(solution)/shard_map/ppermute | solution.py:254
  98.6 0.0 all-to-all-done.2.gathered_ref
  98.6 1.0 shard_map.50
  99.6 44.5 %all_to_all.21 = bf16[16,16,1024]{2,1,0:T(8,128)(2,1)S(1)} all-to-all(bf16[16,16,1024]{2,1,0:T(8,128)(2,1)S(1)} %shard_map.50), channel_id=1, replica_groups={{0,32,4,36,8,40,12,44,16,48,20,52,24,56,28,60},{1,33,5,37,9,41,13,45,17..., dimensions={0} | all-to-all | bytes 1048576 | tf_op jit(solution)/shard_map/all_to_all | solution.py:259
  144.1 0.1 convert_reduce_fusion
  144.2 0.7 broadcast_multiply_fusion
Async XLA Ops:
  0.0 24.1 %collective-permute-start = (bf16[2048,128]{1,0:T(8,128)(2,1)}, bf16[2048,128]{1,0:T(8,128)(2,1)S(1)}, u32[]{:S(2)}, u32[]{:S(2)}) collective-permute-start(bf16[2048,128]{1,0:T(8,128)(2,1)} %bitcast.9), channel_id=1, source_target_pairs={{0,256},{32,288},{64,320},{96,352},{128,384},{160,416},{192,448},{... | collective-permute-start | bytes 1572872 | tf_op jit(solution)/shard_map/ppermute | solution.py:234
  5.5 1.0 copy-start.2
  7.5 21.9 %all-to-all-start = ((bf16[8,32,2048]{2,1,0:T(8,128)(2,1)}), bf16[8,32,2048]{2,1,0:T(8,128)(2,1)S(1)}, u32[]{:S(2)}, u32[]{:S(2)}) async-start(bf16[8,32,2048]{2,1,0:T(8,128)(2,1)} %shard_map.46), calls=%async_computation | async-start | bytes 2097152 | tf_op jit(solution)/shard_map/all_to_all | solution.py:239
  14.2 12.3 %collective-permute-start.1 = (bf16[2048,128]{1,0:T(8,128)(2,1)}, bf16[2048,128]{1,0:T(8,128)(2,1)S(1)}, u32[]{:S(2)}, u32[]{:S(2)}) collective-permute-start(bf16[2048,128]{1,0:T(8,128)(2,1)} %bitcast.10), channel_id=1, source_target_pairs={{0,32},{32,0},{64,96},{96,64},{128,160},{160,128},{192,224},{224,1... | collective-permute-start | bytes 1572872 | tf_op jit(solution)/shard_map/ppermute | solution.py:233
  18.2 11.2 %copy-start.1 = (bf16[1,2048,128]{2,1,0:T(8,128)(2,1)S(1)}, bf16[1,2048,128]{2,1,0:T(8,128)(2,1)}, u32[]{:S(2)}) copy-start(bf16[1,2048,128]{2,1,0:T(8,128)(2,1)} %param.5) | copy-start | bytes 1572868
  24.1 5.2 %collective-permute-start.2 = (bf16[2048,128]{1,0:T(8,128)(2,1)S(1)}, bf16[2048,128]{1,0:T(8,128)(2,1)S(1)}, u32[]{:S(2)}, u32[]{:S(2)}) collective-permute-start(bf16[2048,128]{1,0:T(8,128)(2,1)S(1)} %collective-permute-done.refs_3_), channel_id=1, source_target_pairs={{0,32},{32,0},{64,96},{96,64},{128,160},{160,128},{192,224},{224,1... | collective-permute-start | bytes 1572872 | tf_op jit(solution)/shard_map/ppermute | solution.py:237
  29.4 2.2 %copy-start = (bf16[1024,2048]{1,0:T(8,128)(2,1)S(1)}, bf16[1024,2048]{1,0:T(8,128)(2,1)}, u32[]{:S(2)}) copy-start(bf16[1024,2048]{1,0:T(8,128)(2,1)} %shard_map.47.mine_ref) | copy-start | bytes 12582916
  31.5 34.9 %collective-permute-start.3 = (bf16[1024,2048]{1,0:T(8,128)(2,1)S(1)}, bf16[1024,2048]{1,0:T(8,128)(2,1)S(1)}, u32[]{:S(2)}, u32[]{:S(2)}) collective-permute-start(bf16[1024,2048]{1,0:T(8,128)(2,1)S(1)} %copy-done), channel_id=1, source_target_pairs={{0,32},{32,0},{64,96},{96,64},{128,160},{160,128},{192,224},{224,1... | collective-permute-start | bytes 12582920 | tf_op jit(solution)/shard_map/ppermute | solution.py:248
  73.2 25.4 %all-to-all-start.2 = ((bf16[4,128,1024]{2,1,0:T(8,128)(2,1)}), bf16[4,128,1024]{2,1,0:T(8,128)(2,1)S(1)}, u32[]{:S(2)}, u32[]{:S(2)}) async-start(bf16[4,128,1024]{2,1,0:T(8,128)(2,1)} %get-tuple-element.28), calls=%async_computation.2 | async-start | bytes 2097152 | tf_op jit(solution)/shard_map/all_to_all | solution.py:252
  76.8 18.7 %collective-permute-start.4 = (bf16[128,1024]{1,0:T(8,128)(2,1)S(1)}, bf16[128,1024]{1,0:T(8,128)(2,1)S(1)}, u32[]{:S(2)}, u32[]{:S(2)}) collective-permute-start(bf16[128,1024]{1,0:T(8,128)(2,1)S(1)} %get-tuple-element.30), channel_id=1, source_target_pairs={{0,1},{1,0},{2,3},{3,2},{4,5},{5,4},{6,7},{7,6},{8,9},{9,8},{10,11... | collective-permute-start | bytes 786440 | tf_op jit(solution)/shard_map/ppermute | solution.py:254
  80.1 15.4 %collective-permute-start.5 = (bf16[128,1024]{1,0:T(8,128)(2,1)S(1)}, bf16[128,1024]{1,0:T(8,128)(2,1)S(1)}, u32[]{:S(2)}, u32[]{:S(2)}) collective-permute-start(bf16[128,1024]{1,0:T(8,128)(2,1)S(1)} %get-tuple-element.31), channel_id=1, source_target_pairs={{0,30},{1,31},{2,4},{3,5},{4,2},{5,3},{6,8},{7,9},{8,6},{9,7},{10,... | collective-permute-start | bytes 786440 | tf_op jit(solution)/shard_map/ppermute | solution.py:254
  88.5 10.2 %collective-permute-start.6 = (bf16[128,1024]{1,0:T(8,128)(2,1)S(1)}, bf16[128,1024]{1,0:T(8,128)(2,1)S(1)}, u32[]{:S(2)}, u32[]{:S(2)}) collective-permute-start(bf16[128,1024]{1,0:T(8,128)(2,1)S(1)} %get-tuple-element.32), channel_id=1, source_target_pairs={{0,31},{1,30},{2,5},{3,4},{4,3},{5,2},{6,9},{7,8},{8,7},{9,6},{10,... | collective-permute-start | bytes 786440 | tf_op jit(solution)/shard_map/ppermute | solution.py:254

commit v10 on v9

--- a/solution.py
+++ b/solution.py
@@ -127,8 +127,8 @@
 
     for k, entries in enumerate(times(mine_ref)):
         out_ref[k ^ place_ref[1]] = entries
-    for ref, entries in zip(apart_refs, times(theirs_ref), strict=True):
-        ref[...] = entries
+    for k, entries in enumerate(times(theirs_ref)):
+        apart_refs[k // SIDES][k % SIDES] = entries
 
 
 def scores_of(place, parts, mine, theirs):
@@ -149,11 +149,11 @@
                 store_spec,
             ],
             out_specs=[pl.BlockSpec((NEAR, rows // NEAR, tile), lambda n, place_ref: (0, 0, n))]
-            + [pl.BlockSpec((rows // NEAR, tile), lambda n, place_ref: (0, n))] * NEAR,
+            + [pl.BlockSpec((SIDES, rows // NEAR, tile), lambda n, place_ref: (0, 0, n))] * 2,
             scratch_shapes=[pltpu.VMEM((rows, width), jnp.bfloat16)],
         ),
         out_shape=[pltpu.HBM(shape, jnp.bfloat16)]
-        + [jax.ShapeDtypeStruct(shape[1:], jnp.bfloat16)] * NEAR,
+        + [jax.ShapeDtypeStruct((SIDES,) + shape[1:], jnp.bfloat16)] * 2,
         compiler_params=pltpu.CompilerParams(vmem_limit_bytes=32 * MIB),
         cost_estimate=pl.CostEstimate(
             flops=2 * CORES * rows * width * examples,
@@ -161,6 +161,28 @@
             transcendentals=0,
         ),
     )(place, parts, mine, theirs)
+
+
+def fold(here_ref, came_ref, kept_ref, sent_ref):
+    kept_ref[...] = here_ref[0].astype(jnp.float32) + came_ref[0].astype(jnp.float32)
+    sent_ref[...] = (here_ref[1].astype(jnp.float32) + came_ref[1].astype(jnp.float32)).astype(sent_ref.dtype)
+
+
+def folded(here, came):
+    steps = 4
+    sides, rows, examples = here.shape
+    block = pl.BlockSpec((sides, rows // steps, examples), lambda s: (0, s, 0))
+    return pl.pallas_call(
+        fold,
+        grid=(steps,),
+        in_specs=[block, block],
+        out_specs=[pl.BlockSpec((rows // steps, examples), lambda s: (s, 0))] * 2,
+        out_shape=[jax.ShapeDtypeStruct((rows, examples), dtype) for dtype in (jnp.float32, jnp.bfloat16)],
+        compiler_params=pltpu.CompilerParams(vmem_limit_bytes=16 * MIB),
+        cost_estimate=pl.CostEstimate(
+            flops=2 * rows * examples, bytes_accessed=14 * rows * examples, transcendentals=0
+        ),
+    )(here, came)
 
 
 def add(place_ref, gathered_ref, *refs):
@@ -168,10 +190,9 @@
     tile = out_ref.shape[1]
     sums = gathered_ref[0].astype(jnp.float32), other_refs[0][...].astype(jnp.float32)
     for k in range(1, NEAR):
-        sums = (
-            sums[0] + gathered_ref[k].astype(jnp.float32),
-            sums[1] + other_refs[k][...].astype(jnp.float32),
-        )
+        sums = sums[0] + gathered_ref[k].astype(jnp.float32), sums[1]
+    for ref in other_refs[1:]:
+        sums = sums[0], sums[1] + ref[...].astype(jnp.float32)
     for i, total in enumerate(sums):
         for p in range(out_ref.shape[0] // CORES):
             at = p * CORES + (place_ref[0] ^ i)
@@ -187,7 +208,7 @@
             num_scalar_prefetch=1,
             grid=(steps,),
             in_specs=[pl.BlockSpec((NEAR, rows // steps, examples), lambda s, place_ref: (0, s, 0))]
-            + [pl.BlockSpec((rows // steps, examples), lambda s, place_ref: (s, 0))] * NEAR,
+            + [pl.BlockSpec((rows // steps, examples), lambda s, place_ref: (s, 0))] * len(others),
             out_specs=pl.BlockSpec(
                 (PAIRS * CORES // steps, tile, examples), lambda s, place_ref: (s, 0, 0)
             ),
@@ -248,14 +269,13 @@
     theirs = lax.ppermute(mine, "ex", shift(0, 0, 1))
     parts = lax.all_to_all(copies, "ex", 0, 0, tiled=True, axis_index_groups=same_core)
 
-    terms, here, *away = scores_of(place, parts, mine, theirs)
+    terms, here, away = scores_of(place, parts, mine, theirs)
     gathered = lax.all_to_all(terms, "dim", 0, 0, tiled=True, axis_index_groups=near)
-    others = [here] + [
-        lax.ppermute(
-            term, "dim", [(d, (((d + SIDES) ^ k) - SIDES) % slots if k & SIDES else d ^ k) for d in range(slots)]
-        )
-        for k, term in enumerate(away, 1)
-    ]
+    came = lax.ppermute(
+        away, "dim", [(d, (((d + SIDES) ^ SIDES) - SIDES) % slots) for d in range(slots)]
+    )
+    kept, sent = folded(here, came)
+    others = [kept, lax.ppermute(sent, "dim", [(d, d ^ 1) for d in range(slots)])]
     sums = lax.all_to_all(
         added(place, tile, gathered, others), ("ex", "dim"), 0, 0, tiled=True, axis_index_groups=far
     )

time: 146 us -> 149 us (1.021)
  waiting for transfers between devices: 11.1 us -> 18.1 us
  starting transfers between devices: 36.5 us -> 34.5 us
  blocking collectives: 76.6 us -> 75 us
    ppermute x3 -> x2, waiting for transfers between devices: 8.24 us -> 15.3 us  [the longest x1 10.8 us: shards(): lax.ppermute(away, 'dim', [(d, ((d + SIDES ^ SIDES) - SIDES) % slots) for...]
    ppermute x3 -> x2, starting transfers between devices: 13.6 us -> 11.7 us  [the longest x1 8.6 us: shards(): lax.ppermute(away, 'dim', [(d, ((d + SIDES ^ SIDES) - SIDES) % slots) for...]
    all_to_all x1, blocking collectives: 44.5 us -> 42.9 us  [shards(): lax.all_to_all(added(place, tile, gathered, others), ('ex', 'dim'), 0, 0,...]
  transfers between devices with their start and end apart: 9 -> 8, of which waited for: 3 -> 3; matrix products, arithmetic and copies ran while one was open for 1% -> 1% of each run, Pallas kernels for 5% -> 5%
where the time goes in v10:
time: 149 us
  blocking collectives  75 us (50%)
  starting transfers between devices  34.5 us (23%)
  waiting for transfers between devices  18.1 us (12%)
  Pallas kernels  16.6 us (11%)
  local copies, waits for them, and re-layouts  3.32 us (2%)
    all_to_all x1, blocking collectives, shards(): lax.all_to_all(added(place, tile, gathered, others), ('ex', 'dim'), 0, 0,...  42.9 us
    all_to_all x1, blocking collectives, shards(): lax.all_to_all(copies, 'ex', 0, 0, tiled=True, axis_index_groups=same_core)  32.2 us
    ppermute x1, waiting for transfers between devices, shards(): lax.ppermute(away, 'dim', [(d, ((d + SIDES ^ SIDES) - SIDES) % slots) for...  10.8 us
    ppermute x1, starting transfers between devices, shards(): lax.ppermute(away, 'dim', [(d, ((d + SIDES ^ SIDES) - SIDES) % slots) for...  8.6 us
    all_to_all x1, starting transfers between devices, shards(): lax.all_to_all(halves, 'ex', 0, 0, tiled=True, axis_index_groups=beside)  6.78 us
    pallas_call x1, Pallas kernels, scores_of(): pl.pallas_call(score, grid_spec=pltpu.PrefetchScalarGridSpec(num_scalar_p...  6.7 us
    pallas_call x1, Pallas kernels, dequantized(): pl.pallas_call(dequantize, grid=(rows // tile,), in_specs=[pl.BlockSpec((...  5.99 us
    ppermute x1, starting transfers between devices, shards(): across = lax.ppermute(own, 'ex', shift(1, 0, 0))  5.47 us
  transfers between devices with their start and end apart: 8, of which 3 were waited for; matrix products, arithmetic and copies ran while one was open for 1% of the time, Pallas kernels for 5%

profile of v10, /device:TPU:1, one launch (start us, length us, event | category | flops | bytes accessed | tf_op | source)
XLA Modules:
  0.0 148.6 jit_solution(4509006036952501290)
XLA Ops:
  0.0 5.5 %collective-permute-start = (bf16[2048,128]{1,0:T(8,128)(2,1)}, bf16[2048,128]{1,0:T(8,128)(2,1)S(1)}, u32[]{:S(2)}, u32[]{:S(2)}) collective-permute-start(bf16[2048,128]{1,0:T(8,128)(2,1)} %bitcast.9), channel_id=1, source_target_pairs={{0,256},{32,288},{64,320},{96,352},{128,384},{160,416},{192,448},{... | collective-permute-start | bytes 1572872 | tf_op jit(solution)/shard_map/ppermute | solution.py:255
  5.5 0.0 copy-start.2
  5.5 0.9 copy-done.2
  6.4 1.0 shard_map.46
  7.5 6.8 %all-to-all-start = ((bf16[8,32,2048]{2,1,0:T(8,128)(2,1)}), bf16[8,32,2048]{2,1,0:T(8,128)(2,1)S(1)}, u32[]{:S(2)}, u32[]{:S(2)}) async-start(bf16[8,32,2048]{2,1,0:T(8,128)(2,1)} %shard_map.46), calls=%async_computation | async-start | bytes 2097152 | tf_op jit(solution)/shard_map/all_to_all | solution.py:260
  14.2 2.0 %collective-permute-start.1 = (bf16[2048,128]{1,0:T(8,128)(2,1)}, bf16[2048,128]{1,0:T(8,128)(2,1)S(1)}, u32[]{:S(2)}, u32[]{:S(2)}) collective-permute-start(bf16[2048,128]{1,0:T(8,128)(2,1)} %bitcast.10), channel_id=1, source_target_pairs={{0,32},{32,0},{64,96},{96,64},{128,160},{160,128},{192,224},{224,1... | collective-permute-start | bytes 1572872 | tf_op jit(solution)/shard_map/ppermute | solution.py:254
  16.3 1.9 %copy.5.scales_ref = f32[1024,16]{1,0:T(8,128)} copy(f32[1024,16]{0,1:T(8,128)} %param.7) | data formatting | bytes 131072 | tf_op args[3]
  18.2 0.0 copy-start.1
  18.2 6.0 %shard_map.47.mine_ref = bf16[1024,2048]{1,0:T(8,128)(2,1)} custom-call(bf16[1024,2048]{1,0:T(8,128)(2,1)} %codes_ref.1, f32[1024,16]{1,0:T(8,128)} %copy.5.scales_ref), custom_call_target="tpu_custom_call" | custom-call | flops 2097152 | bytes 8388608 | tf_op jit(solution)/shard_map/pallas_call | solution.py:25
  24.1 0.0 collective-permute-done.refs_3_
  24.1 2.3 %collective-permute-start.2 = (bf16[2048,128]{1,0:T(8,128)(2,1)S(1)}, bf16[2048,128]{1,0:T(8,128)(2,1)S(1)}, u32[]{:S(2)}, u32[]{:S(2)}) collective-permute-start(bf16[2048,128]{1,0:T(8,128)(2,1)S(1)} %collective-permute-done.refs_3_), channel_id=1, source_target_pairs={{0,32},{32,0},{64,96},{96,64},{128,160},{160,128},{192,224},{224,1... | collective-permute-start | bytes 1572872 | tf_op jit(solution)/shard_map/ppermute | solution.py:258
  26.5 0.1 pad_add_fusion.place_ref
  26.5 0.0 collective-permute-done.1.refs_2_
  26.5 2.8 %all-to-all-done = bf16[8,32,2048]{2,1,0:T(8,128)(2,1)S(1)} async-done(((bf16[8,32,2048]{2,1,0:T(8,128)(2,1)}), bf16[8,32,2048]{2,1,0:T(8,128)(2,1)S(1)}, u32[]{:S(2)}, u32[]{:S(2)}) %all-to-all-start) | async-done | bytes 1048608 | tf_op jit(solution)/shard_map/all_to_all | solution.py:260
  29.4 0.0 copy-start
  29.4 0.0 collective-permute-done.2.refs_4_
  29.4 0.0 copy-done.1
  29.4 1.7 %shard_map.48 = bf16[8,256,512]{2,1,0:T(8,128)(2,1)S(1)} custom-call(s32[2]{0:T(128)S(1)} %pad_add_fusion.place_ref, bf16[256,2048]{1,0:T(8,128)(2,1)S(1)} %bitcast.8, bf16[2048,128]{1,0:T(8,128)(2,1)S(1)} %bitcast.11, bf16[2048,128]{1,0:T(8,128)(2,1)S(1)} %collective-permute-done.1.refs_2_, bf16[2048,128]{1,0:T(8,128)(2,1)S(1)} %collective-permute-done.refs_3_, ...), custom_call_target="tpu_custom_call" | custom-call | flops 536870912 | bytes 5242880 | tf_op jit(solution)/shard_map/pallas_call | solution.py:84
  31.1 0.5 copy-done
  31.5 2.8 %collective-permute-start.3 = (bf16[1024,2048]{1,0:T(8,128)(2,1)S(1)}, bf16[1024,2048]{1,0:T(8,128)(2,1)S(1)}, u32[]{:S(2)}, u32[]{:S(2)}) collective-permute-start(bf16[1024,2048]{1,0:T(8,128)(2,1)S(1)} %copy-done), channel_id=1, source_target_pairs={{0,32},{32,0},{64,96},{96,64},{128,160},{160,128},{192,224},{224,1... | collective-permute-start | bytes 12582920 | tf_op jit(solution)/shard_map/ppermute | solution.py:269
  34.3 32.2 %all_to_all.20.parts_ref = bf16[8,256,512]{2,1,0:T(8,128)(2,1)S(1)} all-to-all(bf16[8,256,512]{2,1,0:T(8,128)(2,1)S(1)} %shard_map.48), channel_id=1, replica_groups={{0,64,128,192,256,320,384,448},{32,96,160,224,288,352,416,480},{1,65,12..., dimensions={0} | all-to-all | bytes 4194304 | tf_op jit(solution)/shard_map/all_to_all | solution.py:270
  66.5 0.0 collective-permute-done.3.theirs_ref
  66.5 6.7 %shard_map.49 = (bf16[4,128,1024]{2,1,0:T(8,128)(2,1)}, bf16[2,128,1024]{2,1,0:T(8,128)(2,1)S(1)}, bf16[2,128,1024]{2,1,0:T(8,128)(2,1)S(1)}) custom-call(s32[2]{0:T(128)S(1)} %pad_add_fusion.place_ref, bf16[8,256,512]{2,1,0:T(8,128)(2,1)S(1)} %all_to_all.20.parts_ref, bf16[1024,2048]{1,0:T(8,128)(2,1)S(1)} %copy-done, ...), custom_call_target="tpu_custom_call" | custom-call | flops 4294967296 | bytes 12582912 | tf_op jit(solution)/shard_map/pallas_call | solution.py:141
  73.2 3.5 %all-to-all-start.2 = ((bf16[4,128,1024]{2,1,0:T(8,128)(2,1)}), bf16[4,128,1024]{2,1,0:T(8,128)(2,1)S(1)}, u32[]{:S(2)}, u32[]{:S(2)}) async-start(bf16[4,128,1024]{2,1,0:T(8,128)(2,1)} %get-tuple-element.28), calls=%async_computation.2 | async-start | bytes 2097152 | tf_op jit(solution)/shard_map/all_to_all | solution.py:273
  76.7 8.6 %collective-permute-start.4 = (bf16[2,128,1024]{2,1,0:T(8,128)(2,1)S(1)}, bf16[2,128,1024]{2,1,0:T(8,128)(2,1)S(1)}, u32[]{:S(2)}, u32[]{:S(2)}) collective-permute-start(bf16[2,128,1024]{2,1,0:T(8,128)(2,1)S(1)} %get-tuple-element.30), channel_id=1, source_target_pairs={{0,30},{1,31},{2,4},{3,5},{4,2},{5,3},{6,8},{7,9},{8,6},{9,7},{10,... | collective-permute-start | bytes 1572872 | tf_op jit(solution)/shard_map/ppermute | solution.py:274
  85.3 10.8 %collective-permute-done.4.came_ref = bf16[2,128,1024]{2,1,0:T(8,128)(2,1)S(1)} collective-permute-done((bf16[2,128,1024]{2,1,0:T(8,128)(2,1)S(1)}, bf16[2,128,1024]{2,1,0:T(8,128)(2,1)S(1)}, u32[]{:S(2)}, u32[]{:S(2)}) %collective-permute-start.4) | collective-permute-done | bytes 524320 | tf_op jit(solution)/shard_map/ppermute | solution.py:274
  96.1 0.3 shard_map.50
  96.4 3.1 %collective-permute-start.5 = (bf16[128,1024]{1,0:T(8,128)(2,1)S(1)}, bf16[128,1024]{1,0:T(8,128)(2,1)S(1)}, u32[]{:S(2)}, u32[]{:S(2)}) collective-permute-start(bf16[128,1024]{1,0:T(8,128)(2,1)S(1)} %get-tuple-element.32), channel_id=1, source_target_pairs={{0,1},{1,0},{2,3},{3,2},{4,5},{5,4},{6,7},{7,6},{8,9},{9,8},{10,11... | collective-permute-start | bytes 786440 | tf_op jit(solution)/shard_map/ppermute | solution.py:278
  99.5 4.5 %collective-permute-done.5.refs_1_ = bf16[128,1024]{1,0:T(8,128)(2,1)S(1)} collective-permute-done((bf16[128,1024]{1,0:T(8,128)(2,1)S(1)}, bf16[128,1024]{1,0:T(8,128)(2,1)S(1)}, u32[]{:S(2)}, u32[]{:S(2)}) %collective-permute-start.5) | collective-permute-done | bytes 262176 | tf_op jit(solution)/shard_map/ppermute | solution.py:278
  104.0 0.0 all-to-all-done.2.gathered_ref
  104.0 0.9 shard_map.51
  104.9 42.9 %all_to_all.21 = bf16[16,16,1024]{2,1,0:T(8,128)(2,1)S(1)} all-to-all(bf16[16,16,1024]{2,1,0:T(8,128)(2,1)S(1)} %shard_map.51), channel_id=1, replica_groups={{0,32,4,36,8,40,12,44,16,48,20,52,24,56,28,60},{1,33,5,37,9,41,13,45,17..., dimensions={0} | all-to-all | bytes 1048576 | tf_op jit(solution)/shard_map/all_to_all | solution.py:279
  147.8 0.1 convert_reduce_fusion
  147.9 0.7 broadcast_multiply_fusion
Async XLA Ops:
  0.0 24.1 %collective-permute-start = (bf16[2048,128]{1,0:T(8,128)(2,1)}, bf16[2048,128]{1,0:T(8,128)(2,1)S(1)}, u32[]{:S(2)}, u32[]{:S(2)}) collective-permute-start(bf16[2048,128]{1,0:T(8,128)(2,1)} %bitcast.9), channel_id=1, source_target_pairs={{0,256},{32,288},{64,320},{96,352},{128,384},{160,416},{192,448},{... | collective-permute-start | bytes 1572872 | tf_op jit(solution)/shard_map/ppermute | solution.py:255
  5.5 1.0 copy-start.2
  7.5 21.9 %all-to-all-start = ((bf16[8,32,2048]{2,1,0:T(8,128)(2,1)}), bf16[8,32,2048]{2,1,0:T(8,128)(2,1)S(1)}, u32[]{:S(2)}, u32[]{:S(2)}) async-start(bf16[8,32,2048]{2,1,0:T(8,128)(2,1)} %shard_map.46), calls=%async_computation | async-start | bytes 2097152 | tf_op jit(solution)/shard_map/all_to_all | solution.py:260
  14.2 12.3 %collective-permute-start.1 = (bf16[2048,128]{1,0:T(8,128)(2,1)}, bf16[2048,128]{1,0:T(8,128)(2,1)S(1)}, u32[]{:S(2)}, u32[]{:S(2)}) collective-permute-start(bf16[2048,128]{1,0:T(8,128)(2,1)} %bitcast.10), channel_id=1, source_target_pairs={{0,32},{32,0},{64,96},{96,64},{128,160},{160,128},{192,224},{224,1... | collective-permute-start | bytes 1572872 | tf_op jit(solution)/shard_map/ppermute | solution.py:254
  18.2 11.2 %copy-start.1 = (bf16[1,2048,128]{2,1,0:T(8,128)(2,1)S(1)}, bf16[1,2048,128]{2,1,0:T(8,128)(2,1)}, u32[]{:S(2)}) copy-start(bf16[1,2048,128]{2,1,0:T(8,128)(2,1)} %param.5) | copy-start | bytes 1572868
  24.1 5.2 %collective-permute-start.2 = (bf16[2048,128]{1,0:T(8,128)(2,1)S(1)}, bf16[2048,128]{1,0:T(8,128)(2,1)S(1)}, u32[]{:S(2)}, u32[]{:S(2)}) collective-permute-start(bf16[2048,128]{1,0:T(8,128)(2,1)S(1)} %collective-permute-done.refs_3_), channel_id=1, source_target_pairs={{0,32},{32,0},{64,96},{96,64},{128,160},{160,128},{192,224},{224,1... | collective-permute-start | bytes 1572872 | tf_op jit(solution)/shard_map/ppermute | solution.py:258
  29.4 2.2 %copy-start = (bf16[1024,2048]{1,0:T(8,128)(2,1)S(1)}, bf16[1024,2048]{1,0:T(8,128)(2,1)}, u32[]{:S(2)}) copy-start(bf16[1024,2048]{1,0:T(8,128)(2,1)} %shard_map.47.mine_ref) | copy-start | bytes 12582916
  31.5 34.9 %collective-permute-start.3 = (bf16[1024,2048]{1,0:T(8,128)(2,1)S(1)}, bf16[1024,2048]{1,0:T(8,128)(2,1)S(1)}, u32[]{:S(2)}, u32[]{:S(2)}) collective-permute-start(bf16[1024,2048]{1,0:T(8,128)(2,1)S(1)} %copy-done), channel_id=1, source_target_pairs={{0,32},{32,0},{64,96},{96,64},{128,160},{160,128},{192,224},{224,1... | collective-permute-start | bytes 12582920 | tf_op jit(solution)/shard_map/ppermute | solution.py:269
  73.2 30.8 %all-to-all-start.2 = ((bf16[4,128,1024]{2,1,0:T(8,128)(2,1)}), bf16[4,128,1024]{2,1,0:T(8,128)(2,1)S(1)}, u32[]{:S(2)}, u32[]{:S(2)}) async-start(bf16[4,128,1024]{2,1,0:T(8,128)(2,1)} %get-tuple-element.28), calls=%async_computation.2 | async-start | bytes 2097152 | tf_op jit(solution)/shard_map/all_to_all | solution.py:273
  76.7 19.4 %collective-permute-start.4 = (bf16[2,128,1024]{2,1,0:T(8,128)(2,1)S(1)}, bf16[2,128,1024]{2,1,0:T(8,128)(2,1)S(1)}, u32[]{:S(2)}, u32[]{:S(2)}) collective-permute-start(bf16[2,128,1024]{2,1,0:T(8,128)(2,1)S(1)} %get-tuple-element.30), channel_id=1, source_target_pairs={{0,30},{1,31},{2,4},{3,5},{4,2},{5,3},{6,8},{7,9},{8,6},{9,7},{10,... | collective-permute-start | bytes 1572872 | tf_op jit(solution)/shard_map/ppermute | solution.py:274
  96.4 7.6 %collective-permute-start.5 = (bf16[128,1024]{1,0:T(8,128)(2,1)S(1)}, bf16[128,1024]{1,0:T(8,128)(2,1)S(1)}, u32[]{:S(2)}, u32[]{:S(2)}) collective-permute-start(bf16[128,1024]{1,0:T(8,128)(2,1)S(1)} %get-tuple-element.32), channel_id=1, source_target_pairs={{0,1},{1,0},{2,3},{3,2},{4,5},{5,4},{6,7},{7,6},{8,9},{9,8},{10,11... | collective-permute-start | bytes 786440 | tf_op jit(solution)/shard_map/ppermute | solution.py:278

commit v11 on v7

--- a/solution.py
+++ b/solution.py
@@ -255,12 +255,10 @@
     (terms,) = scores_of(False, place, parts, mine)
     gathered = lax.all_to_all(terms, "dim", 0, 0, tiled=True, axis_index_groups=near)
     here, *away = scores_of(True, place, parts, theirs)
-    others = [here] + [
-        lax.ppermute(
-            term, "dim", [(d, (((d + SIDES) ^ k) - SIDES) % slots if k & SIDES else d ^ k) for d in range(slots)]
-        )
-        for k, term in enumerate(away, 1)
-    ]
+    others = [here]
+    for k in (1, 3, 2):
+        swap = [(d, (((d + SIDES) ^ k) - SIDES) % slots if k & SIDES else d ^ k) for d in range(slots)]
+        others.append(lax.ppermute(away[k - 1], "dim", swap))
     sums = lax.all_to_all(
         added(place, tile, gathered, others), ("ex", "dim"), 0, 0, tiled=True, axis_index_groups=far
     )

time: 146 us -> 146 us (level)
  transfers between devices with their start and end apart: 10 -> 10, of which waited for: 5 -> 4; matrix products, arithmetic and copies ran while one was open for 1% -> 1% of each run, Pallas kernels for 13% -> 13%
where the time goes in v11:
time: 146 us; the launch traced here: 144 us
  starting transfers between devices  41.3 us (28%)
  blocking collectives  40.4 us (28%)
  waiting for transfers between devices  35.8 us (25%)
  Pallas kernels  22.9 us (16%)
  local copies, waits for them, and re-layouts  2.83 us (2%)
    all_to_all x1, blocking collectives, shards(): lax.all_to_all(added(place, tile, gathered, others), ('ex', 'dim'), 0, 0,...  40.4 us
    all_to_all x1, waiting for transfers between devices, shards(): lax.all_to_all(copies, 'ex', 0, 0, tiled=True, axis_index_groups=same_core)  23.9 us
    ppermute x3, starting transfers between devices, shards(): others.append(lax.ppermute(away[k - 1], 'dim', swap))  13 us
    pallas_call x2, Pallas kernels, scores_of(): pl.pallas_call(functools.partial(score, apart), grid_spec=pltpu.PrefetchS...  11.9 us
    ppermute x3, waiting for transfers between devices, shards(): others.append(lax.ppermute(away[k - 1], 'dim', swap))  9.08 us
    all_to_all x1, starting transfers between devices, shards(): lax.all_to_all(halves, 'ex', 0, 0, tiled=True, axis_index_groups=beside)  6.78 us
    pallas_call x1, Pallas kernels, dequantized(): pl.pallas_call(dequantize, grid=(rows // tile,), in_specs=[pl.BlockSpec((...  5.99 us
    all_to_all x1, starting transfers between devices, shards(): lax.all_to_all(copies, 'ex', 0, 0, tiled=True, axis_index_groups=same_core)  5.96 us
  transfers between devices with their start and end apart: 10, of which 4 were waited for; matrix products, arithmetic and copies ran while one was open for 1% of the time, Pallas kernels for 13%

profile of v11, /device:TPU:1, one launch (start us, length us, event | category | flops | bytes accessed | tf_op | source)
XLA Modules:
  0.0 144.2 jit_solution(1363296643657313224)
XLA Ops:
  0.0 5.5 %collective-permute-start = (bf16[2048,128]{1,0:T(8,128)(2,1)}, bf16[2048,128]{1,0:T(8,128)(2,1)S(1)}, u32[]{:S(2)}, u32[]{:S(2)}) collective-permute-start(bf16[2048,128]{1,0:T(8,128)(2,1)} %bitcast.9), channel_id=1, source_target_pairs={{0,256},{32,288},{64,320},{96,352},{128,384},{160,416},{192,448},{... | collective-permute-start | bytes 1572872 | tf_op jit(solution)/shard_map/ppermute | solution.py:238
  5.5 0.0 copy-start.1
  5.5 0.9 copy-done.1
  6.4 1.0 shard_map.46
  7.5 6.8 %all-to-all-start = ((bf16[8,32,2048]{2,1,0:T(8,128)(2,1)}), bf16[8,32,2048]{2,1,0:T(8,128)(2,1)S(1)}, u32[]{:S(2)}, u32[]{:S(2)}) async-start(bf16[8,32,2048]{2,1,0:T(8,128)(2,1)} %shard_map.46), calls=%async_computation | async-start | bytes 2097152 | tf_op jit(solution)/shard_map/all_to_all | solution.py:243
  14.2 2.0 %collective-permute-start.1 = (bf16[2048,128]{1,0:T(8,128)(2,1)}, bf16[2048,128]{1,0:T(8,128)(2,1)S(1)}, u32[]{:S(2)}, u32[]{:S(2)}) collective-permute-start(bf16[2048,128]{1,0:T(8,128)(2,1)} %bitcast.10), channel_id=1, source_target_pairs={{0,32},{32,0},{64,96},{96,64},{128,160},{160,128},{192,224},{224,1... | collective-permute-start | bytes 1572872 | tf_op jit(solution)/shard_map/ppermute | solution.py:237
  16.3 1.9 %copy.5.scales_ref = f32[1024,16]{1,0:T(8,128)} copy(f32[1024,16]{0,1:T(8,128)} %param.7) | data formatting | bytes 131072 | tf_op args[3]
  18.1 0.0 copy-start
  18.1 6.0 %shard_map.47.store_ref = bf16[1024,2048]{1,0:T(8,128)(2,1)} custom-call(bf16[1024,2048]{1,0:T(8,128)(2,1)} %codes_ref.1, f32[1024,16]{1,0:T(8,128)} %copy.5.scales_ref), custom_call_target="tpu_custom_call" | custom-call | flops 2097152 | bytes 8388608 | tf_op jit(solution)/shard_map/pallas_call | solution.py:27
  24.1 0.0 collective-permute-done.refs_3_
  24.1 2.3 %collective-permute-start.2 = (bf16[2048,128]{1,0:T(8,128)(2,1)S(1)}, bf16[2048,128]{1,0:T(8,128)(2,1)S(1)}, u32[]{:S(2)}, u32[]{:S(2)}) collective-permute-start(bf16[2048,128]{1,0:T(8,128)(2,1)S(1)} %collective-permute-done.refs_3_), channel_id=1, source_target_pairs={{0,32},{32,0},{64,96},{96,64},{128,160},{160,128},{192,224},{224,1... | collective-permute-start | bytes 1572872 | tf_op jit(solution)/shard_map/ppermute | solution.py:241
  26.5 0.1 pad_add_fusion.place_ref
  26.5 0.0 collective-permute-done.1.refs_2_
  26.5 2.8 %all-to-all-done = bf16[8,32,2048]{2,1,0:T(8,128)(2,1)S(1)} async-done(((bf16[8,32,2048]{2,1,0:T(8,128)(2,1)}), bf16[8,32,2048]{2,1,0:T(8,128)(2,1)S(1)}, u32[]{:S(2)}, u32[]{:S(2)}) %all-to-all-start) | async-done | bytes 1048608 | tf_op jit(solution)/shard_map/all_to_all | solution.py:243
  29.4 0.0 collective-permute-done.2.refs_4_
  29.4 0.0 copy-done
  29.4 3.1 %shard_map.48 = bf16[8,256,512]{2,1,0:T(8,128)(2,1)} custom-call(s32[2]{0:T(128)S(1)} %pad_add_fusion.place_ref, bf16[256,2048]{1,0:T(8,128)(2,1)S(1)} %bitcast.8, bf16[2048,128]{1,0:T(8,128)(2,1)S(1)} %bitcast.11, bf16[2048,128]{1,0:T(8,128)(2,1)S(1)} %collective-permute-done.1.refs_2_, bf16[2048,128]{1,0:T(8,128)(2,1)S(1)} %collective-permute-done.refs_3_, ...), custom_call_target="tpu_custom_call" | custom-call | flops 536870912 | bytes 5242880 | tf_op jit(solution)/shard_map/pallas_call | solution.py:86
  32.4 6.0 %all-to-all-start.1 = ((bf16[8,256,512]{2,1,0:T(8,128)(2,1)}), bf16[8,256,512]{2,1,0:T(8,128)(2,1)S(1)}, u32[]{:S(2)}, u32[]{:S(2)}) async-start(bf16[8,256,512]{2,1,0:T(8,128)(2,1)} %shard_map.48), calls=%async_computation.1 | async-start | bytes 4194304 | tf_op jit(solution)/shard_map/all_to_all | solution.py:253
  38.4 2.3 %collective-permute-start.3 = (bf16[1024,2048]{1,0:T(8,128)(2,1)}, bf16[1024,2048]{1,0:T(8,128)(2,1)}, u32[]{:S(2)}, u32[]{:S(2)}) collective-permute-start(bf16[1024,2048]{1,0:T(8,128)(2,1)} %shard_map.47.store_ref), channel_id=1, source_target_pairs={{0,32},{32,0},{64,96},{96,64},{128,160},{160,128},{192,224},{224,1... | collective-permute-start | bytes 12582920 | tf_op jit(solution)/shard_map/ppermute | solution.py:252
  40.7 23.9 %all-to-all-done.1.parts_ref = bf16[8,256,512]{2,1,0:T(8,128)(2,1)S(1)} async-done(((bf16[8,256,512]{2,1,0:T(8,128)(2,1)}), bf16[8,256,512]{2,1,0:T(8,128)(2,1)S(1)}, u32[]{:S(2)}, u32[]{:S(2)}) %all-to-all-start.1) | async-done | bytes 2097184 | tf_op jit(solution)/shard_map/all_to_all | solution.py:253
  64.6 6.3 %shard_map.49 = bf16[4,128,1024]{2,1,0:T(8,128)(2,1)} custom-call(s32[2]{0:T(128)S(1)} %pad_add_fusion.place_ref, bf16[8,256,512]{2,1,0:T(8,128)(2,1)S(1)} %all-to-all-done.1.parts_ref, bf16[1024,2048]{1,0:T(8,128)(2,1)} %shard_map.47.store_ref), custom_call_target="tpu_custom_call" | custom-call | flops 2147483648 | bytes 7340032 | tf_op jit(solution)/shard_map/pallas_call | solution.py:148
  70.9 3.5 %all-to-all-start.2 = ((bf16[4,128,1024]{2,1,0:T(8,128)(2,1)}), bf16[4,128,1024]{2,1,0:T(8,128)(2,1)S(1)}, u32[]{:S(2)}, u32[]{:S(2)}) async-start(bf16[4,128,1024]{2,1,0:T(8,128)(2,1)} %shard_map.49), calls=%async_computation.2 | async-start | bytes 2097152 | tf_op jit(solution)/shard_map/all_to_all | solution.py:256
  74.4 0.0 collective-permute-done.3.store_ref
  74.4 5.6 %shard_map.50 = (bf16[128,1024]{1,0:T(8,128)(2,1)S(1)}, bf16[128,1024]{1,0:T(8,128)(2,1)S(1)}, bf16[128,1024]{1,0:T(8,128)(2,1)S(1)}, bf16[128,1024]{1,0:T(8,128)(2,1)S(1)}) custom-call(s32[2]{0:T(128)S(1)} %pad_add_fusion.place_ref, bf16[8,256,512]{2,1,0:T(8,128)(2,1)S(1)} %all-to-all-done.1.parts_ref, bf16[1024,2048]{1,0:T(8,128)(2,1)} %collective-permute-done.3.store_ref), custom_call_target="tpu_custom_call" | custom-call | flops 2147483648 | bytes 7340032 | tf_op jit(solution)/shard_map/pallas_call | solution.py:148
  80.0 3.3 %collective-permute-start.4 = (bf16[128,1024]{1,0:T(8,128)(2,1)S(1)}, bf16[128,1024]{1,0:T(8,128)(2,1)S(1)}, u32[]{:S(2)}, u32[]{:S(2)}) collective-permute-start(bf16[128,1024]{1,0:T(8,128)(2,1)S(1)} %get-tuple-element.28), channel_id=1, source_target_pairs={{0,1},{1,0},{2,3},{3,2},{4,5},{5,4},{6,7},{7,6},{8,9},{9,8},{10,11... | collective-permute-start | bytes 786440 | tf_op jit(solution)/shard_map/ppermute | solution.py:261
  83.3 7.7 %collective-permute-start.5 = (bf16[128,1024]{1,0:T(8,128)(2,1)S(1)}, bf16[128,1024]{1,0:T(8,128)(2,1)S(1)}, u32[]{:S(2)}, u32[]{:S(2)}) collective-permute-start(bf16[128,1024]{1,0:T(8,128)(2,1)S(1)} %get-tuple-element.29), channel_id=1, source_target_pairs={{0,31},{1,30},{2,5},{3,4},{4,3},{5,2},{6,9},{7,8},{8,7},{9,6},{10,... | collective-permute-start | bytes 786440 | tf_op jit(solution)/shard_map/ppermute | solution.py:261
  91.1 1.9 %collective-permute-start.6 = (bf16[128,1024]{1,0:T(8,128)(2,1)S(1)}, bf16[128,1024]{1,0:T(8,128)(2,1)S(1)}, u32[]{:S(2)}, u32[]{:S(2)}) collective-permute-start(bf16[128,1024]{1,0:T(8,128)(2,1)S(1)} %get-tuple-element.30), channel_id=1, source_target_pairs={{0,30},{1,31},{2,4},{3,5},{4,2},{5,3},{6,8},{7,9},{8,6},{9,7},{10,... | collective-permute-start | bytes 786440 | tf_op jit(solution)/shard_map/ppermute | solution.py:261
  93.0 5.7 %collective-permute-done.4.refs_1_ = bf16[128,1024]{1,0:T(8,128)(2,1)S(1)} collective-permute-done((bf16[128,1024]{1,0:T(8,128)(2,1)S(1)}, bf16[128,1024]{1,0:T(8,128)(2,1)S(1)}, u32[]{:S(2)}, u32[]{:S(2)}) %collective-permute-start.4) | collective-permute-done | bytes 262176 | tf_op jit(solution)/shard_map/ppermute | solution.py:261
  98.7 0.0 collective-permute-done.5.refs_2_
  98.7 3.4 %collective-permute-done.6.refs_3_ = bf16[128,1024]{1,0:T(8,128)(2,1)S(1)} collective-permute-done((bf16[128,1024]{1,0:T(8,128)(2,1)S(1)}, bf16[128,1024]{1,0:T(8,128)(2,1)S(1)}, u32[]{:S(2)}, u32[]{:S(2)}) %collective-permute-start.6) | collective-permute-done | bytes 262176 | tf_op jit(solution)/shard_map/ppermute | solution.py:261
  102.1 0.0 all-to-all-done.2.gathered_ref
  102.1 1.0 shard_map.51
  103.1 40.4 %all_to_all.20 = bf16[16,16,1024]{2,1,0:T(8,128)(2,1)S(1)} all-to-all(bf16[16,16,1024]{2,1,0:T(8,128)(2,1)S(1)} %shard_map.51), channel_id=1, replica_groups={{0,32,4,36,8,40,12,44,16,48,20,52,24,56,28,60},{1,33,5,37,9,41,13,45,17..., dimensions={0} | all-to-all | bytes 1048576 | tf_op jit(solution)/shard_map/all_to_all | solution.py:262
  143.5 0.1 convert_reduce_fusion
  143.6 0.7 broadcast_multiply_fusion
Async XLA Ops:
  0.0 24.1 %collective-permute-start = (bf16[2048,128]{1,0:T(8,128)(2,1)}, bf16[2048,128]{1,0:T(8,128)(2,1)S(1)}, u32[]{:S(2)}, u32[]{:S(2)}) collective-permute-start(bf16[2048,128]{1,0:T(8,128)(2,1)} %bitcast.9), channel_id=1, source_target_pairs={{0,256},{32,288},{64,320},{96,352},{128,384},{160,416},{192,448},{... | collective-permute-start | bytes 1572872 | tf_op jit(solution)/shard_map/ppermute | solution.py:238
  5.5 1.0 copy-start.1
  7.5 21.9 %all-to-all-start = ((bf16[8,32,2048]{2,1,0:T(8,128)(2,1)}), bf16[8,32,2048]{2,1,0:T(8,128)(2,1)S(1)}, u32[]{:S(2)}, u32[]{:S(2)}) async-start(bf16[8,32,2048]{2,1,0:T(8,128)(2,1)} %shard_map.46), calls=%async_computation | async-start | bytes 2097152 | tf_op jit(solution)/shard_map/all_to_all | solution.py:243
  14.2 12.3 %collective-permute-start.1 = (bf16[2048,128]{1,0:T(8,128)(2,1)}, bf16[2048,128]{1,0:T(8,128)(2,1)S(1)}, u32[]{:S(2)}, u32[]{:S(2)}) collective-permute-start(bf16[2048,128]{1,0:T(8,128)(2,1)} %bitcast.10), channel_id=1, source_target_pairs={{0,32},{32,0},{64,96},{96,64},{128,160},{160,128},{192,224},{224,1... | collective-permute-start | bytes 1572872 | tf_op jit(solution)/shard_map/ppermute | solution.py:237
  18.1 11.2 %copy-start = (bf16[1,2048,128]{2,1,0:T(8,128)(2,1)S(1)}, bf16[1,2048,128]{2,1,0:T(8,128)(2,1)}, u32[]{:S(2)}) copy-start(bf16[1,2048,128]{2,1,0:T(8,128)(2,1)} %param.5) | copy-start | bytes 1572868
  24.1 5.2 %collective-permute-start.2 = (bf16[2048,128]{1,0:T(8,128)(2,1)S(1)}, bf16[2048,128]{1,0:T(8,128)(2,1)S(1)}, u32[]{:S(2)}, u32[]{:S(2)}) collective-permute-start(bf16[2048,128]{1,0:T(8,128)(2,1)S(1)} %collective-permute-done.refs_3_), channel_id=1, source_target_pairs={{0,32},{32,0},{64,96},{96,64},{128,160},{160,128},{192,224},{224,1... | collective-permute-start | bytes 1572872 | tf_op jit(solution)/shard_map/ppermute | solution.py:241
  32.4 32.2 %all-to-all-start.1 = ((bf16[8,256,512]{2,1,0:T(8,128)(2,1)}), bf16[8,256,512]{2,1,0:T(8,128)(2,1)S(1)}, u32[]{:S(2)}, u32[]{:S(2)}) async-start(bf16[8,256,512]{2,1,0:T(8,128)(2,1)} %shard_map.48), calls=%async_computation.1 | async-start | bytes 4194304 | tf_op jit(solution)/shard_map/all_to_all | solution.py:253
  38.4 36.1 %collective-permute-start.3 = (bf16[1024,2048]{1,0:T(8,128)(2,1)}, bf16[1024,2048]{1,0:T(8,128)(2,1)}, u32[]{:S(2)}, u32[]{:S(2)}) collective-permute-start(bf16[1024,2048]{1,0:T(8,128)(2,1)} %shard_map.47.store_ref), channel_id=1, source_target_pairs={{0,32},{32,0},{64,96},{96,64},{128,160},{160,128},{192,224},{224,1... | collective-permute-start | bytes 12582920 | tf_op jit(solution)/shard_map/ppermute | solution.py:252
  70.9 31.2 %all-to-all-start.2 = ((bf16[4,128,1024]{2,1,0:T(8,128)(2,1)}), bf16[4,128,1024]{2,1,0:T(8,128)(2,1)S(1)}, u32[]{:S(2)}, u32[]{:S(2)}) async-start(bf16[4,128,1024]{2,1,0:T(8,128)(2,1)} %shard_map.49), calls=%async_computation.2 | async-start | bytes 2097152 | tf_op jit(solution)/shard_map/all_to_all | solution.py:256
  80.0 18.7 %collective-permute-start.4 = (bf16[128,1024]{1,0:T(8,128)(2,1)S(1)}, bf16[128,1024]{1,0:T(8,128)(2,1)S(1)}, u32[]{:S(2)}, u32[]{:S(2)}) collective-permute-start(bf16[128,1024]{1,0:T(8,128)(2,1)S(1)} %get-tuple-element.28), channel_id=1, source_target_pairs={{0,1},{1,0},{2,3},{3,2},{4,5},{5,4},{6,7},{7,6},{8,9},{9,8},{10,11... | collective-permute-start | bytes 786440 | tf_op jit(solution)/shard_map/ppermute | solution.py:261
  83.3 15.4 %collective-permute-start.5 = (bf16[128,1024]{1,0:T(8,128)(2,1)S(1)}, bf16[128,1024]{1,0:T(8,128)(2,1)S(1)}, u32[]{:S(2)}, u32[]{:S(2)}) collective-permute-start(bf16[128,1024]{1,0:T(8,128)(2,1)S(1)} %get-tuple-element.29), channel_id=1, source_target_pairs={{0,31},{1,30},{2,5},{3,4},{4,3},{5,2},{6,9},{7,8},{8,7},{9,6},{10,... | collective-permute-start | bytes 786440 | tf_op jit(solution)/shard_map/ppermute | solution.py:261
  91.1 11.0 %collective-permute-start.6 = (bf16[128,1024]{1,0:T(8,128)(2,1)S(1)}, bf16[128,1024]{1,0:T(8,128)(2,1)S(1)}, u32[]{:S(2)}, u32[]{:S(2)}) collective-permute-start(bf16[128,1024]{1,0:T(8,128)(2,1)S(1)} %get-tuple-element.30), channel_id=1, source_target_pairs={{0,30},{1,31},{2,4},{3,5},{4,2},{5,3},{6,8},{7,9},{8,6},{9,7},{10,... | collective-permute-start | bytes 786440 | tf_op jit(solution)/shard_map/ppermute | solution.py:261

commit v12 on v7

--- a/solution.py
+++ b/solution.py
@@ -139,7 +139,7 @@
     chips, block_rows, columns = parts.shape
     rows = ROWS_X * block_rows
     examples, width = store.shape
-    tile = 256
+    tile = 512
     if apart:
         block, index, shape, count = (rows // NEAR, tile), lambda n, place_ref: (0, n), (rows // NEAR, examples), NEAR
     else:

time: 146 us -> 144 us (0.986)
  the two profiles are of different devices: /device:TPU:1 before, /device:TPU:7 now
where the time goes in v12:
time: 144 us
  starting transfers between devices  41.4 us (29%)
  blocking collectives  41.4 us (29%)
  waiting for transfers between devices  35.4 us (25%)
  Pallas kernels  21.8 us (15%)
  local copies, waits for them, and re-layouts  2.83 us (2%)
    all_to_all x1, blocking collectives, shards(): lax.all_to_all(added(place, tile, gathered, others), ('ex', 'dim'), 0, 0,...  41.4 us
    all_to_all x1, waiting for transfers between devices, shards(): lax.all_to_all(copies, 'ex', 0, 0, tiled=True, axis_index_groups=same_core)  23.2 us
    ppermute x3, starting transfers between devices, shards(): lax.ppermute(term, 'dim', [(d, ((d + SIDES ^ k) - SIDES) % slots if k & S...  12.7 us
    pallas_call x2, Pallas kernels, scores_of(): pl.pallas_call(functools.partial(score, apart), grid_spec=pltpu.PrefetchS...  10.7 us
    ppermute x3, waiting for transfers between devices, shards(): lax.ppermute(term, 'dim', [(d, ((d + SIDES ^ k) - SIDES) % slots if k & S...  9.37 us
    all_to_all x1, starting transfers between devices, shards(): lax.all_to_all(terms, 'dim', 0, 0, tiled=True, axis_index_groups=near)  7.53 us
    pallas_call x1, Pallas kernels, dequantized(): pl.pallas_call(dequantize, grid=(rows // tile,), in_specs=[pl.BlockSpec((...  5.99 us
    all_to_all x1, starting transfers between devices, shards(): lax.all_to_all(copies, 'ex', 0, 0, tiled=True, axis_index_groups=same_core)  5.68 us
  transfers between devices with their start and end apart: 10, of which 4 were waited for; matrix products, arithmetic and copies ran while one was open for 1% of the time, Pallas kernels for 12%

profile of v12, /device:TPU:7, one launch (start us, length us, event | category | flops | bytes accessed | tf_op | source)
XLA Modules:
  0.0 143.7 jit_solution(12597303252201917321)
XLA Ops:
  0.0 3.0 %collective-permute-start = (bf16[2048,128]{1,0:T(8,128)(2,1)}, bf16[2048,128]{1,0:T(8,128)(2,1)S(1)}, u32[]{:S(2)}, u32[]{:S(2)}) collective-permute-start(bf16[2048,128]{1,0:T(8,128)(2,1)} %bitcast.9), channel_id=1, source_target_pairs={{0,256},{32,288},{64,320},{96,352},{128,384},{160,416},{192,448},{... | collective-permute-start | bytes 1572872 | tf_op jit(solution)/shard_map/ppermute | solution.py:238
  3.0 0.0 copy-start.1
  3.0 0.9 copy-done.1
  4.0 1.0 shard_map.46
  5.0 5.4 %all-to-all-start = ((bf16[8,32,2048]{2,1,0:T(8,128)(2,1)}), bf16[8,32,2048]{2,1,0:T(8,128)(2,1)S(1)}, u32[]{:S(2)}, u32[]{:S(2)}) async-start(bf16[8,32,2048]{2,1,0:T(8,128)(2,1)} %shard_map.46), calls=%async_computation | async-start | bytes 2097152 | tf_op jit(solution)/shard_map/all_to_all | solution.py:243
  10.4 1.9 %collective-permute-start.1 = (bf16[2048,128]{1,0:T(8,128)(2,1)}, bf16[2048,128]{1,0:T(8,128)(2,1)S(1)}, u32[]{:S(2)}, u32[]{:S(2)}) collective-permute-start(bf16[2048,128]{1,0:T(8,128)(2,1)} %bitcast.10), channel_id=1, source_target_pairs={{0,32},{32,0},{64,96},{96,64},{128,160},{160,128},{192,224},{224,1... | collective-permute-start | bytes 1572872 | tf_op jit(solution)/shard_map/ppermute | solution.py:237
  12.4 1.9 %copy.5.scales_ref = f32[1024,16]{1,0:T(8,128)} copy(f32[1024,16]{0,1:T(8,128)} %param.7) | data formatting | bytes 131072 | tf_op args[3]
  14.2 0.0 copy-start
  14.2 6.0 %shard_map.47.store_ref = bf16[1024,2048]{1,0:T(8,128)(2,1)} custom-call(bf16[1024,2048]{1,0:T(8,128)(2,1)} %codes_ref.1, f32[1024,16]{1,0:T(8,128)} %copy.5.scales_ref), custom_call_target="tpu_custom_call" | custom-call | flops 2097152 | bytes 8388608 | tf_op jit(solution)/shard_map/pallas_call | solution.py:27
  20.2 0.0 collective-permute-done.refs_3_
  20.2 2.4 %collective-permute-start.2 = (bf16[2048,128]{1,0:T(8,128)(2,1)S(1)}, bf16[2048,128]{1,0:T(8,128)(2,1)S(1)}, u32[]{:S(2)}, u32[]{:S(2)}) collective-permute-start(bf16[2048,128]{1,0:T(8,128)(2,1)S(1)} %collective-permute-done.refs_3_), channel_id=1, source_target_pairs={{0,32},{32,0},{64,96},{96,64},{128,160},{160,128},{192,224},{224,1... | collective-permute-start | bytes 1572872 | tf_op jit(solution)/shard_map/ppermute | solution.py:241
  22.7 0.1 pad_add_fusion.place_ref
  22.7 0.0 collective-permute-done.1.refs_2_
  22.7 2.8 %all-to-all-done = bf16[8,32,2048]{2,1,0:T(8,128)(2,1)S(1)} async-done(((bf16[8,32,2048]{2,1,0:T(8,128)(2,1)}), bf16[8,32,2048]{2,1,0:T(8,128)(2,1)S(1)}, u32[]{:S(2)}, u32[]{:S(2)}) %all-to-all-start) | async-done | bytes 1048608 | tf_op jit(solution)/shard_map/all_to_all | solution.py:243
  25.5 0.0 collective-permute-done.2.refs_4_
  25.5 0.0 copy-done
  25.5 3.1 %shard_map.48 = bf16[8,256,512]{2,1,0:T(8,128)(2,1)} custom-call(s32[2]{0:T(128)S(1)} %pad_add_fusion.place_ref, bf16[256,2048]{1,0:T(8,128)(2,1)S(1)} %bitcast.8, bf16[2048,128]{1,0:T(8,128)(2,1)S(1)} %bitcast.11, bf16[2048,128]{1,0:T(8,128)(2,1)S(1)} %collective-permute-done.1.refs_2_, bf16[2048,128]{1,0:T(8,128)(2,1)S(1)} %collective-permute-done.refs_3_, ...), custom_call_target="tpu_custom_call" | custom-call | flops 536870912 | bytes 5242880 | tf_op jit(solution)/shard_map/pallas_call | solution.py:86
  28.6 5.7 %all-to-all-start.1 = ((bf16[8,256,512]{2,1,0:T(8,128)(2,1)}), bf16[8,256,512]{2,1,0:T(8,128)(2,1)S(1)}, u32[]{:S(2)}, u32[]{:S(2)}) async-start(bf16[8,256,512]{2,1,0:T(8,128)(2,1)} %shard_map.48), calls=%async_computation.1 | async-start | bytes 4194304 | tf_op jit(solution)/shard_map/all_to_all | solution.py:253
  34.3 2.7 %collective-permute-start.3 = (bf16[1024,2048]{1,0:T(8,128)(2,1)}, bf16[1024,2048]{1,0:T(8,128)(2,1)}, u32[]{:S(2)}, u32[]{:S(2)}) collective-permute-start(bf16[1024,2048]{1,0:T(8,128)(2,1)} %shard_map.47.store_ref), channel_id=1, source_target_pairs={{0,32},{32,0},{64,96},{96,64},{128,160},{160,128},{192,224},{224,1... | collective-permute-start | bytes 12582920 | tf_op jit(solution)/shard_map/ppermute | solution.py:252
  37.0 23.2 %all-to-all-done.1.parts_ref = bf16[8,256,512]{2,1,0:T(8,128)(2,1)S(1)} async-done(((bf16[8,256,512]{2,1,0:T(8,128)(2,1)}), bf16[8,256,512]{2,1,0:T(8,128)(2,1)S(1)}, u32[]{:S(2)}, u32[]{:S(2)}) %all-to-all-start.1) | async-done | bytes 2097184 | tf_op jit(solution)/shard_map/all_to_all | solution.py:253
  60.2 5.7 %shard_map.49 = bf16[4,128,1024]{2,1,0:T(8,128)(2,1)} custom-call(s32[2]{0:T(128)S(1)} %pad_add_fusion.place_ref, bf16[8,256,512]{2,1,0:T(8,128)(2,1)S(1)} %all-to-all-done.1.parts_ref, bf16[1024,2048]{1,0:T(8,128)(2,1)} %shard_map.47.store_ref), custom_call_target="tpu_custom_call" | custom-call | flops 2147483648 | bytes 7340032 | tf_op jit(solution)/shard_map/pallas_call | solution.py:148
  65.9 7.5 %all-to-all-start.2 = ((bf16[4,128,1024]{2,1,0:T(8,128)(2,1)}), bf16[4,128,1024]{2,1,0:T(8,128)(2,1)S(1)}, u32[]{:S(2)}, u32[]{:S(2)}) async-start(bf16[4,128,1024]{2,1,0:T(8,128)(2,1)} %shard_map.49), calls=%async_computation.2 | async-start | bytes 2097152 | tf_op jit(solution)/shard_map/all_to_all | solution.py:256
  73.5 0.0 collective-permute-done.3.store_ref
  73.5 5.0 %shard_map.50 = (bf16[128,1024]{1,0:T(8,128)(2,1)S(1)}, bf16[128,1024]{1,0:T(8,128)(2,1)S(1)}, bf16[128,1024]{1,0:T(8,128)(2,1)S(1)}, bf16[128,1024]{1,0:T(8,128)(2,1)S(1)}) custom-call(s32[2]{0:T(128)S(1)} %pad_add_fusion.place_ref, bf16[8,256,512]{2,1,0:T(8,128)(2,1)S(1)} %all-to-all-done.1.parts_ref, bf16[1024,2048]{1,0:T(8,128)(2,1)} %collective-permute-done.3.store_ref), custom_call_target="tpu_custom_call" | custom-call | flops 2147483648 | bytes 7340032 | tf_op jit(solution)/shard_map/pallas_call | solution.py:148
  78.4 2.0 %collective-permute-start.4 = (bf16[128,1024]{1,0:T(8,128)(2,1)S(1)}, bf16[128,1024]{1,0:T(8,128)(2,1)S(1)}, u32[]{:S(2)}, u32[]{:S(2)}) collective-permute-start(bf16[128,1024]{1,0:T(8,128)(2,1)S(1)} %get-tuple-element.28), channel_id=1, source_target_pairs={{0,1},{1,0},{2,3},{3,2},{4,5},{5,4},{6,7},{7,6},{8,9},{9,8},{10,11... | collective-permute-start | bytes 786440 | tf_op jit(solution)/shard_map/ppermute | solution.py:259
  80.4 8.0 %collective-permute-start.5 = (bf16[128,1024]{1,0:T(8,128)(2,1)S(1)}, bf16[128,1024]{1,0:T(8,128)(2,1)S(1)}, u32[]{:S(2)}, u32[]{:S(2)}) collective-permute-start(bf16[128,1024]{1,0:T(8,128)(2,1)S(1)} %get-tuple-element.29), channel_id=1, source_target_pairs={{0,30},{1,31},{2,4},{3,5},{4,2},{5,3},{6,8},{7,9},{8,6},{9,7},{10,... | collective-permute-start | bytes 786440 | tf_op jit(solution)/shard_map/ppermute | solution.py:259
  88.4 2.8 %collective-permute-start.6 = (bf16[128,1024]{1,0:T(8,128)(2,1)S(1)}, bf16[128,1024]{1,0:T(8,128)(2,1)S(1)}, u32[]{:S(2)}, u32[]{:S(2)}) collective-permute-start(bf16[128,1024]{1,0:T(8,128)(2,1)S(1)} %get-tuple-element.30), channel_id=1, source_target_pairs={{0,31},{1,30},{2,5},{3,4},{4,3},{5,2},{6,9},{7,8},{8,7},{9,6},{10,... | collective-permute-start | bytes 786440 | tf_op jit(solution)/shard_map/ppermute | solution.py:259
  91.2 0.0 collective-permute-done.4.refs_1_
  91.2 2.4 %collective-permute-done.5.refs_2_ = bf16[128,1024]{1,0:T(8,128)(2,1)S(1)} collective-permute-done((bf16[128,1024]{1,0:T(8,128)(2,1)S(1)}, bf16[128,1024]{1,0:T(8,128)(2,1)S(1)}, u32[]{:S(2)}, u32[]{:S(2)}) %collective-permute-start.5) | collective-permute-done | bytes 262176 | tf_op jit(solution)/shard_map/ppermute | solution.py:259
  93.6 7.0 %collective-permute-done.6.refs_3_ = bf16[128,1024]{1,0:T(8,128)(2,1)S(1)} collective-permute-done((bf16[128,1024]{1,0:T(8,128)(2,1)S(1)}, bf16[128,1024]{1,0:T(8,128)(2,1)S(1)}, u32[]{:S(2)}, u32[]{:S(2)}) %collective-permute-start.6) | collective-permute-done | bytes 262176 | tf_op jit(solution)/shard_map/ppermute | solution.py:259
  100.6 0.0 all-to-all-done.2.gathered_ref
  100.6 1.0 shard_map.51
  101.6 41.4 %all_to_all.20 = bf16[16,16,1024]{2,1,0:T(8,128)(2,1)S(1)} all-to-all(bf16[16,16,1024]{2,1,0:T(8,128)(2,1)S(1)} %shard_map.51), channel_id=1, replica_groups={{0,32,4,36,8,40,12,44,16,48,20,52,24,56,28,60},{1,33,5,37,9,41,13,45,17..., dimensions={0} | all-to-all | bytes 1048576 | tf_op jit(solution)/shard_map/all_to_all | solution.py:264
  143.0 0.1 convert_reduce_fusion
  143.1 0.7 broadcast_multiply_fusion
Async XLA Ops:
  0.0 20.2 %collective-permute-start = (bf16[2048,128]{1,0:T(8,128)(2,1)}, bf16[2048,128]{1,0:T(8,128)(2,1)S(1)}, u32[]{:S(2)}, u32[]{:S(2)}) collective-permute-start(bf16[2048,128]{1,0:T(8,128)(2,1)} %bitcast.9), channel_id=1, source_target_pairs={{0,256},{32,288},{64,320},{96,352},{128,384},{160,416},{192,448},{... | collective-permute-start | bytes 1572872 | tf_op jit(solution)/shard_map/ppermute | solution.py:238
  3.0 1.0 copy-start.1
  5.0 20.5 %all-to-all-start = ((bf16[8,32,2048]{2,1,0:T(8,128)(2,1)}), bf16[8,32,2048]{2,1,0:T(8,128)(2,1)S(1)}, u32[]{:S(2)}, u32[]{:S(2)}) async-start(bf16[8,32,2048]{2,1,0:T(8,128)(2,1)} %shard_map.46), calls=%async_computation | async-start | bytes 2097152 | tf_op jit(solution)/shard_map/all_to_all | solution.py:243
  10.4 12.3 %collective-permute-start.1 = (bf16[2048,128]{1,0:T(8,128)(2,1)}, bf16[2048,128]{1,0:T(8,128)(2,1)S(1)}, u32[]{:S(2)}, u32[]{:S(2)}) collective-permute-start(bf16[2048,128]{1,0:T(8,128)(2,1)} %bitcast.10), channel_id=1, source_target_pairs={{0,32},{32,0},{64,96},{96,64},{128,160},{160,128},{192,224},{224,1... | collective-permute-start | bytes 1572872 | tf_op jit(solution)/shard_map/ppermute | solution.py:237
  14.2 11.3 %copy-start = (bf16[1,2048,128]{2,1,0:T(8,128)(2,1)S(1)}, bf16[1,2048,128]{2,1,0:T(8,128)(2,1)}, u32[]{:S(2)}) copy-start(bf16[1,2048,128]{2,1,0:T(8,128)(2,1)} %param.5) | copy-start | bytes 1572868
  20.2 5.3 %collective-permute-start.2 = (bf16[2048,128]{1,0:T(8,128)(2,1)S(1)}, bf16[2048,128]{1,0:T(8,128)(2,1)S(1)}, u32[]{:S(2)}, u32[]{:S(2)}) collective-permute-start(bf16[2048,128]{1,0:T(8,128)(2,1)S(1)} %collective-permute-done.refs_3_), channel_id=1, source_target_pairs={{0,32},{32,0},{64,96},{96,64},{128,160},{160,128},{192,224},{224,1... | collective-permute-start | bytes 1572872 | tf_op jit(solution)/shard_map/ppermute | solution.py:241
  28.6 31.6 %all-to-all-start.1 = ((bf16[8,256,512]{2,1,0:T(8,128)(2,1)}), bf16[8,256,512]{2,1,0:T(8,128)(2,1)S(1)}, u32[]{:S(2)}, u32[]{:S(2)}) async-start(bf16[8,256,512]{2,1,0:T(8,128)(2,1)} %shard_map.48), calls=%async_computation.1 | async-start | bytes 4194304 | tf_op jit(solution)/shard_map/all_to_all | solution.py:253
  34.3 39.2 %collective-permute-start.3 = (bf16[1024,2048]{1,0:T(8,128)(2,1)}, bf16[1024,2048]{1,0:T(8,128)(2,1)}, u32[]{:S(2)}, u32[]{:S(2)}) collective-permute-start(bf16[1024,2048]{1,0:T(8,128)(2,1)} %shard_map.47.store_ref), channel_id=1, source_target_pairs={{0,32},{32,0},{64,96},{96,64},{128,160},{160,128},{192,224},{224,1... | collective-permute-start | bytes 12582920 | tf_op jit(solution)/shard_map/ppermute | solution.py:252
  65.9 34.7 %all-to-all-start.2 = ((bf16[4,128,1024]{2,1,0:T(8,128)(2,1)}), bf16[4,128,1024]{2,1,0:T(8,128)(2,1)S(1)}, u32[]{:S(2)}, u32[]{:S(2)}) async-start(bf16[4,128,1024]{2,1,0:T(8,128)(2,1)} %shard_map.49), calls=%async_computation.2 | async-start | bytes 2097152 | tf_op jit(solution)/shard_map/all_to_all | solution.py:256
  78.4 12.8 %collective-permute-start.4 = (bf16[128,1024]{1,0:T(8,128)(2,1)S(1)}, bf16[128,1024]{1,0:T(8,128)(2,1)S(1)}, u32[]{:S(2)}, u32[]{:S(2)}) collective-permute-start(bf16[128,1024]{1,0:T(8,128)(2,1)S(1)} %get-tuple-element.28), channel_id=1, source_target_pairs={{0,1},{1,0},{2,3},{3,2},{4,5},{5,4},{6,7},{7,6},{8,9},{9,8},{10,11... | collective-permute-start | bytes 786440 | tf_op jit(solution)/shard_map/ppermute | solution.py:259
  80.4 13.2 %collective-permute-start.5 = (bf16[128,1024]{1,0:T(8,128)(2,1)S(1)}, bf16[128,1024]{1,0:T(8,128)(2,1)S(1)}, u32[]{:S(2)}, u32[]{:S(2)}) collective-permute-start(bf16[128,1024]{1,0:T(8,128)(2,1)S(1)} %get-tuple-element.29), channel_id=1, source_target_pairs={{0,30},{1,31},{2,4},{3,5},{4,2},{5,3},{6,8},{7,9},{8,6},{9,7},{10,... | collective-permute-start | bytes 786440 | tf_op jit(solution)/shard_map/ppermute | solution.py:259
  88.4 12.2 %collective-permute-start.6 = (bf16[128,1024]{1,0:T(8,128)(2,1)S(1)}, bf16[128,1024]{1,0:T(8,128)(2,1)S(1)}, u32[]{:S(2)}, u32[]{:S(2)}) collective-permute-start(bf16[128,1024]{1,0:T(8,128)(2,1)S(1)} %get-tuple-element.30), channel_id=1, source_target_pairs={{0,31},{1,30},{2,5},{3,4},{4,3},{5,2},{6,9},{7,8},{8,7},{9,6},{10,... | collective-permute-start | bytes 786440 | tf_op jit(solution)/shard_map/ppermute | solution.py:259

commit v13 on v12

--- a/solution.py
+++ b/solution.py
@@ -41,23 +41,22 @@
 
 
 def copy_halves(grads_ref, out_ref):
-    tile = out_ref.shape[1] // 2
-    for b in range(2):
-        for core in range(CORES):
-            row = (b * CORES + core) * tile
-            entries = grads_ref[row : row + tile, :]
-            for y in range(ROWS_Y):
-                out_ref[y * CORES + core, b * tile : (b + 1) * tile, :] = entries
+    tile = out_ref.shape[1]
+    for core in range(CORES):
+        entries = grads_ref[core * tile : (core + 1) * tile, :]
+        for y in range(ROWS_Y):
+            out_ref[y * CORES + core] = entries
 
 
 def spread(grads, tile):
     rows, width = grads.shape
     return pl.pallas_call(
         copy_halves,
-        in_specs=[pl.BlockSpec(memory_space=pltpu.VMEM)],
-        out_specs=pl.BlockSpec(memory_space=pltpu.VMEM),
-        out_shape=jax.ShapeDtypeStruct((ROWS_Y * CORES, 2 * tile, width), grads.dtype),
-        compiler_params=pltpu.CompilerParams(vmem_limit_bytes=8 * MIB),
+        grid=(2,),
+        in_specs=[pl.BlockSpec((CORES * tile, width), lambda b: (b, 0))],
+        out_specs=pl.BlockSpec((ROWS_Y * CORES, tile, width), lambda b: (0, b, 0)),
+        out_shape=pltpu.HBM((ROWS_Y * CORES, 2 * tile, width), grads.dtype),
+        compiler_params=pltpu.CompilerParams(vmem_limit_bytes=60 * MIB),
         cost_estimate=pl.CostEstimate(
             flops=0, bytes_accessed=2 * (1 + ROWS_Y) * rows * width, transcendentals=0
         ),

time: 144 us -> 144 us (level)
  transfers between devices with their start and end apart: 10 -> 10, of which waited for: 4 -> 4; matrix products, arithmetic and copies ran while one was open for 1% -> 1% of each run, Pallas kernels for 12% -> 13%
where the time goes in v13:
time: 144 us
  starting transfers between devices  41.4 us (29%)
  blocking collectives  41.3 us (29%)
  waiting for transfers between devices  35.4 us (25%)
  Pallas kernels  22.7 us (16%)
  local copies, waits for them, and re-layouts  1.89 us (1%)
    all_to_all x1, blocking collectives, shards(): lax.all_to_all(added(place, tile, gathered, others), ('ex', 'dim'), 0, 0,...  41.3 us
    all_to_all x1, waiting for transfers between devices, shards(): lax.all_to_all(copies, 'ex', 0, 0, tiled=True, axis_index_groups=same_core)  23.2 us
    ppermute x3, starting transfers between devices, shards(): lax.ppermute(term, 'dim', [(d, ((d + SIDES ^ k) - SIDES) % slots if k & S...  12.7 us
    pallas_call x2, Pallas kernels, scores_of(): pl.pallas_call(functools.partial(score, apart), grid_spec=pltpu.PrefetchS...  10.7 us
    ppermute x3, waiting for transfers between devices, shards(): lax.ppermute(term, 'dim', [(d, ((d + SIDES ^ k) - SIDES) % slots if k & S...  9.37 us
    all_to_all x1, starting transfers between devices, shards(): lax.all_to_all(terms, 'dim', 0, 0, tiled=True, axis_index_groups=near)  7.53 us
    pallas_call x1, Pallas kernels, dequantized(): pl.pallas_call(dequantize, grid=(rows // tile,), in_specs=[pl.BlockSpec((...  5.99 us
    all_to_all x1, starting transfers between devices, shards(): lax.all_to_all(copies, 'ex', 0, 0, tiled=True, axis_index_groups=same_core)  5.69 us
  transfers between devices with their start and end apart: 10, of which 4 were waited for; matrix products, arithmetic and copies ran while one was open for 1% of the time, Pallas kernels for 13%

profile of v13, /device:TPU:7, one launch (start us, length us, event | category | flops | bytes accessed | tf_op | source)
XLA Modules:
  0.0 143.6 jit_solution(731633907612949215)
XLA Ops:
  0.0 3.0 %collective-permute-start = (bf16[2048,128]{1,0:T(8,128)(2,1)}, bf16[2048,128]{1,0:T(8,128)(2,1)S(1)}, u32[]{:S(2)}, u32[]{:S(2)}) collective-permute-start(bf16[2048,128]{1,0:T(8,128)(2,1)} %bitcast.9), channel_id=1, source_target_pairs={{0,256},{32,288},{64,320},{96,352},{128,384},{160,416},{192,448},{... | collective-permute-start | bytes 1572872 | tf_op jit(solution)/shard_map/ppermute | solution.py:237
  3.0 1.9 %shard_map.46 = bf16[8,32,2048]{2,1,0:T(8,128)(2,1)} custom-call(bf16[64,2048]{1,0:T(8,128)(2,1)} %grads_ref.1), custom_call_target="tpu_custom_call" | custom-call | bytes 1310720 | tf_op jit(solution)/shard_map/pallas_call | solution.py:53
  5.0 5.4 %all-to-all-start = ((bf16[8,32,2048]{2,1,0:T(8,128)(2,1)}), bf16[8,32,2048]{2,1,0:T(8,128)(2,1)S(1)}, u32[]{:S(2)}, u32[]{:S(2)}) async-start(bf16[8,32,2048]{2,1,0:T(8,128)(2,1)} %shard_map.46), calls=%async_computation | async-start | bytes 2097152 | tf_op jit(solution)/shard_map/all_to_all | solution.py:242
  10.4 1.9 %collective-permute-start.1 = (bf16[2048,128]{1,0:T(8,128)(2,1)}, bf16[2048,128]{1,0:T(8,128)(2,1)S(1)}, u32[]{:S(2)}, u32[]{:S(2)}) collective-permute-start(bf16[2048,128]{1,0:T(8,128)(2,1)} %bitcast.10), channel_id=1, source_target_pairs={{0,32},{32,0},{64,96},{96,64},{128,160},{160,128},{192,224},{224,1... | collective-permute-start | bytes 1572872 | tf_op jit(solution)/shard_map/ppermute | solution.py:236
  12.3 1.9 %copy.5.scales_ref = f32[1024,16]{1,0:T(8,128)} copy(f32[1024,16]{0,1:T(8,128)} %param.7) | data formatting | bytes 131072 | tf_op args[3]
  14.2 0.0 copy-start
  14.2 6.0 %shard_map.47.store_ref = bf16[1024,2048]{1,0:T(8,128)(2,1)} custom-call(bf16[1024,2048]{1,0:T(8,128)(2,1)} %codes_ref.1, f32[1024,16]{1,0:T(8,128)} %copy.5.scales_ref), custom_call_target="tpu_custom_call" | custom-call | flops 2097152 | bytes 8388608 | tf_op jit(solution)/shard_map/pallas_call | solution.py:27
  20.2 0.0 collective-permute-done.refs_3_
  20.2 2.4 %collective-permute-start.2 = (bf16[2048,128]{1,0:T(8,128)(2,1)S(1)}, bf16[2048,128]{1,0:T(8,128)(2,1)S(1)}, u32[]{:S(2)}, u32[]{:S(2)}) collective-permute-start(bf16[2048,128]{1,0:T(8,128)(2,1)S(1)} %collective-permute-done.refs_3_), channel_id=1, source_target_pairs={{0,32},{32,0},{64,96},{96,64},{128,160},{160,128},{192,224},{224,1... | collective-permute-start | bytes 1572872 | tf_op jit(solution)/shard_map/ppermute | solution.py:240
  22.6 0.1 pad_add_fusion.place_ref
  22.7 0.0 collective-permute-done.1.refs_2_
  22.7 2.8 %all-to-all-done = bf16[8,32,2048]{2,1,0:T(8,128)(2,1)S(1)} async-done(((bf16[8,32,2048]{2,1,0:T(8,128)(2,1)}), bf16[8,32,2048]{2,1,0:T(8,128)(2,1)S(1)}, u32[]{:S(2)}, u32[]{:S(2)}) %all-to-all-start) | async-done | bytes 1048608 | tf_op jit(solution)/shard_map/all_to_all | solution.py:242
  25.5 0.0 collective-permute-done.2.refs_4_
  25.5 0.0 copy-done
  25.5 3.1 %shard_map.48 = bf16[8,256,512]{2,1,0:T(8,128)(2,1)} custom-call(s32[2]{0:T(128)S(1)} %pad_add_fusion.place_ref, bf16[256,2048]{1,0:T(8,128)(2,1)S(1)} %bitcast.8, bf16[2048,128]{1,0:T(8,128)(2,1)S(1)} %bitcast.11, bf16[2048,128]{1,0:T(8,128)(2,1)S(1)} %collective-permute-done.1.refs_2_, bf16[2048,128]{1,0:T(8,128)(2,1)S(1)} %collective-permute-done.refs_3_, ...), custom_call_target="tpu_custom_call" | custom-call | flops 536870912 | bytes 5242880 | tf_op jit(solution)/shard_map/pallas_call | solution.py:85
  28.6 5.7 %all-to-all-start.1 = ((bf16[8,256,512]{2,1,0:T(8,128)(2,1)}), bf16[8,256,512]{2,1,0:T(8,128)(2,1)S(1)}, u32[]{:S(2)}, u32[]{:S(2)}) async-start(bf16[8,256,512]{2,1,0:T(8,128)(2,1)} %shard_map.48), calls=%async_computation.1 | async-start | bytes 4194304 | tf_op jit(solution)/shard_map/all_to_all | solution.py:252
  34.3 2.7 %collective-permute-start.3 = (bf16[1024,2048]{1,0:T(8,128)(2,1)}, bf16[1024,2048]{1,0:T(8,128)(2,1)}, u32[]{:S(2)}, u32[]{:S(2)}) collective-permute-start(bf16[1024,2048]{1,0:T(8,128)(2,1)} %shard_map.47.store_ref), channel_id=1, source_target_pairs={{0,32},{32,0},{64,96},{96,64},{128,160},{160,128},{192,224},{224,1... | collective-permute-start | bytes 12582920 | tf_op jit(solution)/shard_map/ppermute | solution.py:251
  37.0 23.2 %all-to-all-done.1.parts_ref = bf16[8,256,512]{2,1,0:T(8,128)(2,1)S(1)} async-done(((bf16[8,256,512]{2,1,0:T(8,128)(2,1)}), bf16[8,256,512]{2,1,0:T(8,128)(2,1)S(1)}, u32[]{:S(2)}, u32[]{:S(2)}) %all-to-all-start.1) | async-done | bytes 2097184 | tf_op jit(solution)/shard_map/all_to_all | solution.py:252
  60.2 5.7 %shard_map.49 = bf16[4,128,1024]{2,1,0:T(8,128)(2,1)} custom-call(s32[2]{0:T(128)S(1)} %pad_add_fusion.place_ref, bf16[8,256,512]{2,1,0:T(8,128)(2,1)S(1)} %all-to-all-done.1.parts_ref, bf16[1024,2048]{1,0:T(8,128)(2,1)} %shard_map.47.store_ref), custom_call_target="tpu_custom_call" | custom-call | flops 2147483648 | bytes 7340032 | tf_op jit(solution)/shard_map/pallas_call | solution.py:147
  65.9 7.5 %all-to-all-start.2 = ((bf16[4,128,1024]{2,1,0:T(8,128)(2,1)}), bf16[4,128,1024]{2,1,0:T(8,128)(2,1)S(1)}, u32[]{:S(2)}, u32[]{:S(2)}) async-start(bf16[4,128,1024]{2,1,0:T(8,128)(2,1)} %shard_map.49), calls=%async_computation.2 | async-start | bytes 2097152 | tf_op jit(solution)/shard_map/all_to_all | solution.py:255
  73.4 0.0 collective-permute-done.3.store_ref
  73.4 5.0 %shard_map.50 = (bf16[128,1024]{1,0:T(8,128)(2,1)S(1)}, bf16[128,1024]{1,0:T(8,128)(2,1)S(1)}, bf16[128,1024]{1,0:T(8,128)(2,1)S(1)}, bf16[128,1024]{1,0:T(8,128)(2,1)S(1)}) custom-call(s32[2]{0:T(128)S(1)} %pad_add_fusion.place_ref, bf16[8,256,512]{2,1,0:T(8,128)(2,1)S(1)} %all-to-all-done.1.parts_ref, bf16[1024,2048]{1,0:T(8,128)(2,1)} %collective-permute-done.3.store_ref), custom_call_target="tpu_custom_call" | custom-call | flops 2147483648 | bytes 7340032 | tf_op jit(solution)/shard_map/pallas_call | solution.py:147
  78.4 2.0 %collective-permute-start.4 = (bf16[128,1024]{1,0:T(8,128)(2,1)S(1)}, bf16[128,1024]{1,0:T(8,128)(2,1)S(1)}, u32[]{:S(2)}, u32[]{:S(2)}) collective-permute-start(bf16[128,1024]{1,0:T(8,128)(2,1)S(1)} %get-tuple-element.28), channel_id=1, source_target_pairs={{0,1},{1,0},{2,3},{3,2},{4,5},{5,4},{6,7},{7,6},{8,9},{9,8},{10,11... | collective-permute-start | bytes 786440 | tf_op jit(solution)/shard_map/ppermute | solution.py:258
  80.4 8.0 %collective-permute-start.5 = (bf16[128,1024]{1,0:T(8,128)(2,1)S(1)}, bf16[128,1024]{1,0:T(8,128)(2,1)S(1)}, u32[]{:S(2)}, u32[]{:S(2)}) collective-permute-start(bf16[128,1024]{1,0:T(8,128)(2,1)S(1)} %get-tuple-element.29), channel_id=1, source_target_pairs={{0,30},{1,31},{2,4},{3,5},{4,2},{5,3},{6,8},{7,9},{8,6},{9,7},{10,... | collective-permute-start | bytes 786440 | tf_op jit(solution)/shard_map/ppermute | solution.py:258
  88.3 2.8 %collective-permute-start.6 = (bf16[128,1024]{1,0:T(8,128)(2,1)S(1)}, bf16[128,1024]{1,0:T(8,128)(2,1)S(1)}, u32[]{:S(2)}, u32[]{:S(2)}) collective-permute-start(bf16[128,1024]{1,0:T(8,128)(2,1)S(1)} %get-tuple-element.30), channel_id=1, source_target_pairs={{0,31},{1,30},{2,5},{3,4},{4,3},{5,2},{6,9},{7,8},{8,7},{9,6},{10,... | collective-permute-start | bytes 786440 | tf_op jit(solution)/shard_map/ppermute | solution.py:258
  91.2 0.0 collective-permute-done.4.refs_1_
  91.2 2.4 %collective-permute-done.5.refs_2_ = bf16[128,1024]{1,0:T(8,128)(2,1)S(1)} collective-permute-done((bf16[128,1024]{1,0:T(8,128)(2,1)S(1)}, bf16[128,1024]{1,0:T(8,128)(2,1)S(1)}, u32[]{:S(2)}, u32[]{:S(2)}) %collective-permute-start.5) | collective-permute-done | bytes 262176 | tf_op jit(solution)/shard_map/ppermute | solution.py:258
  93.5 7.0 %collective-permute-done.6.refs_3_ = bf16[128,1024]{1,0:T(8,128)(2,1)S(1)} collective-permute-done((bf16[128,1024]{1,0:T(8,128)(2,1)S(1)}, bf16[128,1024]{1,0:T(8,128)(2,1)S(1)}, u32[]{:S(2)}, u32[]{:S(2)}) %collective-permute-start.6) | collective-permute-done | bytes 262176 | tf_op jit(solution)/shard_map/ppermute | solution.py:258
  100.6 0.0 all-to-all-done.2.gathered_ref
  100.6 1.0 shard_map.51
  101.6 41.3 %all_to_all.20 = bf16[16,16,1024]{2,1,0:T(8,128)(2,1)S(1)} all-to-all(bf16[16,16,1024]{2,1,0:T(8,128)(2,1)S(1)} %shard_map.51), channel_id=1, replica_groups={{0,32,4,36,8,40,12,44,16,48,20,52,24,56,28,60},{1,33,5,37,9,41,13,45,17..., dimensions={0} | all-to-all | bytes 1048576 | tf_op jit(solution)/shard_map/all_to_all | solution.py:263
  142.9 0.1 convert_reduce_fusion
  143.0 0.7 broadcast_multiply_fusion
Async XLA Ops:
  0.0 20.2 %collective-permute-start = (bf16[2048,128]{1,0:T(8,128)(2,1)}, bf16[2048,128]{1,0:T(8,128)(2,1)S(1)}, u32[]{:S(2)}, u32[]{:S(2)}) collective-permute-start(bf16[2048,128]{1,0:T(8,128)(2,1)} %bitcast.9), channel_id=1, source_target_pairs={{0,256},{32,288},{64,320},{96,352},{128,384},{160,416},{192,448},{... | collective-permute-start | bytes 1572872 | tf_op jit(solution)/shard_map/ppermute | solution.py:237
  5.0 20.5 %all-to-all-start = ((bf16[8,32,2048]{2,1,0:T(8,128)(2,1)}), bf16[8,32,2048]{2,1,0:T(8,128)(2,1)S(1)}, u32[]{:S(2)}, u32[]{:S(2)}) async-start(bf16[8,32,2048]{2,1,0:T(8,128)(2,1)} %shard_map.46), calls=%async_computation | async-start | bytes 2097152 | tf_op jit(solution)/shard_map/all_to_all | solution.py:242
  10.4 12.3 %collective-permute-start.1 = (bf16[2048,128]{1,0:T(8,128)(2,1)}, bf16[2048,128]{1,0:T(8,128)(2,1)S(1)}, u32[]{:S(2)}, u32[]{:S(2)}) collective-permute-start(bf16[2048,128]{1,0:T(8,128)(2,1)} %bitcast.10), channel_id=1, source_target_pairs={{0,32},{32,0},{64,96},{96,64},{128,160},{160,128},{192,224},{224,1... | collective-permute-start | bytes 1572872 | tf_op jit(solution)/shard_map/ppermute | solution.py:236
  14.2 11.3 %copy-start = (bf16[1,2048,128]{2,1,0:T(8,128)(2,1)S(1)}, bf16[1,2048,128]{2,1,0:T(8,128)(2,1)}, u32[]{:S(2)}) copy-start(bf16[1,2048,128]{2,1,0:T(8,128)(2,1)} %param.5) | copy-start | bytes 1572868
  20.2 5.3 %collective-permute-start.2 = (bf16[2048,128]{1,0:T(8,128)(2,1)S(1)}, bf16[2048,128]{1,0:T(8,128)(2,1)S(1)}, u32[]{:S(2)}, u32[]{:S(2)}) collective-permute-start(bf16[2048,128]{1,0:T(8,128)(2,1)S(1)} %collective-permute-done.refs_3_), channel_id=1, source_target_pairs={{0,32},{32,0},{64,96},{96,64},{128,160},{160,128},{192,224},{224,1... | collective-permute-start | bytes 1572872 | tf_op jit(solution)/shard_map/ppermute | solution.py:240
  28.6 31.6 %all-to-all-start.1 = ((bf16[8,256,512]{2,1,0:T(8,128)(2,1)}), bf16[8,256,512]{2,1,0:T(8,128)(2,1)S(1)}, u32[]{:S(2)}, u32[]{:S(2)}) async-start(bf16[8,256,512]{2,1,0:T(8,128)(2,1)} %shard_map.48), calls=%async_computation.1 | async-start | bytes 4194304 | tf_op jit(solution)/shard_map/all_to_all | solution.py:252
  34.3 39.2 %collective-permute-start.3 = (bf16[1024,2048]{1,0:T(8,128)(2,1)}, bf16[1024,2048]{1,0:T(8,128)(2,1)}, u32[]{:S(2)}, u32[]{:S(2)}) collective-permute-start(bf16[1024,2048]{1,0:T(8,128)(2,1)} %shard_map.47.store_ref), channel_id=1, source_target_pairs={{0,32},{32,0},{64,96},{96,64},{128,160},{160,128},{192,224},{224,1... | collective-permute-start | bytes 12582920 | tf_op jit(solution)/shard_map/ppermute | solution.py:251
  65.9 34.7 %all-to-all-start.2 = ((bf16[4,128,1024]{2,1,0:T(8,128)(2,1)}), bf16[4,128,1024]{2,1,0:T(8,128)(2,1)S(1)}, u32[]{:S(2)}, u32[]{:S(2)}) async-start(bf16[4,128,1024]{2,1,0:T(8,128)(2,1)} %shard_map.49), calls=%async_computation.2 | async-start | bytes 2097152 | tf_op jit(solution)/shard_map/all_to_all | solution.py:255
  78.4 12.8 %collective-permute-start.4 = (bf16[128,1024]{1,0:T(8,128)(2,1)S(1)}, bf16[128,1024]{1,0:T(8,128)(2,1)S(1)}, u32[]{:S(2)}, u32[]{:S(2)}) collective-permute-start(bf16[128,1024]{1,0:T(8,128)(2,1)S(1)} %get-tuple-element.28), channel_id=1, source_target_pairs={{0,1},{1,0},{2,3},{3,2},{4,5},{5,4},{6,7},{7,6},{8,9},{9,8},{10,11... | collective-permute-start | bytes 786440 | tf_op jit(solution)/shard_map/ppermute | solution.py:258
  80.4 13.2 %collective-permute-start.5 = (bf16[128,1024]{1,0:T(8,128)(2,1)S(1)}, bf16[128,1024]{1,0:T(8,128)(2,1)S(1)}, u32[]{:S(2)}, u32[]{:S(2)}) collective-permute-start(bf16[128,1024]{1,0:T(8,128)(2,1)S(1)} %get-tuple-element.29), channel_id=1, source_target_pairs={{0,30},{1,31},{2,4},{3,5},{4,2},{5,3},{6,8},{7,9},{8,6},{9,7},{10,... | collective-permute-start | bytes 786440 | tf_op jit(solution)/shard_map/ppermute | solution.py:258
  88.3 12.2 %collective-permute-start.6 = (bf16[128,1024]{1,0:T(8,128)(2,1)S(1)}, bf16[128,1024]{1,0:T(8,128)(2,1)S(1)}, u32[]{:S(2)}, u32[]{:S(2)}) collective-permute-start(bf16[128,1024]{1,0:T(8,128)(2,1)S(1)} %get-tuple-element.30), channel_id=1, source_target_pairs={{0,31},{1,30},{2,5},{3,4},{4,3},{5,2},{6,9},{7,8},{8,7},{9,6},{10,... | collective-permute-start | bytes 786440 | tf_op jit(solution)/shard_map/ppermute | solution.py:258
